TPU v7x, 32 devices: a whole 2x2x4 slice. The times are simulated.
32 devices in a mesh: dp: 4 (over z), fsdp: 8 (over y, x, core).
Axes of the slice: x: 2, y: 2, z: 4, core: 2. Of those that a mesh axis runs over, the one named last changes fastest.
Arguments:
- visual: bfloat16 [8, 288, 12, 768], P('dp', 'fsdp'), may hold values from -6 to 6
- query_slots: bfloat16 [8, 128, 768], P('dp', 'fsdp'), may hold values from -6 to 6
- lengths: int32 [8], P('dp'), may hold values from 1 to 128, as said below
- slot_order: int32 [8, 8], P('dp'), may hold values from 0 to 7, each once within a row
- norm_window: bfloat16 [768], P(('dp', 'fsdp')), may hold values from 0.099609375 to 1.8984375
- window_qkv: bfloat16 [768, 2304], P(('dp', 'fsdp')), may hold values from -0.21875 to 0.21875
- window_out: bfloat16 [768, 768], P(('dp', 'fsdp')), may hold values from -1.5 to 1.5
- norm_slots: bfloat16 [768], P(('dp', 'fsdp')), may hold values from 0.099609375 to 1.8984375
- slots_qkv: bfloat16 [768, 2304], P(('dp', 'fsdp')), may hold values from -0.21875 to 0.21875
- slots_out: bfloat16 [768, 768], P(('dp', 'fsdp')), may hold values from -0.875 to 0.875
- norm_reader: bfloat16 [768], P(('dp', 'fsdp')), may hold values from 0.099609375 to 1.8984375
- norm_page: bfloat16 [768], P(('dp', 'fsdp')), may hold values from 0.099609375 to 1.8984375
- reader_qkv: bfloat16 [768, 2304], P(('dp', 'fsdp')), may hold values from -0.21875 to 0.21875
- reader_out: bfloat16 [768, 768], P(('dp', 'fsdp')), may hold values from -6 to 6
- writer_qkv: bfloat16 [768, 2304], P(('dp', 'fsdp')), may hold values from -0.21875 to 0.21875
- writer_out: bfloat16 [768, 768], P(('dp', 'fsdp')), may hold values from -0.875 to 0.875
- norm_visual_mlp: bfloat16 [768], P(('dp', 'fsdp')), may hold values from 0.099609375 to 1.8984375
- visual_up: bfloat16 [768, 3072], P(('dp', 'fsdp')), may hold values from -0.21875 to 0.21875
- visual_down: bfloat16 [3072, 768], P(('dp', 'fsdp')), may hold values from -0.109375 to 0.109375
- norm_query_mlp: bfloat16 [768], P(('dp', 'fsdp')), may hold values from 0.099609375 to 1.8984375
- query_up: bfloat16 [768, 3072], P(('dp', 'fsdp')), may hold values from -0.21875 to 0.21875
- query_down: bfloat16 [3072, 768], P(('dp', 'fsdp')), may hold values from -0.109375 to 0.109375
- visual_cot: bfloat16 [8, 288, 12, 768], P('dp', 'fsdp'), may hold values from -6 to 6
- query_cot: bfloat16 [8, 128, 768], P('dp', 'fsdp'), may hold values from -6 to 6
Outputs:
- visual_out: bfloat16 [8, 288, 12, 768], P('dp', 'fsdp')
- query_out: bfloat16 [8, 128, 768], P('dp', 'fsdp')
- visual_grad: bfloat16 [8, 288, 12, 768], P('dp', 'fsdp')
- query_grad: bfloat16 [8, 128, 768], P('dp', 'fsdp')
- grad_norm_window: float32 [768], P(('dp', 'fsdp'))
- grad_window_qkv: float32 [768, 2304], P(('dp', 'fsdp'))
- grad_window_out: float32 [768, 768], P(('dp', 'fsdp'))
- grad_norm_slots: float32 [768], P(('dp', 'fsdp'))
- grad_slots_qkv: float32 [768, 2304], P(('dp', 'fsdp'))
- grad_slots_out: float32 [768, 768], P(('dp', 'fsdp'))
- grad_norm_reader: float32 [768], P(('dp', 'fsdp'))
- grad_norm_page: float32 [768], P(('dp', 'fsdp'))
- grad_reader_qkv: float32 [768, 2304], P(('dp', 'fsdp'))
- grad_reader_out: float32 [768, 768], P(('dp', 'fsdp'))
- grad_writer_qkv: float32 [768, 2304], P(('dp', 'fsdp'))
- grad_writer_out: float32 [768, 768], P(('dp', 'fsdp'))
- grad_norm_visual_mlp: float32 [768], P(('dp', 'fsdp'))
- grad_visual_up: float32 [768, 3072], P(('dp', 'fsdp'))
- grad_visual_down: float32 [3072, 768], P(('dp', 'fsdp'))
- grad_norm_query_mlp: float32 [768], P(('dp', 'fsdp'))
- grad_query_up: float32 [768, 3072], P(('dp', 'fsdp'))
- grad_query_down: float32 [3072, 768], P(('dp', 'fsdp'))
Inputs may be any that keep to these rules, and one draw needn't show every extreme that they name: `lengths`: in each group of 2 consecutive pages one page has length 128; the others follow a heavy-tailed law.
All inputs are finite; a program needn't handle non-finite values.
Results may differ from a plain program's by a relative error of at most 0.025.
Values may be sent and summed in bfloat16 or wider, within the bound.
No kernel may reach another device: no remote copies, remote signals or barrier semaphores. Data moves between devices by JAX's collectives and lax.ppermute only.
A program may use at most 384 MiB of HBM per device.

v0:
```python
from functools import partial

import jax
import jax.numpy as jnp
from jax import lax
from jax.experimental import pallas as pl
from jax.experimental.pallas import tpu as pltpu
from jax.sharding import PartitionSpec as P

D = 768
HEADS = 12
HEAD = 64
WIN = 12
WCOLS = 8
Q_DEV = 16
MICRO = 2
PATCH = WIN * WIN
PAIRS = HEADS // 2
GROUPS = 4
GHEADS = HEADS // GROUPS
GCOLS = GHEADS * HEAD
SCALE = HEAD ** (-0.5)

bf = jnp.bfloat16
f32 = jnp.float32


def dot(a, b):
    return lax.dot_general(a, b, (((1,), (0,)), ((), ())), preferred_element_type=f32)


def dot_t(a, b):
    return lax.dot_general(a, b, (((1,), (1,)), ((), ())), preferred_element_type=f32)


def t_dot(a, b):
    return lax.dot_general(a, b, (((0,), (0,)), ((), ())), preferred_element_type=f32)


def normalise(x):
    centred = x - jnp.mean(x, axis=-1, keepdims=True)
    inv = lax.rsqrt(jnp.mean(centred * centred, axis=-1, keepdims=True) + 1e-05)
    return centred * inv, inv


def norm_back(grad, hat, inv, gain):
    scaled = grad * gain
    mean_one = jnp.mean(scaled, axis=-1, keepdims=True)
    mean_two = jnp.mean(scaled * hat, axis=-1, keepdims=True)
    return inv * (scaled - mean_one - hat * mean_two), jnp.sum(grad * hat, axis=0, keepdims=True)


def gelu_both(u):
    k = 0.7978845608028654
    t = jnp.tanh(k * (u + 0.044715 * u * u * u))
    slope = 0.5 * (1.0 + t) + 0.5 * u * (1.0 - t * t) * k * (1.0 + 3 * 0.044715 * u * u)
    return 0.5 * u * (1.0 + t), slope


def low_lanes(rows):
    return lax.broadcasted_iota(jnp.int32, (rows, 2 * HEAD), 1) < HEAD


def twofold(pair, mask):
    zero = jnp.zeros_like(pair)
    return jnp.concatenate([jnp.where(mask, pair, zero), jnp.where(mask, zero, pair)], axis=0)


def onefold(stacked, mask):
    rows = stacked.shape[0] // 2
    return jnp.where(mask, stacked[:rows], stacked[rows:])


def pair_forward(q2, k2, v2, bias):
    mask = low_lanes(q2.shape[0])
    s = dot_t(twofold(q2, mask), k2) * SCALE
    if bias is not None:
        s = s + bias
    m = jnp.max(s, axis=-1, keepdims=True)
    e = jnp.exp(s - m)
    l = jnp.sum(e, axis=-1, keepdims=True)
    out = dot(e.astype(bf), v2) / l
    return onefold(out, mask), m, l


def pair_backward(q2, k2, v2, d2, a2, bias, lse=None):
    mask = low_lanes(q2.shape[0])
    qs = twofold(q2, mask)
    ds = twofold(d2, mask)
    s = dot_t(qs, k2) * SCALE
    if bias is not None:
        s = s + bias
    if lse is None:
        e = jnp.exp(s - jnp.max(s, axis=-1, keepdims=True))
        p = e * (1.0 / jnp.sum(e, axis=-1, keepdims=True))
    else:
        p = jnp.exp(s - lse)
    corr = jnp.sum(ds.astype(f32) * twofold(a2, mask).astype(f32), axis=-1, keepdims=True)
    dp = dot_t(ds, v2)
    dsc = (p * (dp - corr)).astype(bf)
    dq = onefold(dot(dsc, k2), mask) * SCALE
    dk = t_dot(dsc, qs) * SCALE
    dv = t_dot(p.astype(bf), ds)
    return dq, dk, dv


def call(body, name, out_shape, in_specs, out_specs, grid, args, scratch=(), flops=0):
    return pl.pallas_call(
        body,
        name=name,
        out_shape=out_shape,
        grid=grid,
        in_specs=in_specs,
        out_specs=out_specs,
        scratch_shapes=scratch,
        compiler_params=pltpu.CompilerParams(vmem_limit_bytes=58 * 1024 * 1024),
        cost_estimate=pl.CostEstimate(flops=flops, bytes_accessed=1 << 20, transcendentals=0),
    )(*args)


def whole(shape):
    zeros = (0,) * len(shape)
    return pl.BlockSpec(shape, lambda *_: zeros, pipeline_mode=pl.Buffered(1))


def per_page(shape, axis):
    def place(p):
        return tuple(p if k == axis else 0 for k in range(len(shape)))

    return pl.BlockSpec(shape, place)


def sds(shape, dtype):
    return jax.ShapeDtypeStruct(shape, dtype)


def window_fwd(x_ref, bias_ref, gw_ref, gp_ref, w_ref, mix_ref, att_ref, v1_ref, pk_ref):
    rows = x_ref.shape[0]
    x = x_ref[...].astype(f32)
    xn = (normalise(x)[0] * gw_ref[...]).astype(bf)
    for u in range(3):
        mix_ref[u] = dot(xn, w_ref[3 + u]).astype(bf)

    def window(w, carry):
        at = pl.ds(pl.multiple_of(w * PATCH, 16), PATCH)
        bias = bias_ref[w]
        bias = jnp.concatenate([bias, bias], axis=0)
        for p in range(PAIRS):
            c = slice(p * 128, p * 128 + 128)
            out = pair_forward(mix_ref[0, at, c], mix_ref[1, at, c], mix_ref[2, at, c], bias)[0]
            att_ref[at, c] = out.astype(bf)
        return carry

    lax.fori_loop(0, rows // PATCH, window, 0)
    v1 = x_ref[...].astype(f32) + dot(att_ref[...], w_ref[6])
    v1_ref[...] = v1
    pn = (normalise(v1)[0] * gp_ref[...]).astype(bf)
    for u in range(3):
        pk_ref[u] = dot(pn, w_ref[u]).astype(bf)


def read_fwd(rq_ref, k_ref, v_ref, o_ref, lse_ref):
    slots = rq_ref.shape[1]
    lane = lax.broadcasted_iota(jnp.int32, (slots, 128), 1)
    acc = jnp.zeros((slots, 128), f32)
    for p in range(PAIRS):
        c = slice(p * 128, p * 128 + 128)
        out, m, l = pair_forward(rq_ref[0, :, c], k_ref[0, :, c], v_ref[0, :, c], None)
        o_ref[0, :, c] = out
        lse = m + jnp.log(l)
        acc = jnp.where(lane == 2 * p, lse[:slots], acc)
        acc = jnp.where(lane == 2 * p + 1, lse[slots:], acc)
    lse_ref[0] = acc


def write_fwd(v1_ref, wq_ref, wk_ref, wv_ref, bias_ref, wo_ref, wr_ref, v2_ref):
    for p in range(PAIRS):
        c = slice(p * 128, p * 128 + 128)
        out = pair_forward(wq_ref[0, :, c], wk_ref[0, :, c], wv_ref[0, :, c], bias_ref[0])[0]
        wr_ref[:, c] = out.astype(bf)
    v2_ref[...] = v1_ref[...] + dot(wr_ref[...], wo_ref[0])


def mlp_both(
    steps,
    R,
    core_ref,
    x_ref,
    g_ref,
    up_ref,
    down_ref,
    cot_ref,
    out_ref,
    dx_ref,
    keep_up_ref,
    give_up_ref,
    keep_down_ref,
    give_down_ref,
    dg_ref,
    xn_ref,
    y_ref,
    dxn_ref,
    tall_ref,
):
    j = pl.program_id(0)
    core = core_ref[0]
    chunk = up_ref.shape[-1]

    @pl.when(j == 0)
    def _():
        xn_ref[...] = (normalise(x_ref[...])[0] * g_ref[...]).astype(bf)

    xn = xn_ref[...]
    cot = cot_ref[...]
    up = up_ref[0]
    if R:
        chips = chunk // (4 * R)
        pieces = [down_ref[u // 2, u % 2, i] for i in range(chips) for u in range(4)]
        down = jnp.concatenate(pieces, axis=0)
    else:
        down = down_ref[...]
    act, slope = gelu_both(dot(xn, up))
    act = act.astype(bf)
    y = dot(act, down)
    dpre = (dot_t(cot, down) * slope).astype(bf)
    dxn = dot_t(dpre, up)
    dup = t_dot(xn, dpre).astype(bf)

    @pl.when(j // (steps // 2) == core)
    def _():
        keep_up_ref[0] = dup

    @pl.when(j // (steps // 2) != core)
    def _():
        give_up_ref[0] = dup

    if R:
        tall_ref[...] = t_dot(act, cot).astype(bf)
        for i in range(chips):
            for k in range(2):
                keep_down_ref[k, i] = tall_ref[pl.ds(pl.multiple_of((4 * i + k + 2 * core) * R, R), R), :]
                give_down_ref[k, i] = tall_ref[pl.ds(pl.multiple_of((4 * i + k + 2 - 2 * core) * R, R), R), :]
    else:
        keep_down_ref[...] = t_dot(act, cot).astype(bf)

    @pl.when(j == 0)
    def _():
        y_ref[...] = y
        dxn_ref[...] = dxn

    @pl.when(j > 0)
    def _():
        y_ref[...] += y
        dxn_ref[...] += dxn

    @pl.when(j == steps - 1)
    def _():
        x = x_ref[...]
        out_ref[...] = (x + y_ref[...]).astype(bf)
        hat, inv = normalise(x)
        dx, dg = norm_back(dxn_ref[...], hat, inv, g_ref[...])
        dx_ref[...] = cot_ref[...].astype(f32) + dx
        dg_ref[...] = dg


def write_bwd(dv2_ref, wr_ref, wq_ref, wk_ref, wv_ref, bias_ref, wo_ref, dwq_ref, dwk_ref, dwv_ref, dwo_ref, acc_ref):
    page = pl.program_id(0)
    d = dv2_ref[...].astype(bf)
    dwr = dot_t(d, wo_ref[0]).astype(bf)
    part = t_dot(wr_ref[...], d)

    @pl.when(page == 0)
    def _():
        acc_ref[...] = part

    @pl.when(page > 0)
    def _():
        acc_ref[...] += part

    dwo_ref[...] = acc_ref[...].astype(bf)
    for p in range(PAIRS):
        c = slice(p * 128, p * 128 + 128)
        dq, dk, dv = pair_backward(
            wq_ref[0, :, c], wk_ref[0, :, c], wv_ref[0, :, c], dwr[:, c], wr_ref[:, c], bias_ref[0]
        )
        dwq_ref[:, c] = dq.astype(bf)
        dwk_ref[0, :, c] = dk.astype(bf)
        dwv_ref[0, :, c] = dv.astype(bf)


def read_bwd(rq_ref, k_ref, v_ref, d_ref, r_ref, lse_ref, dq_ref, dk_ref, dv_ref):
    slots = rq_ref.shape[1]
    lse = lse_ref[0]
    for p in range(PAIRS):
        c = slice(p * 128, p * 128 + 128)
        both = jnp.concatenate([lse[:, 2 * p : 2 * p + 1], lse[:, 2 * p + 1 : 2 * p + 2]], axis=0)
        dq, dk, dv = pair_backward(
            rq_ref[0, :, c], k_ref[0, :, c], v_ref[0, :, c], d_ref[0, :, c], r_ref[0, :, c], None, both
        )
        dq_ref[0, :, c] = dq.astype(bf)
        dk_ref[:, c] = dk.astype(bf)
        dv_ref[:, c] = dv.astype(bf)


def page_bwd(
    core_ref,
    v1_ref,
    dv2_ref,
    dk_ref,
    dv_ref,
    dwq_ref,
    gp_ref,
    wp_ref,
    dwo_ref,
    dv1_ref,
    keep_ref,
    give_ref,
    dg_ref,
    acc_ref,
    gacc_ref,
):
    page = pl.program_id(0)
    hat, inv = normalise(v1_ref[...])
    pn = (hat * gp_ref[...]).astype(bf)
    grads = (dk_ref, dv_ref, dwq_ref)
    dpn = dot_t(dk_ref[...], wp_ref[0]) + dot_t(dv_ref[...], wp_ref[1]) + dot_t(dwq_ref[...], wp_ref[2])
    dx, dg = norm_back(dpn, hat, inv, gp_ref[...])
    dv1_ref[...] = dv2_ref[...] + dx

    @pl.when(page == 0)
    def _():
        gacc_ref[...] = dg
        for u in range(3):
            acc_ref[u] = t_dot(pn, grads[u][...])

    @pl.when(page > 0)
    def _():
        gacc_ref[...] += dg
        for u in range(3):
            acc_ref[u] += t_dot(pn, grads[u][...])

    @pl.when(page == pl.num_programs(0) - 1)
    def _():
        dg_ref[...] = gacc_ref[...]

    def split(first_ref, second_ref):
        first_ref[...] = acc_ref[:2].astype(bf)
        second_ref[0] = acc_ref[2].astype(bf)
        second_ref[1] = dwo_ref[...]

    @pl.when((page == pl.num_programs(0) - 1) & (core_ref[0] == 0))
    def _():
        split(keep_ref, give_ref)

    @pl.when((page == pl.num_programs(0) - 1) & (core_ref[0] == 1))
    def _():
        split(give_ref, keep_ref)


def window_bwd(
    core_ref,
    dv1_ref,
    x_ref,
    mix_ref,
    att_ref,
    bias_ref,
    gw_ref,
    w_ref,
    dmix_ref,
    keep_ref,
    give_ref,
    acc_ref,
    datt_ref,
):
    page = pl.program_id(0)
    rows = x_ref.shape[0]
    d1b = dv1_ref[...].astype(bf)
    datt_ref[...] = dot_t(d1b, w_ref[6]).astype(bf)

    def window(w, carry):
        at = pl.ds(pl.multiple_of(w * PATCH, 16), PATCH)
        bias = bias_ref[w]
        bias = jnp.concatenate([bias, bias], axis=0)
        for p in range(PAIRS):
            c = slice(p * 128, p * 128 + 128)
            dq, dk, dv = pair_backward(
                mix_ref[0, at, c], mix_ref[1, at, c], mix_ref[2, at, c], datt_ref[at, c], att_ref[at, c], bias
            )
            dmix_ref[0, at, c] = dq.astype(bf)
            dmix_ref[1, at, c] = dk.astype(bf)
            dmix_ref[2, at, c] = dv.astype(bf)
        return carry

    lax.fori_loop(0, rows // PATCH, window, 0)
    xn = (normalise(x_ref[...].astype(f32))[0] * gw_ref[...]).astype(bf)

    @pl.when(page == 0)
    def _():
        for u in range(3):
            acc_ref[u] = t_dot(xn, dmix_ref[u])
        acc_ref[3] = t_dot(att_ref[...], d1b)

    @pl.when(page > 0)
    def _():
        for u in range(3):
            acc_ref[u] += t_dot(xn, dmix_ref[u])
        acc_ref[3] += t_dot(att_ref[...], d1b)

    def split(first_ref, second_ref):
        first_ref[...] = acc_ref[:2].astype(bf)
        second_ref[...] = acc_ref[2:].astype(bf)

    @pl.when((page == pl.num_programs(0) - 1) & (core_ref[0] == 0))
    def _():
        split(keep_ref, give_ref)

    @pl.when((page == pl.num_programs(0) - 1) & (core_ref[0] == 1))
    def _():
        split(give_ref, keep_ref)


def window_end(dv1_ref, x_ref, dmix_ref, gw_ref, w_ref, grad_ref, dg_ref, gacc_ref):
    page = pl.program_id(0)
    hat, inv = normalise(x_ref[...].astype(f32))
    dxn = dot_t(dmix_ref[0], w_ref[3]) + dot_t(dmix_ref[1], w_ref[4]) + dot_t(dmix_ref[2], w_ref[5])
    dx, dg = norm_back(dxn.astype(bf).astype(f32), hat, inv, gw_ref[...])
    grad_ref[...] = (dv1_ref[...] + dx).astype(bf)

    @pl.when(page == 0)
    def _():
        gacc_ref[...] = dg

    @pl.when(page > 0)
    def _():
        gacc_ref[...] += dg

    dg_ref[...] = gacc_ref[...]


def head_cols(part, h):
    return slice(part * GCOLS + h * HEAD, part * GCOLS + (h + 1) * HEAD)


def slots_fwd(x_ref, g_ref, w_ref, bias_ref, mix_ref, att_ref):
    xn = (normalise(x_ref[...].astype(f32))[0] * g_ref[...]).astype(bf)
    mix_ref[...] = dot(xn, w_ref[...]).astype(bf)
    outs = []
    for h in range(GHEADS):
        s = dot_t(mix_ref[:, head_cols(0, h)], mix_ref[:, head_cols(1, h)]) * SCALE + bias_ref[...]
        e = jnp.exp(s - jnp.max(s, axis=-1, keepdims=True))
        l = jnp.sum(e, axis=-1, keepdims=True)
        outs.append(dot(e.astype(bf), mix_ref[:, head_cols(2, h)]) / l)
    att_ref[...] = jnp.concatenate(outs, axis=-1).astype(bf)


def slots_mid(x_ref, att_ref, wo_ref, g_ref, w_ref, s1_ref, out_ref):
    s1 = x_ref[...].astype(f32) + dot(att_ref[...], wo_ref[0])
    s1_ref[...] = s1
    rn = (normalise(s1)[0] * g_ref[...]).astype(bf)
    out_ref[...] = dot(rn, w_ref[...]).astype(bf)


def query_mlp(s1_ref, read_ref, wo_ref, g_ref, up_ref, down_ref, cot_ref, s2_ref, part_ref, dup_ref, ddown_ref):
    s2 = s1_ref[...] + dot(read_ref[...], wo_ref[0])
    s2_ref[...] = s2
    xn = (normalise(s2)[0] * g_ref[...]).astype(bf)
    act, slope = gelu_both(dot(xn, up_ref[...]))
    act = act.astype(bf)
    part_ref[0] = dot(act, down_ref[...]).astype(bf)
    cot = cot_ref[...]
    dpre = (dot_t(cot, down_ref[...]) * slope).astype(bf)
    part_ref[1] = dot_t(dpre, up_ref[...]).astype(bf)
    dup_ref[...] = t_dot(xn, dpre).astype(bf)
    ddown_ref[...] = t_dot(act, cot).astype(bf)


def query_back(s2_ref, sum_ref, cot_ref, g_ref, wo_ref, out_ref, ds2_ref, dread_ref, dg_ref):
    s2 = s2_ref[...]
    out_ref[...] = (s2 + sum_ref[0].astype(f32)).astype(bf)
    hat, inv = normalise(s2)
    dx, dg = norm_back(sum_ref[1].astype(f32), hat, inv, g_ref[...])
    ds2 = cot_ref[...].astype(f32) + dx
    ds2_ref[...] = ds2
    dg_ref[...] = dg
    dread_ref[...] = dot_t(ds2.astype(bf), wo_ref[0]).astype(bf)


def reader_back(s1_ref, g_ref, w_ref, d_ref, part_ref, dw_ref):
    rn = (normalise(s1_ref[...])[0] * g_ref[...]).astype(bf)
    part_ref[...] = dot_t(d_ref[...], w_ref[...]).astype(bf)
    dw_ref[...] = t_dot(rn, d_ref[...]).astype(bf)


def slots_back(x_ref, s1_ref, ds2_ref, drn_ref, gr_ref, wo_ref, mix_ref, att_ref, bias_ref, gs_ref, w_ref, ds1_ref, part_ref, dw_ref, dg_ref):
    hat, inv = normalise(s1_ref[...])
    dx, dg = norm_back(drn_ref[...].astype(f32), hat, inv, gr_ref[...])
    dg_ref[...] = dg
    ds1 = ds2_ref[...] + dx
    ds1_ref[...] = ds1
    datt = dot_t(ds1.astype(bf), wo_ref[0]).astype(bf)
    att = att_ref[...]
    grads = [[], [], []]
    for h in range(GHEADS):
        q, k, v = (mix_ref[:, head_cols(part, h)] for part in range(3))
        d = datt[:, head_cols(0, h)]
        s = dot_t(q, k) * SCALE + bias_ref[...]
        e = jnp.exp(s - jnp.max(s, axis=-1, keepdims=True))
        p = e * (1.0 / jnp.sum(e, axis=-1, keepdims=True))
        corr = jnp.sum(d.astype(f32) * att[:, head_cols(0, h)].astype(f32), axis=-1, keepdims=True)
        dsc = (p * (dot_t(d, v) - corr)).astype(bf)
        grads[0].append(dot(dsc, k) * SCALE)
        grads[1].append(t_dot(dsc, q) * SCALE)
        grads[2].append(t_dot(p.astype(bf), d))
    dmix = jnp.concatenate(grads[0] + grads[1] + grads[2], axis=-1).astype(bf)
    part_ref[...] = dot_t(dmix, w_ref[...]).astype(bf)
    xn = (normalise(x_ref[...].astype(f32))[0] * gs_ref[...]).astype(bf)
    dw_ref[...] = t_dot(xn, dmix).astype(bf)


def slots_end(x_ref, g_ref, dxn_ref, ds1_ref, out_ref, dg_ref):
    hat, inv = normalise(x_ref[...].astype(f32))
    dx, dg = norm_back(dxn_ref[...].astype(f32), hat, inv, g_ref[...])
    out_ref[...] = (ds1_ref[...] + dx).astype(bf)
    dg_ref[...] = dg


def simple(body, name, args, outs):
    arrays = [a[0] if isinstance(a, tuple) else a for a in args]
    specs = [a[1] if isinstance(a, tuple) else whole(a.shape) for a in args]
    return call(
        body,
        name,
        tuple(sds(*o) for o in outs),
        specs,
        tuple(whole(o[0]) for o in outs),
        (1,),
        arrays,
        flops=1 << 30,
    )


def place_units(place, mine, other, n, R):
    nz, half = mine[0].shape[0], n // 2
    table = jnp.stack([place.core, place.chip % 4]).astype(jnp.int32)

    def body(table_ref, *refs):
        pieces, out_ref, sem = refs[:8], refs[8], refs[9]
        core, chip = table_ref[0], table_ref[1]
        copies = []
        for whose in range(2):
            owner = jnp.bitwise_xor(core, whose)
            for i in range(4):
                mask = jnp.where(owner == 0, i, (0, 2, 1, 3)[i])
                at = jnp.bitwise_xor(chip, mask)
                for u in range(half):
                    copy = pltpu.make_async_copy(
                        pieces[4 * whose + i].at[:, pl.ds(u * R, R)], out_ref.at[owner * half + u, :, at], sem.at[len(copies)]
                    )
                    copy.start()
                    copies.append(copy)
        for copy in copies:
            copy.wait()

    out = pl.pallas_call(
        body,
        name="place_units",
        out_shape=jax.ShapeDtypeStruct((n, nz, 4, R, D), bf),
        in_specs=[pl.BlockSpec(memory_space=pltpu.SMEM)] + [pl.BlockSpec(memory_space=pl.ANY)] * 8,
        out_specs=pl.BlockSpec(memory_space=pltpu.VMEM),
        scratch_shapes=[pltpu.SemaphoreType.DMA((8 * half,))],
        compiler_params=pltpu.CompilerParams(vmem_limit_bytes=58 * 1024 * 1024),
        cost_estimate=pl.CostEstimate(flops=0, bytes_accessed=n * D * D * 4, transcendentals=0),
    )(table, *mine, *other)
    return out.reshape(n, D, D)


def pick(stack, index, axis=0):
    return lax.dynamic_index_in_dim(stack, index, axis, keepdims=False)


def ordered(first, mine, other):
    return jnp.stack([jnp.where(first, mine, other), jnp.where(first, other, mine)])


class Place:
    def __init__(self):
        self.nz = lax.axis_size("dp")
        self.nf = lax.axis_size("fsdp")
        self.nq = self.nf // 2
        self.z = lax.axis_index("dp")
        self.f = lax.axis_index("fsdp")
        self.core = self.f % 2
        self.even = self.core == 0
        self.chip = self.f // 2
        self.group = self.chip % GROUPS

    def sibling(self, x):
        return lax.ppermute(x, "fsdp", [(f, f ^ 1) for f in range(self.nf)])

    def hop(self, x, mask, odd_mask=None):
        odd_mask = mask if odd_mask is None else odd_mask
        route = [(f, f ^ ((odd_mask if f % 2 else mask) << 1)) for f in range(self.nf)]
        return lax.ppermute(x, "fsdp", route)

    def along(self, x):
        route = []
        for z in range(self.nz):
            for f in range(self.nf):
                to = z + 1 if f % 2 == 0 else z - 1
                inside = 0 <= to < self.nz
                route.append((z * self.nf + f, to * self.nf + f if inside else z * self.nf + (f ^ 1)))
        return lax.ppermute(x, ("dp", "fsdp"), route)

    def gather_line(self, block, half):
        def part(x, which):
            return jnp.concatenate([lax.dynamic_slice_in_dim(x, which * half, half, 0), x[2 * half :]])

        got, now = [], block
        for _ in range(self.nz - 1):
            now = self.along(now)
            got.append(now)
        other = self.sibling(jnp.stack([part(x, 1 - self.core) for x in got]))
        row = jnp.concatenate([jnp.stack([part(x, self.core) for x in got + [block]]), other])
        out = []
        for z in range(self.nz):
            steps = jnp.abs(self.z - z)
            passed = jnp.where(self.even, z < self.z, z > self.z)
            at = jnp.where(passed, steps - 1, self.nz + steps - 1)
            out.append(pick(row, jnp.where(steps == 0, self.nz - 1, at)))
        return jnp.stack(out)

    def gather_square(self, block, bit):
        a, b = 1 << bit, 2 << bit
        first = self.hop(block, a, b)
        second = self.hop(block, b, a)
        return [block, first, second, self.hop(first, b, a)]

    def reduce_square(self, parts, bit):
        a, b = 1 << bit, 2 << bit
        here = (self.chip >> bit) % 4
        first = jnp.where(self.even, 1, 2)
        second = self.hop(parts(here ^ (3 - first)).astype(bf), b, a)
        corner = self.hop(parts(here ^ 3).astype(bf), b, a)
        moving = (parts(here ^ first) + corner.astype(f32)).astype(bf)
        first = self.hop(moving, a, b)
        return (parts(here) + first.astype(f32) + second.astype(f32)).astype(bf)

    def arranged(self, pieces, bit, odd):
        here = (self.chip >> bit) % 4
        stack = jnp.stack(pieces)
        at = [0, 1, 2, 3]
        swapped = jnp.where(odd, jnp.array([0, 2, 1, 3]), jnp.array(at))
        return jnp.stack([pick(stack, swapped[here ^ k]) for k in at])

    def gather_chips(self, now, n, R):
        half = n // 2
        bits = range(0, self.nq.bit_length() - 1, 2)
        for bit in bits[:-1]:
            now = self.arranged(self.gather_square(now, bit), bit, ~self.even)
            now = jnp.moveaxis(now, 0, -3)
        bit = bits[-1]
        mine = self.gather_square(now, bit)
        other = [self.sibling(piece) for piece in mine]
        more = self.arranged([piece[..., half * R :, :] for piece in mine], bit, ~self.even)
        more = jnp.moveaxis(more, 1, -3).reshape(self.nq, self.nz, -1, D)
        if R % 16 == 0 and len(bits) == 1:
            return place_units(self, mine, other, n, R), more
        mine = self.arranged([piece[..., : half * R, :] for piece in mine], bit, ~self.even)
        other = self.arranged([piece[..., : half * R, :] for piece in other], bit, self.even)
        units = ordered(self.even, mine, other)
        units = units.reshape((2, 4, self.nz, -1, half, R, D))
        units = jnp.transpose(units, (0, 4, 2, 1, 3, 5, 6))
        return units.reshape(n, D, D), more

    def scatter_whole(self, pairs):
        R = D // (self.nz * self.nq)
        others = [self.sibling(give) for _, give in pairs]
        bits = range(0, self.nq.bit_length() - 1, 2)

        def parts(i):
            blocks = []
            for (keep, _), other in zip(pairs, others):
                shape = (keep.shape[0], self.nz, 4, -1, R, D)
                block = pick(keep.reshape(shape), i, 2).astype(f32) + pick(other.reshape(shape), i, 2).astype(f32)
                blocks.append(jnp.swapaxes(block, 0, 1))
            return jnp.concatenate(blocks, axis=1)

        now = self.reduce_square(parts, bits[-1])
        for bit in reversed(bits[:-1]):
            whole_now = now.reshape(now.shape[:2] + (4, -1, R, D))
            now = self.reduce_square(lambda i: pick(whole_now, i, 2).astype(f32), bit)
        now = now.reshape(self.nz, -1, D)
        return lax.psum_scatter(now, "dp", scatter_dimension=0, tiled=False).reshape(-1, R, D)

    def gather_groups(self, x):
        out = x[None]
        for bit in range(2):
            got = self.hop(out, 1 << bit)
            upper = (self.chip >> bit) % 2 == 1
            out = jnp.concatenate([jnp.where(upper, got, out), jnp.where(upper, out, got)])
        return out

    def sum_groups(self, x):
        x = x + self.hop(x, 1, 2)
        return x + self.hop(x, 2, 1)

    def to_groups(self, blocks, combine):
        def at(mask):
            return jax.tree.map(lambda leaf: pick(leaf, self.group ^ mask), blocks)

        first = jnp.where(self.even, 1, 2)
        second = 3 - first
        pairs = jax.tree.map(lambda *leaves: jnp.stack(leaves), at(second), at(3))
        pairs = combine(jax.tree.map(lambda *leaves: jnp.stack(leaves), at(0), at(first)), pairs, (2, 1))
        out = combine(
            jax.tree.map(lambda leaf: leaf[0], pairs), jax.tree.map(lambda leaf: leaf[1], pairs), (1, 2)
        )
        bit = 2
        while (1 << bit) < self.nq:
            out = combine(out, out, (1 << bit, 1 << bit))
            bit += 1
        return out

    def owned_rows(self, mine, axis=0):
        own = lax.dynamic_slice_in_dim(mine, self.f * Q_DEV, Q_DEV, axis)
        give = lax.dynamic_slice_in_dim(mine, (self.f ^ 1) * Q_DEV, Q_DEV, axis)
        return ordered(self.even, own, self.sibling(give))


def split_three(x):
    hi = lax.reduce_precision(x, 8, 7)
    mid = lax.reduce_precision(x - hi, 8, 7)
    return [hi.astype(bf), mid.astype(bf), (x - hi - mid).astype(bf)]


def join_three(x):
    a, b, c = jnp.split(x.astype(f32), 3, axis=-1)
    return (a + b) + c


def columns(weight):
    rows, width = weight.shape
    return [weight[:, k * D : (k + 1) * D] for k in range(width // D)]


def strip_bias(place, bands, height):
    half = WIN // 2
    rows = (place.f % bands) * height + jnp.arange(height, dtype=jnp.int32)
    cols = (place.f // bands) * WIN + jnp.arange(WIN, dtype=jnp.int32)

    def label(at, total):
        return (at >= total - WIN).astype(jnp.int32) + (at >= total - half).astype(jnp.int32)

    labels = label(rows, height * bands)[:, None] * 3 + label(cols, WIN * WCOLS)
    labels = labels.reshape(height // WIN, PATCH)
    return jnp.where(labels[:, :, None] == labels[:, None, :], 0.0, -1e30).astype(f32)


def roll_in(x, place, bands):
    half = WIN // 2
    below = x[:, :half]
    if bands > 1:
        route = [(f // bands * bands + (f + 1) % bands, f) for f in range(place.nf)]
        below = lax.ppermute(below, "fsdp", route)
    x = jnp.concatenate([x[:, half:], below], axis=1)
    beside = lax.ppermute(x[:, :, :half], "fsdp", [((f + bands) % place.nf, f) for f in range(place.nf)])
    return jnp.concatenate([x[:, :, half:], beside], axis=2)


def roll_out(x, place, bands):
    half = WIN // 2
    beside = lax.ppermute(x[:, :, half:], "fsdp", [(f, (f + bands) % place.nf) for f in range(place.nf)])
    x = jnp.concatenate([beside, x[:, :, :half]], axis=2)
    above = x[:, -half:]
    if bands > 1:
        route = [(f, f // bands * bands + (f + 1) % bands) for f in range(place.nf)]
        above = lax.ppermute(above, "fsdp", route)
    return jnp.concatenate([above, x[:, :-half]], axis=1)


def local(
    visual,
    query_slots,
    lengths,
    slot_order,
    norm_window,
    window_qkv,
    window_out,
    norm_slots,
    slots_qkv,
    slots_out,
    norm_reader,
    norm_page,
    reader_qkv,
    reader_out,
    writer_qkv,
    writer_out,
    norm_visual_mlp,
    visual_up,
    visual_down,
    norm_query_mlp,
    query_up,
    query_down,
    visual_cot,
    query_cot,
):
    place = Place()
    nz, nf, nq, core, even = place.nz, place.nf, place.nq, place.core, place.even
    extra = nq // GROUPS
    bands = nf // WCOLS
    height = visual.shape[1]
    page_rows = height * WIN
    rows = MICRO * page_rows
    slots = Q_DEV * nf
    r = window_out.shape[0]
    R = 2 * r

    def chip_half(units):
        half = len(units) // 2
        flat = jnp.stack(units).reshape(2, half, r, D)
        got = place.sibling(pick(flat, 1 - core))
        both = ordered(even, pick(flat, core), got)
        return jnp.swapaxes(both, 0, 1).reshape(half, R, D)

    gains = jnp.stack([norm_window, norm_slots, norm_reader, norm_page, norm_visual_mlp, norm_query_mlp])
    gain_rows = jnp.zeros((8, D), bf).at[:6, :r].set(gains)
    units = columns(reader_qkv)[1:] + columns(writer_qkv)[:1] + columns(window_qkv)
    units = units + [window_out, writer_out, slots_out, reader_out]
    flat = jnp.concatenate(units + [gain_rows])
    other = place.sibling(flat)
    n = len(units)
    main = ordered(even, flat[: n * r], other[: n * r]).reshape(2, n, r, D)
    block = jnp.concatenate(
        [jnp.swapaxes(main, 0, 1).reshape(n * R, D), ordered(even, flat[n * r :], other[n * r :]).reshape(16, D)]
    )
    w_one, gain_all = place.gather_chips(place.gather_line(block, n // 2 * R), n, R)
    gain_all = gain_all.reshape(nq, nz, 2, 8, D)[:, :, :, :6, :r]
    gain_all = jnp.transpose(gain_all, (3, 1, 0, 2, 4)).reshape(6, 1, D).astype(f32)
    g_window, g_slots, g_reader, g_page, g_vmlp, g_qmlp = (gain_all[k] for k in range(6))
    one_unit = (1, D, D)

    def unit(u):
        return w_one, pl.BlockSpec(one_unit, lambda *_: (u, 0, 0), pipeline_mode=pl.Buffered(1))

    up = jnp.stack(columns(visual_up)).reshape(2, 2, r, D)
    up = ordered(even, pick(up, core), place.sibling(pick(up, 1 - core)))
    up = jnp.swapaxes(up, 0, 1).reshape(2 * R, D)
    now = lax.all_gather(jnp.concatenate([up, visual_down]), "dp")
    w_two = place.gather_chips(now, 8, R)[0]
    direct = R if R % 16 == 0 else 0

    def group_cols(weight):
        wide = weight.reshape(weight.shape[0], -1, GROUPS, GCOLS)
        return jnp.swapaxes(wide, 1, 2).reshape(weight.shape[0], GROUPS, -1)

    def hidden_cols(weight):
        wide = weight.reshape(weight.shape[0], nz, extra, GROUPS, 4 * D // (nz * nq))
        return jnp.transpose(wide, (0, 3, 1, 2, 4)).reshape(weight.shape[0], GROUPS, D)

    by_group = jnp.concatenate(
        [
            group_cols(slots_qkv),
            group_cols(reader_qkv[:, :D]),
            group_cols(writer_qkv[:, D:]),
            hidden_cols(query_up),
        ],
        axis=-1,
    )
    by_group = jnp.swapaxes(by_group, 0, 1)
    arrived = [pick(by_group, place.group)]
    for mask in range(1, nq):
        arrived.append(place.hop(pick(by_group, place.group ^ (mask % GROUPS)), mask))
    arrived = jnp.stack(arrived)
    arrived = jnp.stack([pick(arrived, place.chip ^ k) for k in range(nq)])
    width = arrived.shape[-1]
    downs = [query_down]
    for mask in range(GROUPS, nq, GROUPS):
        downs.append(place.hop(query_down, mask))
    downs = jnp.stack(downs)
    downs = jnp.stack([pick(downs, (place.chip // GROUPS) ^ k) for k in range(extra)])

    def col_half(x, which):
        half = x.shape[-1] // 2
        return lax.dynamic_slice_in_dim(x, which * half, half, x.ndim - 1)

    got = place.sibling(
        jnp.concatenate([col_half(arrived, 1 - core).reshape(nq * r, -1), col_half(downs, 1 - core).reshape(nq * r, -1)], axis=1)
    )
    cols = ordered(even, col_half(arrived, core), got[:, : width // 2].reshape(nq, r, -1))
    cols = jnp.swapaxes(cols, 0, 1).reshape(nq * R, -1)
    downs = ordered(even, col_half(downs, core), got[:, width // 2 :].reshape(extra, 2 * R, -1))
    downs = jnp.swapaxes(downs, 0, 1).reshape(nq * R, -1)
    mine = lax.all_gather(jnp.concatenate([cols, downs], axis=1), "dp").reshape(D, -1)
    other = place.sibling(mine)
    one, two = jnp.where(even, mine, other), jnp.where(even, other, mine)
    w_cols = jnp.concatenate([one[:, : width // 2], two[:, : width // 2]], axis=1)
    w_qdown = jnp.concatenate([one[:, width // 2 :], two[:, width // 2 :]], axis=1)
    w_sq, w_rd, w_qup = w_cols[:, : 3 * GCOLS], w_cols[:, 3 * GCOLS : 6 * GCOLS], w_cols[:, 6 * GCOLS :]

    ends = jnp.stack([query_slots, query_cot])
    give = pick(ends, 1 - core, 1)
    ends = ordered(even, pick(ends, core, 1), place.sibling(give))
    ends = jnp.swapaxes(ends, 0, 1).reshape(2, 2 * Q_DEV, D)
    bit = 0
    while (1 << bit) < nq:
        got = place.hop(ends, 1 << bit)
        upper = (place.chip >> bit) % 2 == 1
        ends = jnp.concatenate([jnp.where(upper, got, ends), jnp.where(upper, ends, got)], axis=1)
        bit += 1
    xs, xs_cot = ends[0], ends[1]

    bias = strip_bias(place, bands, height)
    x = roll_in(visual, place, bands).reshape(rows, D)
    cot = roll_in(visual_cot, place, bands).reshape(rows, D)

    positions = (slot_order[:, :, None] * Q_DEV + jnp.arange(Q_DEV, dtype=jnp.int32)).reshape(MICRO, slots)
    live = jnp.where(positions < lengths[:, None], 0.0, -1e30).astype(f32).reshape(MICRO, 1, slots)
    own_live = pick(live, core)

    mix_q, att_own = simple(
        slots_fwd, "slots_fwd", (xs, g_slots, w_sq, own_live), [((slots, 3 * GCOLS), bf), ((slots, GCOLS), bf)]
    )
    att_q = jnp.swapaxes(place.gather_groups(att_own), 0, 1).reshape(slots, D)
    s1, rd_own = simple(
        slots_mid, "slots_mid", (xs, att_q, unit(8), g_reader, w_rd), [((slots, D), f32), ((slots, 3 * GCOLS), bf)]
    )
    rd_page = place.gather_groups(rd_own)
    rd = ordered(even, rd_page, place.sibling(rd_page)).reshape(MICRO, GROUPS, slots, 3, GCOLS)
    rd = jnp.transpose(rd, (3, 0, 2, 1, 4)).reshape(3, MICRO, slots, D)
    rq, wk, wv = rd[0], rd[1], rd[2]

    act_block = per_page((page_rows, D), 0)
    mix, att, v1, pk = call(
        window_fwd,
        "window_fwd",
        (sds((3, rows, D), bf), sds((rows, D), bf), sds((rows, D), f32), sds((3, rows, D), bf)),
        [
            act_block,
            whole(bias.shape),
            whole((1, D)),
            whole((1, D)),
            whole((7, D, D)),
        ],
        (per_page((3, page_rows, D), 1), act_block, act_block, per_page((3, page_rows, D), 1)),
        (MICRO,),
        (x, bias, g_window, g_page, w_one),
        flops=2 * rows * 7 * D * D,
    )
    slot_block = per_page((1, slots, D), 0)
    stat_block = per_page((1, slots, 128), 0)

    def of_pk(u):
        return pl.BlockSpec((1, page_rows, D), lambda p: (u, p, 0))

    o_part, lse_part = call(
        read_fwd,
        "read_fwd",
        (sds((MICRO, slots, D), f32), sds((MICRO, slots, 128), f32)),
        [slot_block, of_pk(0), of_pk(1)],
        (slot_block, stat_block),
        (MICRO,),
        (rq, pk, pk),
        flops=2 * rows * slots * D * 4,
    )

    def merge(kept, sent, route):
        o, lse = kept
        message = jnp.concatenate(sent, axis=-1)
        got = place.sibling(message) if route is None else place.hop(message, *route)
        width = o.shape[-1]
        o_two, lse_two = got[..., :width], got[..., width:]
        top = jnp.maximum(lse, lse_two)
        a, b = jnp.exp(lse - top), jnp.exp(lse_two - top)
        share = jnp.repeat(a / (a + b), HEAD, axis=-1)
        return o * share + o_two * (1.0 - share), top + jnp.log(a + b)

    heads_part = lse_part[..., :HEADS]
    page_o, page_lse = merge(
        (pick(o_part, core), pick(heads_part, core)), (pick(o_part, 1 - core), pick(heads_part, 1 - core)), None
    )
    blocks = (
        jnp.swapaxes(page_o.reshape(slots, GROUPS, GCOLS), 0, 1),
        jnp.swapaxes(page_lse.reshape(slots, GROUPS, GHEADS), 0, 1),
    )
    reading, lse_own = place.to_groups(blocks, merge)
    message = jnp.concatenate([reading.astype(bf)] + split_three(lse_own), axis=-1)
    message = place.gather_groups(message)
    read_q = jnp.swapaxes(message[..., :GCOLS], 0, 1).reshape(slots, D)
    lse_page = jnp.swapaxes(join_three(message[..., GCOLS:]), 0, 1).reshape(slots, HEADS)

    s2, parts, d_qup, d_qdown = simple(
        query_mlp,
        "query_mlp",
        (s1, read_q, unit(9), g_qmlp, w_qup, w_qdown, xs_cot),
        [((slots, D), f32), ((2, slots, D), bf), ((D, D), bf), ((D, D), bf)],
    )
    sums = place.sum_groups(parts)
    q_out, ds2, d_read, dg_qmlp = simple(
        query_back,
        "query_back",
        (s2, sums, xs_cot, g_qmlp, unit(9)),
        [((slots, D), bf), ((slots, D), f32), ((slots, D), bf), ((1, D), f32)],
    )
    query_out = place.owned_rows(q_out)
    message = jnp.concatenate([d_read, read_q] + split_three(lse_page), axis=-1)
    message = ordered(even, message, place.sibling(message))
    d_read_all, read_all = message[..., :D], message[..., D : 2 * D]
    lse_all = jnp.pad(join_three(message[..., 2 * D :]), ((0, 0), (0, 0), (0, 128 - HEADS)))

    live_block = per_page((1, 1, slots), 0)
    writing, v2 = call(
        write_fwd,
        "write_fwd",
        (sds((rows, D), bf), sds((rows, D), f32)),
        [act_block, of_pk(2), slot_block, slot_block, live_block, unit(7)[1]],
        (act_block, act_block),
        (MICRO,),
        (v1, pk, wk, wv, live, w_one),
        flops=2 * rows * D * D,
    )
    chunk = 384
    steps = 4 * D // chunk
    per_unit = D // chunk
    flat_block = whole((rows, D))
    half_steps = steps // 2
    chips = max(chunk // (4 * R), 1)

    def once(*shape):
        return pl.BlockSpec(shape, lambda j, c: (0,) * len(shape), pipeline_mode=pl.Buffered(1))

    def up_at(j):
        u = j // per_unit
        return (u + u // 2 * 2, 0, j % per_unit)

    def half_at(half):
        def place_of(j, c):
            k = jnp.clip(j - half_steps * (c[0] if half == 0 else 1 - c[0]), 0, half_steps - 1)
            return (k // per_unit, 0, k % per_unit)

        return pl.BlockSpec((1, D, chunk), place_of)

    if direct:
        w_down = w_two.reshape(2, 4, nz * nq, R, D)
        down_block = pl.BlockSpec((2, 2, chips, R, D), lambda j, c: (0, 1, j, 0, 0))
        d_down_block = pl.BlockSpec((2, chips, R, D), lambda j, c: (0, j, 0, 0))
        d_down_shapes = [sds((2, nz * nq, R, D), bf)] * 2
    else:
        w_down = w_two.reshape(2, 2, 2, nz, nq, R, D)[:, 1]
        w_down = jnp.transpose(w_down, (2, 3, 0, 1, 4, 5)).reshape(4 * D, D)
        down_block = d_down_block = pl.BlockSpec((chunk, D), lambda j, c: (j, 0))
        d_down_shapes = [sds((4 * D, D), bf)] * 2
    core_id = core.astype(jnp.int32).reshape(1)
    v3, dv2, keep_up, give_up, keep_down, give_down, dg_vmlp = pl.pallas_call(
        partial(mlp_both, steps, direct),
        name="mlp_both",
        out_shape=(sds((rows, D), bf), sds((rows, D), f32), sds((2, D, D), bf), sds((2, D, D), bf))
        + tuple(d_down_shapes)
        + (sds((1, D), f32),),
        grid_spec=pltpu.PrefetchScalarGridSpec(
            num_scalar_prefetch=1,
            grid=(steps,),
            in_specs=[
                once(rows, D),
                once(1, D),
                pl.BlockSpec((1, D, chunk), lambda j, c: up_at(j)),
                down_block,
                once(rows, D),
            ],
            out_specs=(
                once(rows, D),
                once(rows, D),
                half_at(0),
                half_at(1),
                d_down_block,
                d_down_block,
                once(1, D),
            ),
            scratch_shapes=(
                pltpu.VMEM((rows, D), bf),
                pltpu.VMEM((rows, D), f32),
                pltpu.VMEM((rows, D), f32),
                pltpu.VMEM((chunk, D), bf),
            ),
        ),
        compiler_params=pltpu.CompilerParams(vmem_limit_bytes=58 * 1024 * 1024),
        cost_estimate=pl.CostEstimate(flops=2 * rows * 24 * D * D, bytes_accessed=1 << 24, transcendentals=0),
    )(core_id, v2, g_vmlp, w_two, w_down, cot)
    if not direct:
        units_down = jnp.transpose(keep_down.reshape(nz, nq, 2, 2, R, D), (2, 3, 0, 1, 4, 5))
        keep_down, give_down = pick(units_down, core), pick(units_down, 1 - core)
    keep_down, give_down = keep_down.reshape(2, D, D), give_down.reshape(2, D, D)
    mlp_pairs = [(keep_up, give_up), (keep_down, give_down)]
    visual_out = roll_out(v3.reshape(MICRO, height, WIN, D), place, bands)
    dwq, dwk, dwv, d_wo = call(
        write_bwd,
        "write_bwd",
        (sds((rows, D), bf), sds((MICRO, slots, D), bf), sds((MICRO, slots, D), bf), sds((D, D), bf)),
        [act_block, act_block, of_pk(2), slot_block, slot_block, live_block, unit(7)[1]],
        (act_block, slot_block, slot_block, whole((D, D))),
        (MICRO,),
        (dv2, writing, pk, wk, wv, live, w_one),
        scratch=(pltpu.VMEM((D, D), f32),),
        flops=4 * rows * D * D,
    )

    drq, dk, dv = call(
        read_bwd,
        "read_bwd",
        (sds((MICRO, slots, D), bf), sds((rows, D), bf), sds((rows, D), bf)),
        [slot_block, of_pk(0), of_pk(1), slot_block, slot_block, stat_block],
        (slot_block, act_block, act_block),
        (MICRO,),
        (rq, pk, pk, d_read_all, read_all, lse_all),
        flops=2 * rows * slots * D * 10,
    )
    core_block = pl.BlockSpec(memory_space=pltpu.SMEM)
    two_units = whole((2, D, D))
    dv1, keep_page, give_page, dg_page = call(
        page_bwd,
        "page_bwd",
        (sds((rows, D), f32), sds((2, D, D), bf), sds((2, D, D), bf), sds((1, D), f32)),
        [core_block]
        + [act_block, act_block, act_block, act_block, act_block, whole((1, D)), whole((3, D, D)), whole((D, D))],
        (act_block, two_units, two_units, whole((1, D))),
        (MICRO,),
        (core_id, v1, dv2, dk, dv, dwq, g_page, w_one, d_wo),
        scratch=(pltpu.VMEM((3, D, D), f32), pltpu.VMEM((1, D), f32)),
        flops=2 * rows * 6 * D * D,
    )
    three_block = per_page((3, page_rows, D), 1)
    dmix, keep_window, give_window = call(
        window_bwd,
        "window_bwd",
        (sds((3, rows, D), bf), sds((2, D, D), bf), sds((2, D, D), bf)),
        [core_block, act_block, act_block, three_block, act_block, whole(bias.shape), whole((1, D)), whole((7, D, D))],
        (three_block, two_units, two_units),
        (MICRO,),
        (core_id, dv1, x, mix, att, bias, g_window, w_one),
        scratch=(pltpu.VMEM((4, D, D), f32), pltpu.VMEM((page_rows, D), bf)),
        flops=2 * rows * 5 * D * D,
    )
    v_grad, dg_window = call(
        window_end,
        "window_end",
        (sds((rows, D), bf), sds((1, D), f32)),
        [act_block, act_block, three_block, whole((1, D)), whole((7, D, D))],
        (act_block, whole((1, D))),
        (MICRO,),
        (dv1, x, dmix, g_window, w_one),
        scratch=(pltpu.VMEM((1, D), f32),),
        flops=2 * rows * 3 * D * D,
    )
    visual_grad = roll_out(v_grad.reshape(MICRO, height, WIN, D), place, bands)

    def add(kept, sent, route):
        got = place.sibling(sent) if route is None else place.hop(sent, *route)
        return (kept.astype(f32) + got.astype(f32)).astype(bf)

    d_slots = jnp.stack([drq, dwk, dwv], axis=2)
    d_slots = add(pick(d_slots, core), pick(d_slots, 1 - core), None)
    d_slots = jnp.transpose(d_slots.reshape(slots, 3, GROUPS, GCOLS), (2, 0, 1, 3))
    d_rd = place.to_groups(d_slots.reshape(GROUPS, slots, 3 * GCOLS), add)
    part, d_rdw = simple(
        reader_back, "reader_back", (s1, g_reader, w_rd, d_rd), [((slots, D), bf), ((D, 3 * GCOLS), bf)]
    )
    drn = place.sum_groups(part)
    w_so_rows = lax.dynamic_slice(w_one, (8, place.group * GCOLS, 0), (1, GCOLS, D))
    ds1, part, d_sqw, dg_reader = simple(
        slots_back,
        "slots_back",
        (xs, s1, ds2, drn, g_reader, w_so_rows, mix_q, att_own, own_live, g_slots, w_sq),
        [((slots, D), f32), ((slots, D), bf), ((D, 3 * GCOLS), bf), ((1, D), f32)],
    )
    dxn = place.sum_groups(part)
    x_grad, dg_slots = simple(
        slots_end, "slots_end", (xs, g_slots, dxn, ds1), [((slots, D), bf), ((1, D), f32)]
    )
    query_grad = place.owned_rows(x_grad)

    def own_cols(grad):
        return lax.dynamic_slice_in_dim(grad, place.group * GCOLS, GCOLS, 1).astype(bf)

    d_so = t_dot(att_q, own_cols(ds1)).astype(bf)
    d_ro = t_dot(read_q, own_cols(ds2)).astype(bf)

    def own_units(mine):
        mine = jnp.swapaxes(mine.reshape(-1, 2, r, D), 0, 1)
        both = ordered(even, pick(mine, core), place.sibling(pick(mine, 1 - core)))
        return both.reshape(-1, r, D).astype(f32)

    mine = place.scatter_whole(mlp_pairs)
    grad_up = own_units(mine[:2])
    grad_down = mine[2:].reshape(2 * R, D).astype(f32)
    grad_page = own_units(place.scatter_whole([(keep_page, give_page)]))
    grad_win = own_units(place.scatter_whole([(keep_window, give_window)]))

    d_cols = jnp.concatenate([d_sqw, d_rdw, d_qup, d_so, d_ro], axis=1)
    width = d_cols.shape[1] // 2
    both = jnp.concatenate([col_half(d_cols, core), col_half(d_qdown, core)], axis=1).astype(f32)
    both = both + place.sibling(
        jnp.concatenate([col_half(d_cols, 1 - core), col_half(d_qdown, 1 - core)], axis=1)
    ).astype(f32)
    both = (both * (1.0 / extra)).astype(bf).reshape(nz, nq * R, -1)
    gain_rows = jnp.concatenate([dg_window, dg_page, dg_vmlp] + [g / nq for g in (dg_slots, dg_reader, dg_qmlp)])
    gain_rows = jnp.transpose(gain_rows.reshape(6, nz, nq, 2 * r), (1, 2, 0, 3)).reshape(nz, 1, nq * 12 * r)
    gain_rows = jnp.pad(gain_rows.astype(bf), ((0, 0), (0, 7), (0, both.shape[-1] - nq * 12 * r)))
    mine = lax.psum_scatter(jnp.concatenate([both, gain_rows], axis=1), "dp", scatter_dimension=0)
    cols = mine[: nq * R, :width].reshape(nq, R, width)
    gain_row = mine[nq * R, : nq * 12 * r].reshape(nq, 1, 12 * r)
    cols = jnp.concatenate([cols, jnp.pad(gain_row, ((0, 0), (0, 7), (0, width - 12 * r)))], axis=1)
    total = [pick(cols, place.chip).astype(f32)]
    for mask in range(1, nq):
        total.append(place.hop(pick(cols, place.chip ^ mask), mask).astype(f32))
    gain_sum = sum(part[R, : 12 * r] for part in total)
    total = jnp.stack([part[:R] for part in total])
    by_group = jnp.stack(
        [sum(pick(total, place.chip ^ (k + GROUPS * e)) for e in range(extra)) for k in range(GROUPS)]
    )
    downs = mine[: nq * R, width:].reshape(extra, 4 * R, -1) * jnp.asarray(extra, bf)
    downs = pick(downs, place.chip // GROUPS)

    def halved(x, axis, which):
        half = x.shape[axis] // 2
        return lax.dynamic_slice_in_dim(x, which * half, half, axis)

    give = jnp.concatenate(
        [
            halved(by_group, 1, 1 - core).reshape(-1).astype(f32),
            halved(downs, 0, 1 - core).reshape(-1).astype(f32),
            gain_sum,
        ]
    )
    got = place.sibling(give)
    cut = GROUPS * r * width
    by_group = ordered(even, halved(by_group, 1, core), got[:cut].reshape(GROUPS, r, width))
    by_group = jnp.transpose(by_group, (1, 2, 0, 3)).reshape(GROUPS, r, 2 * width)
    downs = ordered(even, halved(downs, 0, core).astype(f32), got[cut : -12 * r].reshape(2 * R, -1))
    grad_qdown = jnp.swapaxes(downs, 0, 1).reshape(2 * R, D)
    both = pick((gain_sum + got[-12 * r :]).reshape(6, 2, r), core, 1)

    def columns_back(part):
        wide = part.reshape(GROUPS, r, -1, GCOLS)
        return jnp.transpose(wide, (1, 2, 0, 3)).reshape(r, -1)

    grad_sq = columns_back(by_group[..., : 3 * GCOLS])
    grad_rd = columns_back(by_group[..., 3 * GCOLS : 6 * GCOLS])
    hidden = by_group[..., 6 * GCOLS : 10 * GCOLS].reshape(GROUPS, r, nz, extra, 4 * D // (nz * nq))
    grad_qup = jnp.transpose(hidden, (1, 2, 3, 0, 4)).reshape(r, 4 * D)
    grad_so = columns_back(by_group[..., 10 * GCOLS : 11 * GCOLS])
    grad_ro = columns_back(by_group[..., 11 * GCOLS :])

    def wide(units):
        return jnp.concatenate([units[k] for k in range(units.shape[0])], axis=1)

    return (
        visual_out,
        query_out,
        visual_grad,
        query_grad,
        both[0],
        wide(grad_win[:3]),
        grad_win[3],
        both[3],
        grad_sq,
        grad_so,
        both[4],
        both[1],
        jnp.concatenate([grad_rd[:, :D], wide(grad_page[:2])], axis=1),
        grad_ro,
        jnp.concatenate([grad_page[2], grad_rd[:, D:]], axis=1),
        grad_page[3],
        both[2],
        wide(grad_up),
        grad_down,
        both[5],
        grad_qup,
        grad_qdown,
    )


def solution(mesh):
    page = P("dp", "fsdp", None, None)
    slot = P("dp", "fsdp", None)
    gain = P(("dp", "fsdp"))
    matrix = P(("dp", "fsdp"), None)
    weights = (
        gain,
        matrix,
        matrix,
        gain,
        matrix,
        matrix,
        gain,
        gain,
        matrix,
        matrix,
        matrix,
        matrix,
        gain,
        matrix,
        matrix,
        gain,
        matrix,
        matrix,
    )
    return jax.shard_map(
        local,
        mesh=mesh,
        in_specs=(page, slot, P("dp"), P("dp", None)) + weights + (page, slot),
        out_specs=(page, slot, page, slot) + weights,
        check_vma=False,
    )
```

profile of v0, /device:TPU:0, one launch (start us, length us, event | category | flops | bytes accessed | tf_op | source)
XLA Modules:
  0.0 738.9 jit_solution(17826067911453336950)
XLA Ops:
  24.9 7.7 %collective-permute-done.2 = bf16[496,768]{1,0:T(8,128)(2,1)S(1)} collective-permute-done((bf16[496,768]{1,0:T(8,128)(2,1)S(1)}, bf16[496,768]{1,0:T(8,128)(2,1)S(1)}, u32[]{:S(2)}, u32[]{:S(2)}) %collective-permute-start.2) | collective-permute-done | bytes 761888 | tf_op jit(solution)/shard_map/ppermute | solution.py:612
  37.4 7.0 collective-permute-done.3
  47.9 24.5 %collective-permute-done.4 = bf16[496,768]{1,0:T(8,128)(2,1)S(1)} collective-permute-done((bf16[496,768]{1,0:T(8,128)(2,1)S(1)}, bf16[496,768]{1,0:T(8,128)(2,1)S(1)}, u32[]{:S(2)}, u32[]{:S(2)}) %collective-permute-start.4) | collective-permute-done | bytes 761888 | tf_op jit(solution)/shard_map/ppermute | solution.py:612
  98.6 8.4 %collective-permute-done.14 = bf16[2,32,768]{2,1,0:T(8,128)(2,1)S(1)} collective-permute-done((bf16[2,32,768]{2,1,0:T(8,128)(2,1)S(1)}, bf16[2,32,768]{2,1,0:T(8,128)(2,1)S(1)}, u32[]{:S(2)}, u32[]{:S(2)}) %collective-permute-start.14) | collective-permute-done | bytes 98336 | tf_op jit(solution)/shard_map/ppermute | solution.py:603
  108.1 12.3 %collective-permute-done.15 = bf16[2,64,768]{2,1,0:T(8,128)(2,1)S(1)} collective-permute-done((bf16[2,64,768]{2,1,0:T(8,128)(2,1)S(1)}, bf16[2,64,768]{2,1,0:T(8,128)(2,1)S(1)}, u32[]{:S(2)}, u32[]{:S(2)}) %collective-permute-start.15) | collective-permute-done | bytes 196640 | tf_op jit(solution)/shard_map/ppermute | solution.py:603
  162.7 9.7 %place_units.2 = bf16[10,4,4,48,768]{4,3,2,1,0:T(8,128)(2,1)} custom-call(s32[2]{0:T(128)} %pad_add_fusion.table_ref, bf16[4,256,768]{2,1,0:T(8,128)(2,1)} %pad_maximum_fusion.5.refs_0_, bf16[4,256,768]{2,1,0:T(8,128)(2,1)} %collective-permute-done.6.refs_1_, bf16[4,256,768]{2,1,0:T(8,128)(2,1)} %collective-permute-done.7.refs_2_, ...), custom_call_target="tpu_custom_call" | custom-call | bytes 23592960 | tf_op jit(solution)/shard_map/place_units/pallas_call | solution.py:564
  192.6 6.6 all-gather.7.cloned.1.call-done
  204.6 22.6 %window_fwd.1 = (bf16[3,864,768]{2,1,0:T(8,128)(2,1)}, bf16[864,768]{1,0:T(8,128)(2,1)}, f32[864,768]{1,0:T(8,128)}, bf16[3,864,768]{2,1,0:T(8,128)(2,1)}) custom-call(bf16[864,768]{1,0:T(8,128)(2,1)} %reshape.1133.x_ref, f32[3,144,144]{2,1,0:T(8,128)} %compare_select_fusion.bias_ref, f32[1,768]{1,0:T(1,128)} %squeeze.273.gw_ref, f32[1,768]{1,0:T(1,128)} %squeeze.274.gp_ref, ...), custom_call_target="tpu_custom_call" | custom-call | flops 7134511104 | bytes 1048576 | tf_op jit(solution)/shard_map/window_fwd/pallas_call | solution.py:108
  235.8 6.3 read_fwd.1
  263.2 6.8 collective-permute-done.28.refs_2_
  270.1 12.5 %collective-permute-done.29.refs_3_ = bf16[4,192,768]{2,1,0:T(8,128)(2,1)} collective-permute-done((bf16[4,192,768]{2,1,0:T(8,128)(2,1)}, bf16[4,192,768]{2,1,0:T(8,128)(2,1)}, u32[]{:S(2)}, u32[]{:S(2)}) %collective-permute-start.29) | collective-permute-done | bytes 1179680 | tf_op jit(solution)/shard_map/ppermute | solution.py:603
  288.2 12.8 %collective-permute-start.34 = (bf16[2,36,6,768]{3,0,2,1:T(2,128)(2,1)}, bf16[2,36,6,768]{3,0,2,1:T(2,128)(2,1)}, u32[]{:S(2)}, u32[]{:S(2)}) collective-permute-start(bf16[2,36,6,768]{3,0,2,1:T(2,128)(2,1)} %get-tuple-element.264), channel_id=1, source_target_pairs={{1,0},{2,1},{3,2},{4,3},{5,4},{6,5},{7,6},{0,7},{9,8},{10,9},{11,1... | collective-permute-start | bytes 1990664 | tf_op jit(solution)/shard_map/ppermute | solution.py:766
  320.0 8.3 %place_units.3 = bf16[8,4,4,48,768]{4,3,2,1,0:T(8,128)(2,1)} custom-call(s32[2]{0:T(128)} %pad_add_fusion.table_ref, bf16[4,192,768]{2,1,0:T(8,128)(2,1)} %bitcast.86.refs_0_, bf16[4,192,768]{2,1,0:T(8,128)(2,1)} %collective-permute-done.27.refs_1_, bf16[4,192,768]{2,1,0:T(8,128)(2,1)} %collective-permute-done.28.refs_2_, ...), custom_call_target="tpu_custom_call" | custom-call | bytes 18874368 | tf_op jit(solution)/shard_map/place_units/pallas_call | solution.py:564
  332.6 8.0 %write_fwd.1 = (bf16[864,768]{1,0:T(8,128)(2,1)}, f32[864,768]{1,0:T(8,128)}) custom-call(f32[864,768]{1,0:T(8,128)} %get-tuple-element.85.v1_ref, bf16[3,864,768]{2,1,0:T(8,128)(2,1)} %get-tuple-element.86.wq_ref.k_ref.v_ref, bf16[2,128,768]{2,1,0:T(8,128)(2,1)} %copy.380.wk_ref, bf16[2,128,768]{2,1,0:T(8,128)(2,1)} %copy.381.wv_ref, ...), custom_call_target="tpu_custom_call" | custom-call | flops 1019215872 | bytes 1048576 | tf_op jit(solution)/shard_map/write_fwd/pallas_call | solution.py:108
  354.7 54.3 %mlp_both.1 = (bf16[864,768]{1,0:T(8,128)(2,1)}, f32[864,768]{1,0:T(8,128)}, bf16[2,768,768]{2,1,0:T(8,128)(2,1)}, bf16[2,768,768]{2,1,0:T(8,128)(2,1)}, bf16[2,...) custom-call(s32[1]{0:T(128)} %bitcast.core_ref, ...), custom_call_target="tpu_custom_call" | custom-call | flops 24461180928 | bytes 16777216 | tf_op jit(solution)/shard_map/mlp_both/pallas_call | solution.py:1053
  409.6 14.6 %write_bwd.1 = (bf16[864,768]{1,0:T(8,128)(2,1)}, bf16[2,128,768]{2,1,0:T(8,128)(2,1)}, bf16[2,128,768]{2,1,0:T(8,128)(2,1)}, bf16[768,768]{1,0:T(8,128)(2,1)}) custom-call(f32[864,768]{1,0:T(8,128)} %get-tuple-element.97.dv2_ref, bf16[864,768]{1,0:T(8,128)(2,1)} %get-tuple-element.101.wr_ref, bf16[3,864,768]{2,1,0:T(8,128)(2,1)} %get-tuple-element.86.wq_ref.k_ref.v_ref, ...), custom_call_target="tpu_custom_call" | custom-call | flops 2038431744 | bytes 1048576 | tf_op jit(solution)/shard_map/write_bwd/pallas_call | solution.py:108
  427.2 8.7 %read_bwd.1 = (bf16[2,128,768]{2,1,0:T(8,128)(2,1)}, bf16[864,768]{1,0:T(8,128)(2,1)}, bf16[864,768]{1,0:T(8,128)(2,1)}) custom-call(bf16[2,128,768]{2,1,0:T(8,128)(2,1)} %copy.386.rq_ref, bf16[3,864,768]{2,1,0:T(8,128)(2,1)} %get-tuple-element.86.wq_ref.k_ref.v_ref, bf16[3,864,768]{2,1,0:T(8,128)(2,1)} %get-tuple-element.86.wq_ref.k_ref.v_ref, ...), custom_call_target="tpu_custom_call" | custom-call | flops 1698693120 | bytes 1048576 | tf_op jit(solution)/shard_map/read_bwd/pallas_call | solution.py:108
  437.7 15.8 %page_bwd.1 = (f32[864,768]{1,0:T(8,128)}, bf16[2,768,768]{2,1,0:T(8,128)(2,1)}, bf16[2,768,768]{2,1,0:T(8,128)(2,1)}, f32[1,768]{1,0:T(1,128)}) custom-call(s32[1]{0:T(128)} %bitcast.core_ref, f32[864,768]{1,0:T(8,128)} %get-tuple-element.85.v1_ref, f32[864,768]{1,0:T(8,128)} %get-tuple-element.97.dv2_ref, bf16[864,768]{1,0:T(8,128)(2,1)} %get-tuple-element.99.dk_ref, ...), custom_call_target="tpu_custom_call" | custom-call | flops 6115295232 | bytes 1048576 | tf_op jit(solution)/shard_map/page_bwd/pallas_call | solution.py:108
  453.4 33.9 %window_bwd.1 = (bf16[3,864,768]{2,1,0:T(8,128)(2,1)}, bf16[2,768,768]{2,1,0:T(8,128)(2,1)}, bf16[2,768,768]{2,1,0:T(8,128)(2,1)}) custom-call(s32[1]{0:T(128)} %bitcast.core_ref, f32[864,768]{1,0:T(8,128)} %get-tuple-element.104.dv1_ref, bf16[864,768]{1,0:T(8,128)(2,1)} %reshape.1133.x_ref, bf16[3,864,768]{2,1,0:T(8,128)(2,1)} %get-tuple-element.105.mix_ref, ...), custom_call_target="tpu_custom_call" | custom-call | flops 5096079360 | bytes 1048576 | tf_op jit(solution)/shard_map/window_bwd/pallas_call | solution.py:108
  551.1 20.0 %collective-permute-done.67 = bf16[4,2,1,48,768]{4,3,1,0,2:T(8,128)(2,1)} collective-permute-done((bf16[4,2,1,48,768]{4,3,1,0,2:T(8,128)(2,1)}, bf16[4,2,1,48,768]{4,3,1,0,2:T(8,128)(2,1)}, u32[]{:S(2)}, u32[]{:S(2)}) %collective-permute-start.67) | collective-permute-done | bytes 589856 | tf_op jit(solution)/shard_map/ppermute | solution.py:603
  594.3 7.5 %collective-permute-done.72 = bf16[4,4,1,48,768]{4,3,0,1,2:T(8,128)(2,1)S(1)} collective-permute-done((bf16[4,4,1,48,768]{4,3,0,1,2:T(8,128)(2,1)}, bf16[4,4,1,48,768]{4,3,0,1,2:T(8,128)(2,1)S(1)}, u32[]{:S(2)}, u32[]{:S(2)}) %collective-permute-start.72) | collective-permute-done | bytes 1179680 | tf_op jit(solution)/shard_map/ppermute | solution.py:603
  607.5 10.1 %window_end.1 = (bf16[864,768]{1,0:T(8,128)(2,1)}, f32[1,768]{1,0:T(1,128)}) custom-call(f32[864,768]{1,0:T(8,128)} %get-tuple-element.104.dv1_ref, bf16[864,768]{1,0:T(8,128)(2,1)} %reshape.1133.x_ref, bf16[3,864,768]{2,1,0:T(8,128)(2,1)} %get-tuple-element.107.dmix_ref, f32[1,768]{1,0:T(1,128)} %squeeze.273.gw_ref, bf16[10,768,768]{2,1,0:T(8,128)(2,1)} %bitcast.584), custom_call_target="tpu_custom_call" | custom-call | flops 3057647616 | bytes 1048576 | tf_op jit(solution)/shard_map/window_end/pallas_call | solution.py:108
  643.5 8.6 %collective-permute-done.35 = bf16[2,36,6,768]{3,0,2,1:T(2,128)(2,1)} collective-permute-done((bf16[2,36,6,768]{3,0,2,1:T(2,128)(2,1)}, bf16[2,36,6,768]{3,0,2,1:T(2,128)(2,1)}, u32[]{:S(2)}, u32[]{:S(2)}) %collective-permute-start.35) | collective-permute-done | bytes 663584 | tf_op jit(solution)/shard_map/ppermute | solution.py:772
  674.6 33.6 %reduce-scatter.5.cloned.1.call-done = bf16[1,200,1536]{2,1,0:T(8,128)(2,1)} async-done(((bf16[4,200,1536]{2,1,0:T(8,128)(2,1)}), bf16[1,200,1536]{2,1,0:T(8,128)(2,1)}) %reduce-scatter.5.cloned.1.call-update) | async-done | bytes 614416 | tf_op jit(solution)/shard_map/reduce_scatter | solution.py:1207
  (654 shorter events, 353.6 us)
Async XLA Ops:
  7.2 83.0 %all-gather.5.cloned.1.call-start = ((), (), s32[]{:S(2)}) async-start(), calls=%async_computation.8 | async-start | bytes 2703360 | tf_op jit(solution)/shard_map/all_gather | solution.py:893
  17.2 79.9 %collective-permute-start.13 = (bf16[2,16,768]{2,1,0:T(8,128)(2,1)}, bf16[2,16,768]{2,1,0:T(8,128)(2,1)}, u32[]{:S(2)}, u32[]{:S(2)}) collective-permute-start(bf16[2,16,768]{2,1,0:T(8,128)(2,1)} %fusion.65), channel_id=1, source_target_pairs={{0,1},{1,0},{2,3},{3,2},{4,5},{5,4},{6,7},{7,6},{8,9},{9,8},{10,11... | collective-permute-start | bytes 147464 | tf_op jit(solution)/shard_map/ppermute | solution.py:598
  24.5 82.7 %collective-permute-start.26 = (bf16[2,24,768]{2,1,0:T(8,128)(2,1)}, bf16[2,24,768]{2,1,0:T(8,128)(2,1)}, u32[]{:S(2)}, u32[]{:S(2)}) collective-permute-start(bf16[2,24,768]{2,1,0:T(8,128)(2,1)} %dynamic-slice_bitcast_fusion.17), channel_id=1, source_target_pairs={{0,1},{1,0},{2,3},{3,2},{4,5},{5,4},{6,7},{7,6},{8,9},{9,8},{10,11... | collective-permute-start | bytes 221192 | tf_op jit(solution)/shard_map/ppermute | solution.py:598
  37.4 161.8 %all-gather.7.cloned.1.call-start = ((), (), s32[]{:S(2)}) async-start(), calls=%async_computation.9 | async-start | bytes 1474560 | tf_op jit(solution)/shard_map/all_gather | solution.py:848
  80.9 39.6 %collective-permute-start.6 = (bf16[4,256,768]{2,1,0:T(8,128)(2,1)}, bf16[4,256,768]{2,1,0:T(8,128)(2,1)}, u32[]{:S(2)}, u32[]{:S(2)}) collective-permute-start(bf16[4,256,768]{2,1,0:T(8,128)(2,1)} %pad_maximum_fusion.5.refs_0_), channel_id=1, source_target_pairs={{0,2},{1,5},{2,0},{3,7},{4,6},{5,1},{6,4},{7,3},{8,10},{9,13},{10,... | collective-permute-start | bytes 4718600 | tf_op jit(solution)/shard_map/ppermute | solution.py:603
  94.4 36.5 %collective-permute-start.20 = (bf16[768,1344]{0,1:T(8,128)(2,1)}, bf16[768,1344]{0,1:T(8,128)(2,1)S(1)}, u32[]{:S(2)}, u32[]{:S(2)}) collective-permute-start(bf16[768,1344]{0,1:T(8,128)(2,1)} %copy.370), channel_id=1, source_target_pairs={{0,1},{1,0},{2,3},{3,2},{4,5},{5,4},{6,7},{7,6},{8,9},{9,8},{10,11... | collective-permute-start | bytes 6193160 | tf_op jit(solution)/shard_map/ppermute | solution.py:598
  121.6 41.1 %collective-permute-start.9 = (bf16[4,256,768]{2,1,0:T(8,128)(2,1)}, bf16[4,256,768]{2,1,0:T(8,128)(2,1)}, u32[]{:S(2)}, u32[]{:S(2)}) collective-permute-start(bf16[4,256,768]{2,1,0:T(8,128)(2,1)} %pad_maximum_fusion.5.refs_0_), channel_id=1, source_target_pairs={{0,1},{1,0},{2,3},{3,2},{4,5},{5,4},{6,7},{7,6},{8,9},{9,8},{10,11... | collective-permute-start | bytes 4718600 | tf_op jit(solution)/shard_map/ppermute | solution.py:598
  153.0 512.6 %reduce-scatter.9.cloned.1.call-start = ((), (), s32[]{:S(2)}) async-start(), calls=%async_computation.6 | async-start | bytes 737280 | tf_op jit(solution)/shard_map/reduce_scatter | solution.py:693
  199.2 53.2 %collective-permute-start.27 = (bf16[4,192,768]{2,1,0:T(8,128)(2,1)}, bf16[4,192,768]{2,1,0:T(8,128)(2,1)}, u32[]{:S(2)}, u32[]{:S(2)}) collective-permute-start(bf16[4,192,768]{2,1,0:T(8,128)(2,1)} %bitcast.86.refs_0_), channel_id=1, source_target_pairs={{0,2},{1,5},{2,0},{3,7},{4,6},{5,1},{6,4},{7,3},{8,10},{9,13},{10,... | collective-permute-start | bytes 3538952 | tf_op jit(solution)/shard_map/ppermute | solution.py:603
  262.7 57.3 %collective-permute-start.30 = (bf16[4,192,768]{2,1,0:T(8,128)(2,1)}, bf16[4,192,768]{2,1,0:T(8,128)(2,1)}, u32[]{:S(2)}, u32[]{:S(2)}) collective-permute-start(bf16[4,192,768]{2,1,0:T(8,128)(2,1)} %bitcast.86.refs_0_), channel_id=1, source_target_pairs={{0,1},{1,0},{2,3},{3,2},{4,5},{5,4},{6,7},{7,6},{8,9},{9,8},{10,11... | collective-permute-start | bytes 3538952 | tf_op jit(solution)/shard_map/ppermute | solution.py:598
  262.7 57.3 %collective-permute-start.31 = (bf16[4,192,768]{2,1,0:T(8,128)(2,1)}, bf16[4,192,768]{2,1,0:T(8,128)(2,1)}, u32[]{:S(2)}, u32[]{:S(2)}) collective-permute-start(bf16[4,192,768]{2,1,0:T(8,128)(2,1)} %collective-permute-done.27.refs_1_), channel_id=1, source_target_pairs={{0,1},{1,0},{2,3},{3,2},{4,5},{5,4},{6,7},{7,6},{8,9},{9,8},{10,11... | collective-permute-start | bytes 3538952 | tf_op jit(solution)/shard_map/ppermute | solution.py:598
  270.0 50.0 %collective-permute-start.32 = (bf16[4,192,768]{2,1,0:T(8,128)(2,1)}, bf16[4,192,768]{2,1,0:T(8,128)(2,1)}, u32[]{:S(2)}, u32[]{:S(2)}) collective-permute-start(bf16[4,192,768]{2,1,0:T(8,128)(2,1)} %collective-permute-done.28.refs_2_), channel_id=1, source_target_pairs={{0,1},{1,0},{2,3},{3,2},{4,5},{5,4},{6,7},{7,6},{8,9},{9,8},{10,11... | collective-permute-start | bytes 3538952 | tf_op jit(solution)/shard_map/ppermute | solution.py:598
  282.6 37.3 %collective-permute-start.33 = (bf16[4,192,768]{2,1,0:T(8,128)(2,1)}, bf16[4,192,768]{2,1,0:T(8,128)(2,1)}, u32[]{:S(2)}, u32[]{:S(2)}) collective-permute-start(bf16[4,192,768]{2,1,0:T(8,128)(2,1)} %collective-permute-done.29.refs_3_), channel_id=1, source_target_pairs={{0,1},{1,0},{2,3},{3,2},{4,5},{5,4},{6,7},{7,6},{8,9},{9,8},{10,11... | collective-permute-start | bytes 3538952 | tf_op jit(solution)/shard_map/ppermute | solution.py:598
  354.6 70.7 %collective-permute-start.44 = (bf16[128,1572]{1,0:T(8,128)(2,1)S(1)}, bf16[128,1572]{1,0:T(8,128)(2,1)S(1)}, u32[]{:S(2)}, u32[]{:S(2)}) collective-permute-start(bf16[128,1572]{1,0:T(8,128)(2,1)S(1)} %concatenate.217), channel_id=1, source_target_pairs={{0,1},{1,0},{2,3},{3,2},{4,5},{5,4},{6,7},{7,6},{8,9},{9,8},{10,11... | collective-permute-start | bytes 1207304 | tf_op jit(solution)/shard_map/ppermute | solution.py:598
  409.0 93.8 %collective-permute-start.69 = (bf16[2,768,768]{2,1,0:T(8,128)(2,1)}, bf16[2,768,768]{2,1,0:T(8,128)(2,1)}, u32[]{:S(2)}, u32[]{:S(2)}) collective-permute-start(bf16[2,768,768]{2,1,0:T(8,128)(2,1)} %get-tuple-element.133), channel_id=1, source_target_pairs={{0,1},{1,0},{2,3},{3,2},{4,5},{5,4},{6,7},{7,6},{8,9},{9,8},{10,11... | collective-permute-start | bytes 7077896 | tf_op jit(solution)/shard_map/ppermute | solution.py:598
  409.5 102.5 %collective-permute-start.70 = (bf16[2,768,768]{2,1,0:T(8,128)(2,1)}, bf16[2,768,768]{2,1,0:T(8,128)(2,1)}, u32[]{:S(2)}, u32[]{:S(2)}) collective-permute-start(bf16[2,768,768]{2,1,0:T(8,128)(2,1)} %bitcast.662), channel_id=1, source_target_pairs={{0,1},{1,0},{2,3},{3,2},{4,5},{5,4},{6,7},{7,6},{8,9},{9,8},{10,11... | collective-permute-start | bytes 7077896 | tf_op jit(solution)/shard_map/ppermute | solution.py:598
  437.1 53.0 %collective-permute-start.46 = (bf16[128,3,768]{2,0,1:T(8,128)(2,1)S(1)}, bf16[128,3,768]{2,0,1:T(8,128)(2,1)S(1)}, u32[]{:S(2)}, u32[]{:S(2)}) collective-permute-start(bf16[128,3,768]{2,0,1:T(8,128)(2,1)S(1)} %dynamic-slice_bitcast_fusion), channel_id=1, source_target_pairs={{0,1},{1,0},{2,3},{3,2},{4,5},{5,4},{6,7},{7,6},{8,9},{9,8},{10,11... | collective-permute-start | bytes 1769480 | tf_op jit(solution)/shard_map/ppermute | solution.py:598
  525.4 57.2 %collective-permute-start.71 = (bf16[4,4,1,48,768]{4,3,0,1,2:T(8,128)(2,1)}, bf16[4,4,1,48,768]{4,3,0,1,2:T(8,128)(2,1)}, u32[]{:S(2)}, u32[]{:S(2)}) collective-permute-start(bf16[4,4,1,48,768]{4,3,0,1,2:T(8,128)(2,1)} %pad_maximum_fusion.11), channel_id=1, source_target_pairs={{0,4},{1,3},{2,6},{3,1},{4,0},{5,7},{6,2},{7,5},{8,12},{9,11},{10,... | collective-permute-start | bytes 3538952 | tf_op jit(solution)/shard_map/ppermute | solution.py:603
  527.5 66.8 %collective-permute-start.73 = (bf16[4,4,1,48,768]{4,3,0,1,2:T(8,128)(2,1)}, bf16[4,4,1,48,768]{4,3,0,1,2:T(8,128)(2,1)}, u32[]{:S(2)}, u32[]{:S(2)}) collective-permute-start(bf16[4,4,1,48,768]{4,3,0,1,2:T(8,128)(2,1)} %pad_maximum_fusion.12), channel_id=1, source_target_pairs={{0,4},{1,3},{2,6},{3,1},{4,0},{5,7},{6,2},{7,5},{8,12},{9,11},{10,... | collective-permute-start | bytes 3538952 | tf_op jit(solution)/shard_map/ppermute | solution.py:603
  540.6 36.9 %collective-permute-start.60 = (bf16[4,2,1,48,768]{4,3,1,0,2:T(8,128)(2,1)}, bf16[4,2,1,48,768]{4,3,1,0,2:T(8,128)(2,1)}, u32[]{:S(2)}, u32[]{:S(2)}) collective-permute-start(bf16[4,2,1,48,768]{4,3,1,0,2:T(8,128)(2,1)} %fusion.17), channel_id=1, source_target_pairs={{0,4},{1,3},{2,6},{3,1},{4,0},{5,7},{6,2},{7,5},{8,12},{9,11},{10,... | collective-permute-start | bytes 1769480 | tf_op jit(solution)/shard_map/ppermute | solution.py:603
  574.7 92.3 %reduce-scatter.7.cloned.1.call-start = ((), (), s32[]{:S(2)}) async-start(), calls=%async_computation.5 | async-start | bytes 737280 | tf_op jit(solution)/shard_map/reduce_scatter | solution.py:693
  591.5 80.1 %reduce-scatter.11.cloned.1.call-start = ((), (), s32[]{:S(2)}) async-start(), calls=%async_computation.7 | async-start | bytes 1474560 | tf_op jit(solution)/shard_map/reduce_scatter | solution.py:693
  593.2 40.7 %collective-permute-start.54 = (bf16[768,1536]{1,0:T(8,128)(2,1)}, bf16[768,1536]{1,0:T(8,128)(2,1)}, u32[]{:S(2)}, u32[]{:S(2)}) collective-permute-start(bf16[768,1536]{1,0:T(8,128)(2,1)} %pad_maximum_fusion), channel_id=1, source_target_pairs={{0,1},{1,0},{2,3},{3,2},{4,5},{5,4},{6,7},{7,6},{8,9},{9,8},{10,11... | collective-permute-start | bytes 7077896 | tf_op jit(solution)/shard_map/ppermute | solution.py:598
  604.7 103.6 %reduce-scatter.5.cloned.1.call-start = ((), (), s32[]{:S(2)}) async-start(), calls=%async_computation.4 | async-start | bytes 3072000 | tf_op jit(solution)/shard_map/reduce_scatter | solution.py:1207
  (132 other events, 1273.4 us)
Sparse Core Ops, SparseCore 0:
  37.5 51.3 all-gather.4
  153.1 46.0 all-gather.6
  574.9 30.5 reduce-scatter.8
  607.6 20.4 reduce-scatter.6
  630.2 27.4 reduce-scatter.10
  659.9 48.2 reduce-scatter.4
where the time goes:
time: 750 us; the launch traced here: 739 us
  Pallas kernels  218 us (29%)
  waiting for transfers between devices  207 us (28%)
  local copies, waits for them, and re-layouts  110 us (15%)
  other arithmetic  97.6 us (13%)
  starting transfers between devices  79.2 us (11%)
  between operations  24.7 us (3%)
    pallas_call x15, Pallas kernels, call(): pl.pallas_call(body, name=name, out_shape=out_shape, grid=grid, in_specs=...  146 us
    ppermute x39, waiting for transfers between devices, hop(): return lax.ppermute(x, 'fsdp', route)  116 us
    pallas_call x1, Pallas kernels, local(): pl.pallas_call(partial(mlp_both, steps, direct), name='mlp_both', out_sha...  54.3 us
    ppermute x3, waiting for transfers between devices, along(): return lax.ppermute(x, ('dp', 'fsdp'), route)  39.2 us
    ppermute x39, starting transfers between devices, hop(): return lax.ppermute(x, 'fsdp', route)  37.7 us
    reduce_scatter x1, waiting for transfers between devices, local(): lax.psum_scatter(jnp.concatenate([both, gain_rows], axis=1), 'dp', scatte...  33.6 us
    ppermute x29, starting transfers between devices, sibling(): return lax.ppermute(x, 'fsdp', [(f, f ^ 1) for f in range(self.nf)])  20.4 us
    pallas_call x2, Pallas kernels, place_units(): pl.pallas_call(body, name='place_units', out_shape=jax.ShapeDtypeStruct((...  18 us
  transfers between devices with their start and end apart: 81, of which 36 were waited for; matrix products, arithmetic and copies ran while one was open for 26% of the time, Pallas kernels for 29%

commit v1 on v0

v1 whole, which is shorter than its diff:
```python
from functools import partial

import jax
import jax.numpy as jnp
from jax import lax
from jax.experimental import pallas as pl
from jax.experimental.pallas import tpu as pltpu
from jax.sharding import PartitionSpec as P

D = 768
HEADS = 12
HEAD = 64
WIN = 12
WCOLS = 8
Q_DEV = 16
MICRO = 2
PATCH = WIN * WIN
PAIRS = HEADS // 2
GROUPS = 4
GHEADS = HEADS // GROUPS
GCOLS = GHEADS * HEAD
SCALE = HEAD ** (-0.5)

bf = jnp.bfloat16
f32 = jnp.float32


def dot(a, b):
    return lax.dot_general(a, b, (((1,), (0,)), ((), ())), preferred_element_type=f32)


def dot_t(a, b):
    return lax.dot_general(a, b, (((1,), (1,)), ((), ())), preferred_element_type=f32)


def t_dot(a, b):
    return lax.dot_general(a, b, (((0,), (0,)), ((), ())), preferred_element_type=f32)


def normalise(x):
    centred = x - jnp.mean(x, axis=-1, keepdims=True)
    inv = lax.rsqrt(jnp.mean(centred * centred, axis=-1, keepdims=True) + 1e-05)
    return centred * inv, inv


def norm_back(grad, hat, inv, gain):
    scaled = grad * gain
    mean_one = jnp.mean(scaled, axis=-1, keepdims=True)
    mean_two = jnp.mean(scaled * hat, axis=-1, keepdims=True)
    return inv * (scaled - mean_one - hat * mean_two), jnp.sum(grad * hat, axis=0, keepdims=True)


def gelu_both(u):
    k = 0.7978845608028654
    t = jnp.tanh(k * (u + 0.044715 * u * u * u))
    slope = 0.5 * (1.0 + t) + 0.5 * u * (1.0 - t * t) * k * (1.0 + 3 * 0.044715 * u * u)
    return 0.5 * u * (1.0 + t), slope


def low_lanes(rows):
    return lax.broadcasted_iota(jnp.int32, (rows, 2 * HEAD), 1) < HEAD


def twofold(pair, mask):
    zero = jnp.zeros_like(pair)
    return jnp.concatenate([jnp.where(mask, pair, zero), jnp.where(mask, zero, pair)], axis=0)


def onefold(stacked, mask):
    rows = stacked.shape[0] // 2
    return jnp.where(mask, stacked[:rows], stacked[rows:])


def pair_forward(q2, k2, v2, bias):
    mask = low_lanes(q2.shape[0])
    s = dot_t(twofold(q2, mask), k2) * SCALE
    if bias is not None:
        s = s + bias
    m = jnp.max(s, axis=-1, keepdims=True)
    e = jnp.exp(s - m)
    l = jnp.sum(e, axis=-1, keepdims=True)
    out = dot(e.astype(bf), v2) / l
    return onefold(out, mask), m, l


def pair_backward(q2, k2, v2, d2, a2, bias, lse=None):
    mask = low_lanes(q2.shape[0])
    qs = twofold(q2, mask)
    ds = twofold(d2, mask)
    s = dot_t(qs, k2) * SCALE
    if bias is not None:
        s = s + bias
    if lse is None:
        e = jnp.exp(s - jnp.max(s, axis=-1, keepdims=True))
        p = e * (1.0 / jnp.sum(e, axis=-1, keepdims=True))
    else:
        p = jnp.exp(s - lse)
    corr = jnp.sum(ds.astype(f32) * twofold(a2, mask).astype(f32), axis=-1, keepdims=True)
    dp = dot_t(ds, v2)
    dsc = (p * (dp - corr)).astype(bf)
    dq = onefold(dot(dsc, k2), mask) * SCALE
    dk = t_dot(dsc, qs) * SCALE
    dv = t_dot(p.astype(bf), ds)
    return dq, dk, dv


def call(body, name, out_shape, in_specs, out_specs, grid, args, scratch=(), flops=0):
    return pl.pallas_call(
        body,
        name=name,
        out_shape=out_shape,
        grid=grid,
        in_specs=in_specs,
        out_specs=out_specs,
        scratch_shapes=scratch,
        compiler_params=pltpu.CompilerParams(vmem_limit_bytes=58 * 1024 * 1024),
        cost_estimate=pl.CostEstimate(flops=flops, bytes_accessed=1 << 20, transcendentals=0),
    )(*args)


def whole(shape):
    zeros = (0,) * len(shape)
    return pl.BlockSpec(shape, lambda *_: zeros, pipeline_mode=pl.Buffered(1))


def per_page(shape, axis):
    def place(p):
        return tuple(p if k == axis else 0 for k in range(len(shape)))

    return pl.BlockSpec(shape, place)


def sds(shape, dtype):
    return jax.ShapeDtypeStruct(shape, dtype)


def window_fwd(x_ref, bias_ref, gw_ref, w_ref, mix_ref, att_ref, v1_ref):
    rows = x_ref.shape[0]
    x = x_ref[...].astype(f32)
    xn = (normalise(x)[0] * gw_ref[...]).astype(bf)
    for u in range(3):
        mix_ref[u] = dot(xn, w_ref[u]).astype(bf)

    def window(w, carry):
        at = pl.ds(pl.multiple_of(w * PATCH, 16), PATCH)
        bias = bias_ref[w]
        bias = jnp.concatenate([bias, bias], axis=0)
        for p in range(PAIRS):
            c = slice(p * 128, p * 128 + 128)
            out = pair_forward(mix_ref[0, at, c], mix_ref[1, at, c], mix_ref[2, at, c], bias)[0]
            att_ref[at, c] = out.astype(bf)
        return carry

    lax.fori_loop(0, rows // PATCH, window, 0)
    v1_ref[...] = x_ref[...].astype(f32) + dot(att_ref[...], w_ref[3])


def normed_units(x_ref, g_ref, w_ref, out_ref):
    xn = (normalise(x_ref[...])[0] * g_ref[...]).astype(bf)
    for u in range(3):
        out_ref[u] = dot(xn, w_ref[u]).astype(bf)


def read_fwd(rq_ref, k_ref, v_ref, o_ref, lse_ref):
    slots = rq_ref.shape[1]
    lane = lax.broadcasted_iota(jnp.int32, (slots, 128), 1)
    acc = jnp.zeros((slots, 128), f32)
    for p in range(PAIRS):
        c = slice(p * 128, p * 128 + 128)
        out, m, l = pair_forward(rq_ref[0, :, c], k_ref[0, :, c], v_ref[0, :, c], None)
        o_ref[0, :, c] = out
        lse = m + jnp.log(l)
        acc = jnp.where(lane == 2 * p, lse[:slots], acc)
        acc = jnp.where(lane == 2 * p + 1, lse[slots:], acc)
    lse_ref[0] = acc


def write_fwd(v1_ref, wq_ref, wk_ref, wv_ref, bias_ref, wo_ref, wr_ref, v2_ref):
    for p in range(PAIRS):
        c = slice(p * 128, p * 128 + 128)
        out = pair_forward(wq_ref[0, :, c], wk_ref[0, :, c], wv_ref[0, :, c], bias_ref[0])[0]
        wr_ref[:, c] = out.astype(bf)
    v2_ref[...] = v1_ref[...] + dot(wr_ref[...], wo_ref[0])


def mlp_both(steps, last, rows_of_core, core_ref, x_ref, g_ref, up_ref, down_ref, cot_ref, *refs):
    if last:
        y_in_ref, dxn_in_ref, out_ref, dx_ref, dg_ref = refs[:5]
        refs = refs[5:]
        xn_ref, y_ref, dxn_ref = refs[-3:]
        outs = refs[:-3]
    else:
        y_ref, dxn_ref = refs[:2]
        xn_ref = refs[-1]
        outs = refs[2:-1]
    half = len(outs) // 2
    j = pl.program_id(0)

    @pl.when(j == 0)
    def _():
        xn_ref[...] = (normalise(x_ref[...])[0] * g_ref[...]).astype(bf)

    xn = xn_ref[...]
    cot = cot_ref[...]
    up = up_ref[0]
    down = down_ref[...]
    act, slope = gelu_both(dot(xn, up))
    act = act.astype(bf)
    y = dot(act, down)
    dpre = (dot_t(cot, down) * slope).astype(bf)
    dxn = dot_t(dpre, up)
    emit_unit(core_ref, t_dot(xn, dpre), outs[:half], 0)
    d_down = t_dot(act, cot)
    if half == 1:
        outs[1][...] = d_down.astype(bf)
    else:
        span = 2 * rows_of_core
        for i in range(d_down.shape[0] // span):
            emit(core_ref, d_down[i * span : (i + 1) * span], outs[2], outs[3], i)

    @pl.when(j == 0)
    def _():
        y_ref[...] = y_in_ref[...] + y if last else y
        dxn_ref[...] = dxn_in_ref[...] + dxn if last else dxn

    @pl.when(j > 0)
    def _():
        y_ref[...] += y
        dxn_ref[...] += dxn

    if last:

        @pl.when(j == steps - 1)
        def _():
            x = x_ref[...]
            out_ref[...] = (x + y_ref[...]).astype(bf)
            hat, inv = normalise(x)
            dx, dg = norm_back(dxn_ref[...], hat, inv, g_ref[...])
            dx_ref[...] = cot_ref[...].astype(f32) + dx
            dg_ref[...] = dg


def write_bwd(core_ref, dv2_ref, wr_ref, wq_ref, wk_ref, wv_ref, bias_ref, wo_ref, dwq_ref, dwk_ref, dwv_ref, *refs):
    outs, acc_ref = refs[:-1], refs[-1]
    page = pl.program_id(0)
    d = dv2_ref[...].astype(bf)
    dwr = dot_t(d, wo_ref[0]).astype(bf)
    part = t_dot(wr_ref[...], d)

    @pl.when(page == 0)
    def _():
        acc_ref[...] = part

    @pl.when(page > 0)
    def _():
        acc_ref[...] += part

    @pl.when(page == pl.num_programs(0) - 1)
    def _():
        emit_unit(core_ref, acc_ref[...], outs, 0)

    for p in range(PAIRS):
        c = slice(p * 128, p * 128 + 128)
        dq, dk, dv = pair_backward(
            wq_ref[0, :, c], wk_ref[0, :, c], wv_ref[0, :, c], dwr[:, c], wr_ref[:, c], bias_ref[0]
        )
        dwq_ref[:, c] = dq.astype(bf)
        dwk_ref[0, :, c] = dk.astype(bf)
        dwv_ref[0, :, c] = dv.astype(bf)


def read_bwd(rq_ref, k_ref, v_ref, d_ref, r_ref, lse_ref, dq_ref, dk_ref, dv_ref):
    slots = rq_ref.shape[1]
    lse = lse_ref[0]
    for p in range(PAIRS):
        c = slice(p * 128, p * 128 + 128)
        both = jnp.concatenate([lse[:, 2 * p : 2 * p + 1], lse[:, 2 * p + 1 : 2 * p + 2]], axis=0)
        dq, dk, dv = pair_backward(
            rq_ref[0, :, c], k_ref[0, :, c], v_ref[0, :, c], d_ref[0, :, c], r_ref[0, :, c], None, both
        )
        dq_ref[0, :, c] = dq.astype(bf)
        dk_ref[:, c] = dk.astype(bf)
        dv_ref[:, c] = dv.astype(bf)


def emit(core_ref, rows, keep_ref, give_ref, at):
    half = rows.shape[0] // 2
    first, second = rows[:half], rows[half:]
    here = core_ref[0] == 0
    keep_ref[at] = jnp.where(here, first, second).astype(bf)
    give_ref[at] = jnp.where(here, second, first).astype(bf)


def emit_unit(core_ref, unit, outs, u):
    if len(outs) == 1:
        outs[0][u] = unit.astype(bf)
        return
    chips = outs[0].shape[0]
    span = unit.shape[0] // chips
    for i in range(chips):
        emit(core_ref, unit[i * span : (i + 1) * span], outs[0], outs[1], (i, u))


def page_bwd(core_ref, v1_ref, dv2_ref, dk_ref, dv_ref, dwq_ref, gp_ref, wp_ref, dv1_ref, dg_ref, *refs):
    outs, acc_ref, gacc_ref = refs[:-2], refs[-2], refs[-1]
    page = pl.program_id(0)
    hat, inv = normalise(v1_ref[...])
    pn = (hat * gp_ref[...]).astype(bf)
    grads = (dk_ref, dv_ref, dwq_ref)
    dpn = dot_t(dk_ref[...], wp_ref[0]) + dot_t(dv_ref[...], wp_ref[1]) + dot_t(dwq_ref[...], wp_ref[2])
    dx, dg = norm_back(dpn, hat, inv, gp_ref[...])
    dv1_ref[...] = dv2_ref[...] + dx

    @pl.when(page == 0)
    def _():
        gacc_ref[...] = dg
        for u in range(3):
            acc_ref[u] = t_dot(pn, grads[u][...])

    @pl.when(page > 0)
    def _():
        gacc_ref[...] += dg
        for u in range(3):
            acc_ref[u] += t_dot(pn, grads[u][...])

    @pl.when(page == pl.num_programs(0) - 1)
    def _():
        dg_ref[...] = gacc_ref[...]
        for u in range(3):
            emit_unit(core_ref, acc_ref[u], outs, u)


def window_bwd(dv1_ref, mix_ref, att_ref, bias_ref, w_ref, *refs):
    dmix_ref, datt_ref = refs[-2:]
    rows = att_ref.shape[0]
    datt_ref[...] = dot_t(dv1_ref[...].astype(bf), w_ref[3]).astype(bf)

    def window(w, carry):
        at = pl.ds(pl.multiple_of(w * PATCH, 16), PATCH)
        bias = bias_ref[w]
        bias = jnp.concatenate([bias, bias], axis=0)
        for p in range(PAIRS):
            c = slice(p * 128, p * 128 + 128)
            dq, dk, dv = pair_backward(
                mix_ref[0, at, c], mix_ref[1, at, c], mix_ref[2, at, c], datt_ref[at, c], att_ref[at, c], bias
            )
            dmix_ref[0, at, c] = dq.astype(bf)
            dmix_ref[1, at, c] = dk.astype(bf)
            dmix_ref[2, at, c] = dv.astype(bf)
        return carry

    lax.fori_loop(0, rows // PATCH, window, 0)


def window_grads(core_ref, dv1_ref, x_ref, dmix_ref, att_ref, gw_ref, *refs):
    outs, acc_ref = refs[:-1], refs[-1]
    page = pl.program_id(0)
    xn = (normalise(x_ref[...].astype(f32))[0] * gw_ref[...]).astype(bf)
    d1b = dv1_ref[...].astype(bf)

    @pl.when(page == 0)
    def _():
        for u in range(3):
            acc_ref[u] = t_dot(xn, dmix_ref[u])
        acc_ref[3] = t_dot(att_ref[...], d1b)

    @pl.when(page > 0)
    def _():
        for u in range(3):
            acc_ref[u] += t_dot(xn, dmix_ref[u])
        acc_ref[3] += t_dot(att_ref[...], d1b)

    @pl.when(page == pl.num_programs(0) - 1)
    def _():
        for u in range(4):
            emit_unit(core_ref, acc_ref[u], outs, u)


def window_end(dv1_ref, x_ref, dmix_ref, gw_ref, w_ref, grad_ref, dg_ref, gacc_ref):
    page = pl.program_id(0)
    hat, inv = normalise(x_ref[...].astype(f32))
    dxn = dot_t(dmix_ref[0], w_ref[0]) + dot_t(dmix_ref[1], w_ref[1]) + dot_t(dmix_ref[2], w_ref[2])
    dx, dg = norm_back(dxn.astype(bf).astype(f32), hat, inv, gw_ref[...])
    grad_ref[...] = (dv1_ref[...] + dx).astype(bf)

    @pl.when(page == 0)
    def _():
        gacc_ref[...] = dg

    @pl.when(page > 0)
    def _():
        gacc_ref[...] += dg

    dg_ref[...] = gacc_ref[...]


def slots_fwd(x_ref, g_ref, w_ref, bias_ref, mix_ref, att_ref, s1_ref):
    x = x_ref[...].astype(f32)
    xn = (normalise(x)[0] * g_ref[...]).astype(bf)
    for u in range(3):
        mix_ref[u] = dot(xn, w_ref[u]).astype(bf)
    for p in range(PAIRS):
        c = slice(p * 128, p * 128 + 128)
        out = pair_forward(mix_ref[0, :, c], mix_ref[1, :, c], mix_ref[2, :, c], bias_ref[...])[0]
        att_ref[:, c] = out.astype(bf)
    s1_ref[...] = x + dot(att_ref[...], w_ref[3])


def own_columns(x, chip, span, step):
    total = x.shape[1]
    count = total // step * span
    row = lax.broadcasted_iota(jnp.int32, (total, count), 0)
    col = lax.broadcasted_iota(jnp.int32, (total, count), 1)
    at = lax.div(col, span) * step + chip * span + lax.rem(col, span)
    return dot(x, jnp.where(row == at, 1.0, 0.0).astype(bf)).astype(bf)


def query_mlp(
    span,
    step,
    chip_ref,
    s1_ref,
    read_ref,
    wo_ref,
    g_ref,
    up_ref,
    down_ref,
    cot_ref,
    out_ref,
    ds2_ref,
    dread_ref,
    dw_ref,
    ddown_ref,
    dg_ref,
):
    chip = chip_ref[0]
    reading = read_ref[...]
    s2 = s1_ref[...] + dot(reading, wo_ref[0])
    hat, inv = normalise(s2)
    xn = (hat * g_ref[...]).astype(bf)
    x_own = own_columns(xn, chip, span, step)
    cot = cot_ref[...]
    y, dxn = s2, None
    for k in range(4):
        up, down = up_ref[k], down_ref[k * D : (k + 1) * D]
        act, slope = gelu_both(dot(xn, up))
        act = act.astype(bf)
        y = y + dot(act, down)
        dpre = (dot_t(cot, down) * slope).astype(bf)
        part = dot_t(dpre, up)
        dxn = part if dxn is None else dxn + part
        dw_ref[k] = t_dot(x_own, dpre).astype(bf)
        act_own = own_columns(act, chip, 4 * span, 4 * step)
        rows = act_own.shape[1]
        ddown_ref[k * rows : (k + 1) * rows] = t_dot(act_own, cot).astype(bf)
    out_ref[...] = y.astype(bf)
    dx, dg = norm_back(dxn, hat, inv, g_ref[...])
    ds2 = cot.astype(f32) + dx
    ds2_ref[...] = ds2
    dg_ref[...] = dg
    d2b = ds2.astype(bf)
    dread_ref[...] = dot_t(d2b, wo_ref[0]).astype(bf)
    dw_ref[4] = t_dot(own_columns(reading, chip, span, step), d2b).astype(bf)


def query_back(
    span,
    step,
    chip_ref,
    x_ref,
    s1_ref,
    ds2_ref,
    d_ref,
    gr_ref,
    wr_ref,
    ws_ref,
    mix_ref,
    att_ref,
    bias_ref,
    gs_ref,
    out_ref,
    dw_ref,
    dgs_ref,
    dgr_ref,
    dmix_ref,
):
    chip = chip_ref[0]
    hat, inv = normalise(s1_ref[...])
    rn_own = own_columns((hat * gr_ref[...]).astype(bf), chip, span, step)
    drn = dot_t(d_ref[0], wr_ref[0]) + dot_t(d_ref[1], wr_ref[1]) + dot_t(d_ref[2], wr_ref[2])
    dx, dg = norm_back(drn, hat, inv, gr_ref[...])
    dgr_ref[...] = dg
    for u in range(3):
        dw_ref[4 + u] = t_dot(rn_own, d_ref[u]).astype(bf)
    ds1 = ds2_ref[...] + dx
    d1b = ds1.astype(bf)
    datt = dot_t(d1b, ws_ref[3]).astype(bf)
    dw_ref[3] = t_dot(own_columns(att_ref[...], chip, span, step), d1b).astype(bf)
    for p in range(PAIRS):
        c = slice(p * 128, p * 128 + 128)
        grads = pair_backward(
            mix_ref[0, :, c], mix_ref[1, :, c], mix_ref[2, :, c], datt[:, c], att_ref[:, c], bias_ref[...]
        )
        for u in range(3):
            dmix_ref[u, :, c] = grads[u].astype(bf)
    hat, inv = normalise(x_ref[...].astype(f32))
    xn_own = own_columns((hat * gs_ref[...]).astype(bf), chip, span, step)
    dxn = dot_t(dmix_ref[0], ws_ref[0]) + dot_t(dmix_ref[1], ws_ref[1]) + dot_t(dmix_ref[2], ws_ref[2])
    dx, dg = norm_back(dxn, hat, inv, gs_ref[...])
    dgs_ref[...] = dg
    out_ref[...] = (ds1 + dx).astype(bf)
    for u in range(3):
        dw_ref[u] = t_dot(xn_own, dmix_ref[u]).astype(bf)


def simple(body, name, args, outs, scratch=()):
    arrays = [a[0] if isinstance(a, tuple) else a for a in args]
    specs = [
        a[1]
        if isinstance(a, tuple)
        else pl.BlockSpec(memory_space=pltpu.SMEM)
        if a.ndim == 1
        else whole(a.shape)
        for a in args
    ]
    return call(
        body,
        name,
        tuple(sds(*o) for o in outs),
        specs,
        tuple(whole(o[0]) for o in outs),
        (1,),
        arrays,
        scratch=scratch,
        flops=1 << 30,
    )


def pack_rows(place, arrays, gains):
    window, out, slots, rows_of_slots, reader, rows_of_reader, writer, rows_of_writer, up, down, qup, qdown = arrays
    r = window.shape[0]

    def units(w):
        return [w[:, k * D : (k + 1) * D] for k in range(w.shape[1] // D)]

    def groups(win, o, sl, so, rd, ro, wr, wo, u, d, qu, qd, g):
        rd, wr = units(rd), units(wr)
        return (
            units(win) + [o] + units(sl) + [so, g],
            rd[1:] + wr[:1] + rd[:1] + wr[1:] + [wo],
            units(u) + [d[k] for k in range(4)],
            units(qu) + [ro] + [qd[k] for k in range(4)],
        )

    down, qdown = down.reshape(4, r, D), qdown.reshape(4, r, D)
    arrays = (window, out, slots, rows_of_slots, reader, rows_of_reader, writer, rows_of_writer, up, down, qup, qdown)
    if r % 8:
        return [jnp.stack(group) for group in groups(*arrays, gains)]

    def body(*refs):
        for group, out_ref in zip(groups(*refs[:13]), refs[13:]):
            for k, w in enumerate(group):
                out_ref[k] = w[...]

    return simple(body, "pack_rows", arrays + (gains,), [((n, r, D), bf) for n in (9, 7, 8, 9)])


def place_units(place, pieces, plain, tall):
    nz, n, r = pieces[0][0].shape[:3]
    left = n - plain - 4 * tall
    table = jnp.stack([place.core, place.chip % 4, place.z]).astype(jnp.int32)

    def body(table_ref, *args):
        refs, outs, (s_ref, sem) = args[:8], args[8:-2], args[-2:]
        core, chip, z = table_ref[0], table_ref[1], table_ref[2]
        now = pl.program_id(0)

        def targets():
            for c in range(2):
                owner = jnp.bitwise_xor(core, c)
                for i in range(4):
                    mask = jnp.where(owner == 0, i, (0, 2, 1, 3)[i])
                    yield 4 * c + i, s_ref.at[owner, jnp.bitwise_xor(chip, mask)]

        @pl.when(now == 0)
        def _():
            for k, there in targets():
                for m in range(nz):
                    at = jnp.bitwise_xor(z, m)
                    pltpu.make_async_copy(refs[k].at[m], there.at[at], sem.at[k, at]).start()

        for k, there in targets():
            pltpu.make_async_copy(refs[k].at[0], there.at[now], sem.at[k, now]).wait()
        for q in range(4):
            for u in range(plain):
                rows = [s_ref[c, q, now, u].astype(f32) for c in range(2)]
                outs[0][u, q] = jnp.concatenate(rows, axis=0).astype(bf)
            if tall:
                rows = [s_ref[c, q, now, plain + k].astype(f32) for c in range(2) for k in range(4)]
                outs[1][q] = jnp.concatenate(rows, axis=0).astype(bf)
            if left:
                rows = [s_ref[c, q, now, plain].astype(f32)[:1] for c in range(2)]
                outs[-1][q] = jnp.concatenate(rows + [jnp.zeros((6, D), f32)], axis=0)

    shapes = [jax.ShapeDtypeStruct((plain, 4 * nz, 2 * r, D), bf)]
    blocks = [pl.BlockSpec((plain, 4, 2 * r, D), lambda i: (0, i, 0, 0))]
    if tall:
        shapes.append(jax.ShapeDtypeStruct((4 * nz, 8 * r, D), bf))
        blocks.append(pl.BlockSpec((4, 8 * r, D), lambda i: (i, 0, 0)))
    if left:
        shapes.append(jax.ShapeDtypeStruct((4 * nz, 8, D), f32))
        blocks.append(pl.BlockSpec((4, 8, D), lambda i: (i, 0, 0)))
    out = pl.pallas_call(
        body,
        name="place_units",
        grid=(nz,),
        out_shape=tuple(shapes),
        in_specs=[pl.BlockSpec(memory_space=pltpu.SMEM)] + [pl.BlockSpec(memory_space=pl.ANY)] * 8,
        out_specs=tuple(blocks),
        scratch_shapes=[pltpu.VMEM((2, 4, nz, n, r, D), bf), pltpu.SemaphoreType.DMA((8, nz))],
        compiler_params=pltpu.CompilerParams(vmem_limit_bytes=60 * 1024 * 1024),
        cost_estimate=pl.CostEstimate(flops=0, bytes_accessed=n * D * D * 4, transcendentals=0),
    )(table, *pieces[0], *pieces[1])
    out = list(out)
    out[0] = out[0].reshape(plain, D, D)
    if tall:
        out[1] = out[1].reshape(4 * D, D)
    return out


def pick(stack, index, axis=0):
    return lax.dynamic_index_in_dim(stack, index, axis, keepdims=False)


def ordered(first, mine, other):
    return jnp.stack([jnp.where(first, mine, other), jnp.where(first, other, mine)])


class Place:
    def __init__(self):
        self.nz = lax.axis_size("dp")
        self.nf = lax.axis_size("fsdp")
        self.nq = self.nf // 2
        self.z = lax.axis_index("dp")
        self.f = lax.axis_index("fsdp")
        self.core = self.f % 2
        self.even = self.core == 0
        self.chip = self.f // 2
        self.group = self.chip % GROUPS

    def sibling(self, x):
        return lax.ppermute(x, "fsdp", [(f, f ^ 1) for f in range(self.nf)])

    def hop(self, x, mask, odd_mask=None):
        odd_mask = mask if odd_mask is None else odd_mask
        route = [(f, f ^ ((odd_mask if f % 2 else mask) << 1)) for f in range(self.nf)]
        return lax.ppermute(x, "fsdp", route)

    def across(self, x, mask):
        return lax.ppermute(x, "dp", [(z, z ^ mask) for z in range(self.nz)])

    def send_line(self, x):
        return [self.across(x, m) for m in range(1, self.nz)]

    def send_terms(self, now):
        return [self.across(pick(now, self.z ^ m), m) for m in range(1, self.nz)]

    def gather_square(self, block, bit):
        a, b = 1 << bit, 2 << bit
        first = self.hop(block, a, b)
        second = self.hop(block, b, a)
        return [block, first, second, self.hop(first, b, a)]

    def first_hop(self, x):
        return self.hop(x, 1, 2)

    def second_hop(self, x):
        return self.hop(x, 2, 1)

    def arranged(self, pieces, bit, odd):
        here = (self.chip >> bit) % 4
        stack = jnp.stack(pieces)
        at = [0, 1, 2, 3]
        swapped = jnp.where(odd, jnp.array([0, 2, 1, 3]), jnp.array(at))
        return jnp.stack([pick(stack, swapped[here ^ k]) for k in at])

    def gather_plain(self, block):
        stack = jnp.stack([block] + self.send_line(block))
        now = jnp.stack([pick(stack, self.z ^ k) for k in range(self.nz)])
        levels = 0
        for bit in range(0, self.nq.bit_length() - 1, 2):
            now = self.arranged(self.gather_square(now, bit), bit, ~self.even)
            levels += 1
        now = ordered(self.even, now, self.sibling(now))
        n, r = block.shape[:2]
        now = now.reshape(2, self.nq, self.nz, n, r, D)
        return jnp.transpose(now, (3, 2, 1, 0, 4, 5))

    def chip_terms(self, pairs):
        def parts(i):
            blocks = []
            for keep, other in pairs:
                shape = (self.nz, 4) + (() if self.nq == 4 else (self.nq // 4,)) + keep.shape[2:]
                blocks.append(pick(keep.reshape(shape), i, 1).astype(f32) + pick(other.reshape(shape), i, 1).astype(f32))
            return jnp.concatenate(blocks, axis=-3)

        return parts

    def halves(self, x, r):
        x = x.reshape((-1, self.nz, self.nq, 2, r, x.shape[-1]))

        def rows(which):
            return jnp.moveaxis(pick(x, which, 3), 0, 2)

        return rows(self.core), rows(1 - self.core)

    def square_terms(self, parts):
        bit = (self.nq.bit_length() - 1) - 2
        here = (self.chip >> bit) % 4
        first = jnp.where(self.even, 1, 2)
        return [parts(here ^ mask) for mask in (3 - first, jnp.full_like(first, 3), first, jnp.zeros_like(first))]

    def outer_hop(self, which, x):
        bit = (self.nq.bit_length() - 1) - 2
        a, b = 1 << bit, 2 << bit
        return self.hop(x, a, b) if which == 0 else self.hop(x, b, a)

    def inner_square(self, now):
        if now.ndim > 4:
            first = jnp.where(self.even, 1, 2)
            here = self.chip % 4

            def at(mask):
                return pick(now, here ^ mask, 1).astype(f32)

            second = self.hop(at(3 - first).astype(bf), 2, 1)
            corner = self.hop(at(3).astype(bf), 2, 1)
            moved = self.hop((at(first) + corner.astype(f32)).astype(bf), 1, 2)
            now = (at(0) + moved.astype(f32) + second.astype(f32)).astype(bf)
        return now

    def own_terms(self, now):
        return pick(now, self.z).astype(f32)

    def group_hops(self, x):
        return [self.hop(x, mask) for mask in range(1, GROUPS)]

    def in_order(self, pieces):
        stack = jnp.stack(pieces)
        return jnp.stack([pick(stack, self.group ^ k) for k in range(GROUPS)])

    def to_groups(self, blocks):
        return [self.hop(pick(blocks, self.group ^ mask), mask) for mask in range(1, GROUPS)]

    def owned_rows(self, mine, axis=0):
        own = lax.dynamic_slice_in_dim(mine, self.f * Q_DEV, Q_DEV, axis)
        give = lax.dynamic_slice_in_dim(mine, (self.f ^ 1) * Q_DEV, Q_DEV, axis)
        return ordered(self.even, own, self.sibling(give))


def tie(*arrays):
    return lax.optimization_barrier(arrays)


def stage(*moves):
    operands = tie(*[operand for _, operand in moves])
    return tie(*[move(operand) for (move, _), operand in zip(moves, operands)])


def split_three(x):
    hi = lax.reduce_precision(x, 8, 7)
    mid = lax.reduce_precision(x - hi, 8, 7)
    return [hi.astype(bf), mid.astype(bf), (x - hi - mid).astype(bf)]


def join_three(x):
    a, b, c = jnp.split(x.astype(f32), 3, axis=-1)
    return (a + b) + c


def columns(weight):
    rows, width = weight.shape
    return [weight[:, k * D : (k + 1) * D] for k in range(width // D)]


def strip_bias(place, bands, height):
    half = WIN // 2
    rows = (place.f % bands) * height + jnp.arange(height, dtype=jnp.int32)
    cols = (place.f // bands) * WIN + jnp.arange(WIN, dtype=jnp.int32)

    def label(at, total):
        return (at >= total - WIN).astype(jnp.int32) + (at >= total - half).astype(jnp.int32)

    labels = label(rows, height * bands)[:, None] * 3 + label(cols, WIN * WCOLS)
    labels = labels.reshape(height // WIN, PATCH)
    return jnp.where(labels[:, :, None] == labels[:, None, :], 0.0, -1e30).astype(f32)


def roll_beside(x, place, bands):
    route = [((f + bands) % place.nf, f) for f in range(place.nf)]
    return lax.ppermute(x, "fsdp", route)


def roll_in(x, beside, place, bands):
    half = WIN // 2
    pages, height = x.shape[:2]
    if bands > 1:
        x = jnp.concatenate([x[:, :, half:], beside], axis=2)
        route = [(f // bands * bands + (f + 1) % bands, f) for f in range(place.nf)]
        below = lax.ppermute(x[:, :half], "fsdp", route)
        return jnp.concatenate([x[:, half:], below], axis=1).reshape(-1, D)

    def body(x_ref, b_ref, out_ref, tall_ref):
        for to in range(height):
            row = (to + half) % height
            tall_ref[to * WIN : to * WIN + half] = x_ref[0, row].astype(f32)[half:]
            tall_ref[to * WIN + half : (to + 1) * WIN] = b_ref[0, row].astype(f32)
        out_ref[...] = tall_ref[...].astype(bf)

    return call(
        body,
        "roll_in",
        sds((pages * height * WIN, D), bf),
        [per_page((1, height, WIN, D), 0), per_page((1, height, half, D), 0)],
        per_page((height * WIN, D), 0),
        (pages,),
        (x, beside),
        scratch=(pltpu.VMEM((height * WIN, D), f32),),
        flops=1 << 20,
    )


def roll_out(x, place, bands):
    half = WIN // 2
    beside = lax.ppermute(x[:, :, half:], "fsdp", [(f, (f + bands) % place.nf) for f in range(place.nf)])
    x = jnp.concatenate([beside, x[:, :, :half]], axis=2)
    above = x[:, -half:]
    if bands > 1:
        route = [(f, f // bands * bands + (f + 1) % bands) for f in range(place.nf)]
        above = lax.ppermute(above, "fsdp", route)
    return jnp.concatenate([above, x[:, :-half]], axis=1)


def local(
    visual,
    query_slots,
    lengths,
    slot_order,
    norm_window,
    window_qkv,
    window_out,
    norm_slots,
    slots_qkv,
    slots_out,
    norm_reader,
    norm_page,
    reader_qkv,
    reader_out,
    writer_qkv,
    writer_out,
    norm_visual_mlp,
    visual_up,
    visual_down,
    norm_query_mlp,
    query_up,
    query_down,
    visual_cot,
    query_cot,
):
    place = Place()
    nz, nf, nq, core, even = place.nz, place.nf, place.nq, place.core, place.even
    extra = nq // GROUPS
    bands = nf // WCOLS
    height = visual.shape[1]
    page_rows = height * WIN
    rows = MICRO * page_rows
    slots = Q_DEV * nf
    r = window_out.shape[0]

    fast = r % 8 == 0 and nq == 4
    gains = jnp.stack([norm_window, norm_slots, norm_reader, norm_page, norm_visual_mlp, norm_query_mlp])
    gains = jnp.zeros((r, D), bf).at[0, : 6 * r].set(gains.reshape(6 * r))
    arrays = (
        window_qkv,
        window_out,
        slots_qkv,
        slots_out,
        reader_qkv,
        reader_out,
        writer_qkv,
        writer_out,
        visual_up,
        visual_down,
        query_up,
        query_down,
    )
    one, two, three, four = pack_rows(place, arrays, gains)

    def squares(x):
        return [place.first_hop(x), place.second_hop(x)]

    def siblings(x):
        return jax.tree.map(place.sibling, x)

    def assemble(block, pieces, others, plain, tall):
        if fast:
            return place_units(place, [pieces, others], plain, tall)
        units = place.gather_plain(block)
        out = [units[:plain].reshape(plain, D, D)]
        if tall:
            out.append(jnp.transpose(units[plain:], (1, 2, 3, 0, 4, 5)).reshape(4 * D, D))
        elif block.shape[0] > plain:
            rows_left = units[plain, ..., 0, :].reshape(nz * nq, 2, D).astype(f32)
            out.append(jnp.pad(rows_left, ((0, 0), (0, 6), (0, 0))))
        return out

    ends = jnp.stack([query_slots, query_cot])
    positions = (slot_order[:, :, None] * Q_DEV + jnp.arange(Q_DEV, dtype=jnp.int32)).reshape(MICRO, slots)
    live = jnp.where(positions < lengths[:, None], 0.0, -1e30).astype(f32).reshape(MICRO, 1, slots)
    own_live = pick(live, core)
    bias = strip_bias(place, bands, height)
    chip_id = place.chip.astype(jnp.int32).reshape(1)
    core_id = core.astype(jnp.int32).reshape(1)

    def spread(x, bit):
        return place.hop(x, 1 << bit)

    def spread_order(x, got, bit):
        upper = (place.chip >> bit) % 2 == 1
        return jnp.concatenate([jnp.where(upper, got, x), jnp.where(upper, x, got)], axis=1)

    def all_dp(block, got):
        return jnp.stack([block] + list(got))

    got, ends_two, beside_x = stage(
        (place.send_line, one),
        (place.sibling, pick(ends, 1 - core, 1)),
        (partial(roll_beside, place=place, bands=bands), visual[:, :, : WIN // 2]),
    )
    all_one = all_dp(one, got)
    ends = jnp.swapaxes(ordered(even, pick(ends, core, 1), ends_two), 0, 1).reshape(2, 2 * Q_DEV, D)
    got, (f_one, s_one) = stage((place.send_line, two), (squares, all_one))
    all_two = all_dp(two, got)
    x = roll_in(visual, beside_x, place, bands)
    c_one, sib_one, sib_f_one, sib_s_one, ends_two = stage(
        (place.second_hop, f_one),
        (place.sibling, all_one),
        (place.sibling, f_one),
        (place.sibling, s_one),
        (partial(spread, bit=0), ends),
    )
    ends = spread_order(ends, ends_two, 0)
    got, (f_two, s_two) = stage((place.send_line, three), (squares, all_two))
    all_three = all_dp(three, got)
    c_two, ends_two, sib_c_one, sib_two, beside_cot = stage(
        (place.second_hop, f_two),
        (partial(spread, bit=1), ends),
        (place.sibling, c_one),
        (place.sibling, all_two),
        (partial(roll_beside, place=place, bands=bands), visual_cot[:, :, : WIN // 2]),
    )
    ends = spread_order(ends, ends_two, 1)
    for bit in range(2, nq.bit_length() - 1):
        ends = spread_order(ends, spread(ends, bit), bit)
    xs, xs_cot = ends[0], ends[1]

    act_block = per_page((page_rows, D), 0)
    three_block = per_page((3, page_rows, D), 1)

    def part_of(size, index, full):
        return full, pl.BlockSpec((size, D, D), lambda *_: (index, 0, 0), pipeline_mode=pl.Buffered(1))

    def run_first(args):
        sib_c, x, xs = args
        w_one, gain_all = assemble(one, [all_one, f_one, s_one, c_one], [sib_one, sib_f_one, sib_s_one, sib_c], 8, 0)
        gain_all = gain_all[:, :2, : 6 * r].reshape(nz * nq * 2, 6, r)
        gain_all = jnp.transpose(gain_all, (1, 0, 2)).reshape(6, 1, D)
        windows = call(
            window_fwd,
            "window_fwd",
            (sds((3, rows, D), bf), sds((rows, D), bf), sds((rows, D), f32)),
            [act_block, whole(bias.shape), whole((1, D)), part_of(4, 0, None)[1]],
            (three_block, act_block, act_block),
            (MICRO,),
            (x, bias, gain_all[0], w_one),
            flops=2 * rows * 4 * D * D,
        )
        heard = simple(
            slots_fwd,
            "slots_fwd",
            (xs, gain_all[1], part_of(4, 1, w_one), own_live),
            [((3, slots, D), bf), ((slots, D), bf), ((slots, D), f32)],
        )
        return w_one, gain_all, windows, heard

    (f_three, s_three), sib_f_two, sib_s_two, sib_c_two, first = stage(
        (squares, all_three),
        (place.sibling, f_two),
        (place.sibling, s_two),
        (place.sibling, c_two),
        (run_first, (sib_c_one, x, xs)),
    )
    cot = roll_in(visual_cot, beside_cot, place, bands)
    w_one, gain_all, (mix, att, v1), (mix_q, att_q, s1) = first
    g_window, g_slots, g_reader, g_page, g_vmlp, g_qmlp = (gain_all[k] for k in range(6))

    def run_second(args):
        sib_c, v1, s1 = args
        (w_two,) = assemble(two, [all_two, f_two, s_two, c_two], [sib_two, sib_f_two, sib_s_two, sib_c], 7, 0)
        (rd_own,) = simple(
            normed_units, "slots_units", (s1, g_reader, part_of(3, 1, w_two)), [((3, slots, D), bf)]
        )
        pk = call(
            normed_units,
            "page_units",
            sds((3, rows, D), bf),
            [act_block, whole((1, D)), part_of(3, 0, None)[1]],
            three_block,
            (MICRO,),
            (v1, g_page, w_two),
            flops=2 * rows * 3 * D * D,
        )
        return w_two, rd_own, pk

    c_three, sib_three, sib_f_three, sib_s_three, (w_two, rd_own, pk) = stage(
        (place.second_hop, f_three),
        (place.sibling, all_three),
        (place.sibling, f_three),
        (place.sibling, s_three),
        (run_second, (sib_c_two, v1, s1)),
    )
    rd_two, sib_c_three = stage((place.sibling, rd_own), (place.sibling, c_three))
    rd = jnp.swapaxes(ordered(even, rd_own, rd_two), 0, 1)
    rq, wk, wv = rd[0], rd[1], rd[2]
    slot_block = per_page((1, slots, D), 0)
    stat_block = per_page((1, slots, 128), 0)

    def of_pk(u):
        return pl.BlockSpec((1, page_rows, D), lambda p: (u, p, 0))

    o_part, lse_part = call(
        read_fwd,
        "read_fwd",
        (sds((MICRO, slots, D), f32), sds((MICRO, slots, 128), f32)),
        [slot_block, of_pk(0), of_pk(1)],
        (slot_block, stat_block),
        (MICRO,),
        (rq, pk, pk),
        flops=2 * rows * slots * D * 4,
    )

    def merge(terms):
        width = terms[0].shape[-1] // (HEAD + 1) * HEAD
        lse = jnp.stack([t[..., width:] for t in terms])
        top = jnp.max(lse, axis=0)
        weights = jnp.exp(lse - top)
        total = jnp.sum(weights, axis=0)
        shares = weights / total
        out = sum(t[..., :width] * jnp.repeat(share, HEAD, axis=-1) for t, share in zip(terms, shares))
        return jnp.concatenate([out, top + jnp.log(total)], axis=-1)

    terms = jnp.concatenate([o_part, lse_part[..., :HEADS]], axis=-1)
    live_block = per_page((1, 1, slots), 0)

    def run_write(args):
        return call(
            write_fwd,
            "write_fwd",
            (sds((rows, D), bf), sds((rows, D), f32)),
            [act_block, of_pk(2), slot_block, slot_block, live_block, part_of(1, 6, None)[1]],
            (act_block, act_block),
            (MICRO,),
            args,
            flops=2 * rows * D * D,
        )

    terms_two, (writing, v2), (w_up, w_down) = stage(
        (place.sibling, pick(terms, 1 - core)),
        (run_write, (v1, pk, wk, wv, live, w_two)),
        (
            lambda sib_c: assemble(
                three, [all_three, f_three, s_three, c_three], [sib_three, sib_f_three, sib_s_three, sib_c], 4, 1
            ),
            sib_c_three,
        ),
    )
    terms = merge([pick(terms, core), terms_two])
    blocks = jnp.concatenate(
        [terms[:, :D].reshape(slots, GROUPS, GCOLS), terms[:, D:].reshape(slots, GROUPS, GHEADS)], axis=-1
    )
    blocks = jnp.swapaxes(blocks, 0, 1)
    chunk = 384
    steps = 2 * D // chunk
    per_unit = D // chunk

    def once(*shape):
        return pl.BlockSpec(shape, lambda j: (0,) * len(shape), pipeline_mode=pl.Buffered(1))

    smem = pl.BlockSpec(memory_space=pltpu.SMEM)
    zq = nz * nq
    if fast:
        up_shapes = [sds((zq, 2, r, D), bf)] * 2
        up_outs = [pl.BlockSpec((zq, 1, r, chunk), lambda j: (0, j // per_unit, 0, j % per_unit))] * 2
        down_shapes = [sds((zq // 2, 4 * r, D), bf)] * 2
        down_outs = [pl.BlockSpec((chunk // (8 * r), 4 * r, D), lambda j: (j, 0, 0))] * 2
    else:
        up_shapes = [sds((2, D, D), bf)]
        up_outs = [pl.BlockSpec((1, D, chunk), lambda j: (j // per_unit, 0, j % per_unit))]
        down_shapes = [sds((2 * D, D), bf)]
        down_outs = [pl.BlockSpec((chunk, D), lambda j: (j, 0))]

    def run_mlp(last, args):
        at = steps if last else 0
        up_in = pl.BlockSpec((1, D, chunk), lambda j: ((j + at) // per_unit, 0, (j + at) % per_unit))
        down_in = pl.BlockSpec((chunk, D), lambda j: (j + at, 0))
        wide = once(rows, D)
        scratch = (pltpu.VMEM((rows, D), bf),)
        if last:
            shapes = [sds((rows, D), bf), sds((rows, D), f32), sds((1, D), f32)]
            outs = [wide, wide, once(1, D)]
            scratch = scratch + (pltpu.VMEM((rows, D), f32), pltpu.VMEM((rows, D), f32))
        else:
            shapes = [sds((rows, D), f32), sds((rows, D), f32)]
            outs = [wide, wide]
        out = call(
            partial(mlp_both, steps, last, 4 * r),
            "mlp_both",
            tuple(shapes + up_shapes + down_shapes),
            [smem, wide, once(1, D), up_in, down_in, wide] + [wide, wide] * last,
            tuple(outs + up_outs + down_outs),
            (steps,),
            (core_id,) + args,
            scratch=scratch,
            flops=2 * rows * 12 * D * D,
        )
        count = len(outs)
        if fast:
            up = [y.reshape(nz, nq, 2, r, D) for y in out[count : count + 2]]
            down = [y.reshape(nz // 2, nq, 4, r, D) for y in out[count + 2 :]]
        else:
            up = place.halves(out[count], r)
            d = out[count + 1].reshape(nz // 2, nq, 2, 4, r, D)
            down = [pick(d, which, 2) for which in (core, 1 - core)]
        return tuple(out[:count]) + (list(up), list(down))

    def run_grads(body, name, shapes, specs, outs, args, units, scratch, flops):
        if fast:
            unit_shapes = [sds((zq, units, r, D), bf)] * 2
        else:
            unit_shapes = [sds((units, D, D), bf)]
        unit_outs = [whole(y.shape) for y in unit_shapes]
        out = call(
            body,
            name,
            tuple(shapes + unit_shapes),
            [smem] + specs,
            tuple(outs + unit_outs),
            (MICRO,),
            (core_id,) + args,
            scratch=scratch,
            flops=flops,
        )
        count = len(outs)
        if fast:
            pair = [y.reshape(nz, nq, units, r, D) for y in out[count:]]
        else:
            pair = list(place.halves(out[count], r))
        return tuple(out[:count]) + (pair,)

    got = stage((place.to_groups, blocks))[0]
    reading = merge([pick(blocks, place.group)] + list(got))
    for bit in range(2, nq.bit_length() - 1):
        reading = merge([reading, place.hop(reading, 1 << bit)])
    message = jnp.concatenate([reading[:, :GCOLS].astype(bf)] + split_three(reading[:, GCOLS:]), axis=-1)
    got, (y, dxn, up_one, down_one) = stage(
        (place.send_line, four), (partial(run_mlp, False), (v2, g_vmlp, w_up, w_down, cot))
    )
    all_four = all_dp(four, got)
    reads, (f_four, s_four), (v3, dv2, dg_vmlp, up_two, down_two) = stage(
        (place.group_hops, message),
        (squares, all_four),
        (partial(run_mlp, True), (v2, g_vmlp, w_up, w_down, cot, y, dxn)),
    )
    reads = place.in_order([message] + list(reads))
    lse_page = jnp.swapaxes(reads[..., GCOLS:], 0, 1).reshape(slots, 3 * HEADS)
    read_q = jnp.swapaxes(reads[..., :GCOLS], 0, 1).reshape(slots, D)

    def run_write_bwd(args):
        return run_grads(
            write_bwd,
            "write_bwd",
            [sds((rows, D), bf), sds((MICRO, slots, D), bf), sds((MICRO, slots, D), bf)],
            [act_block, act_block, of_pk(2), slot_block, slot_block, live_block, part_of(1, 6, None)[1]],
            [act_block, slot_block, slot_block],
            args,
            1,
            (pltpu.VMEM((D, D), f32),),
            4 * rows * D * D,
        )

    c_four, sib_four, sib_f_four, sib_s_four, (dwq, dwk, dwv, pair_wo) = stage(
        (place.second_hop, f_four),
        (place.sibling, all_four),
        (place.sibling, f_four),
        (place.sibling, s_four),
        (run_write_bwd, (dv2, writing, pk, wk, wv, live, w_two)),
    )
    sib_c_four, *net_got = stage(
        (place.sibling, c_four),
        (place.sibling, up_one[1]),
        (place.sibling, up_two[1]),
        (place.sibling, down_one[1]),
        (place.sibling, down_two[1]),
    )
    keep_down = jnp.concatenate([down_one[0], down_two[0]])
    down_got = jnp.concatenate([net_got[2], net_got[3]])
    second, corner, first, own_net = place.square_terms(
        place.chip_terms([(up_one[0], net_got[0]), (up_two[0], net_got[1]), (keep_down, down_got)])
    )

    def run_query(args):
        units, w_down = assemble(
            four, [all_four, f_four, s_four, c_four], [sib_four, sib_f_four, sib_s_four, sib_c_four], 5, 1
        )
        s1, read_q = args
        up_block = pl.BlockSpec((4, D, D), lambda *_: (0, 0, 0), pipeline_mode=pl.Buffered(1))
        return simple(
            partial(query_mlp, 2 * r, D // nz),
            "query_mlp",
            (chip_id, s1, read_q, part_of(1, 4, units), g_qmlp, (units, up_block), w_down, xs_cot),
            [
                ((slots, D), bf),
                ((slots, D), f32),
                ((slots, D), bf),
                ((5, 2 * r * nz, D), bf),
                ((8 * r * nz, D), bf),
                ((1, D), f32),
            ],
        )

    second, corner, (q_out, ds2, d_read, d_early, d_qdown, dg_qmlp) = stage(
        (partial(place.outer_hop, 1), second.astype(bf)),
        (partial(place.outer_hop, 1), corner.astype(bf)),
        (run_query, (s1, read_q)),
    )
    own_net = own_net + second.astype(f32)
    first = (first + corner.astype(f32)).astype(bf)

    def chip_halves(x, r):
        x = x.reshape(x.shape[0], nz, 2, r, D)
        return [jnp.swapaxes(pick(x, which, 2), 0, 1) for which in (core, 1 - core)]

    tall = [y.reshape(nz, 4, r, D) for y in chip_halves(d_qdown[None], 4 * r)]
    keep_early, give_early = (
        jnp.concatenate([a, b], axis=1) for a, b in zip(chip_halves(d_early, r), tall)
    )
    three_parts = jnp.concatenate([d_read, read_q, lse_page], axis=-1)
    parts_two, early_got = stage((place.sibling, three_parts), (place.sibling, give_early))
    three_parts = ordered(even, three_parts, parts_two)
    d_read_all, read_all = three_parts[..., :D], three_parts[..., D : 2 * D]
    lse_all = join_three(three_parts[..., 2 * D :].reshape(MICRO, slots, GROUPS, 3 * GHEADS))
    lse_all = jnp.pad(lse_all.reshape(MICRO, slots, HEADS), ((0, 0), (0, 0), (0, 128 - HEADS)))
    early = (keep_early.astype(f32) + early_got.astype(f32)).astype(bf)
    early_sum = lax.psum_scatter(early.reshape(nz, 9 * r, D), "dp", scatter_dimension=0).reshape(9, r, D)
    early_sum = early_sum.astype(f32)

    def run_read_bwd(args):
        return call(
            read_bwd,
            "read_bwd",
            (sds((MICRO, slots, D), bf), sds((rows, D), bf), sds((rows, D), bf)),
            [slot_block, of_pk(0), of_pk(1), slot_block, slot_block, stat_block],
            (slot_block, act_block, act_block),
            (MICRO,),
            args,
            flops=2 * rows * slots * D * 10,
        )

    first, (drq, dk, dv) = stage(
        (partial(place.outer_hop, 0), first), (run_read_bwd, (rq, pk, pk, d_read_all, read_all, lse_all))
    )

    def run_page_bwd(args):
        return run_grads(
            page_bwd,
            "page_bwd",
            [sds((rows, D), f32), sds((1, D), f32)],
            [act_block, act_block, act_block, act_block, act_block, whole((1, D)), whole((3, D, D))],
            [act_block, whole((1, D))],
            args,
            3,
            (pltpu.VMEM((3, D, D), f32), pltpu.VMEM((1, D), f32)),
            2 * rows * 6 * D * D,
        )

    d_slots = jnp.stack([drq, dwk, dwv], axis=1)
    own_net = place.inner_square((own_net + first.astype(f32)).astype(bf))
    net_sum = lax.psum_scatter(own_net.reshape(nz, 8 * r, D), "dp", scatter_dimension=0).reshape(8, r, D)
    slots_two, (dv1, dg_page, pair_page) = stage(
        (place.sibling, pick(d_slots, 1 - core)), (run_page_bwd, (v1, dv2, dk, dv, dwq, g_page, w_two))
    )
    d_slots = (pick(d_slots, core).astype(f32) + slots_two.astype(f32)).astype(bf)
    d_slots = jnp.transpose(d_slots.reshape(3, slots, GROUPS, GCOLS), (2, 0, 1, 3))

    def run_window_bwd(page, args):
        here = pl.BlockSpec((page_rows, D), lambda i: (page, 0))
        three_here = pl.BlockSpec((3, page_rows, D), lambda i: (0, page, 0))
        return pl.pallas_call(
            window_bwd,
            name="window_bwd",
            out_shape=sds((3, rows, D), bf),
            grid=(1,),
            in_specs=[here, three_here, here, whole(bias.shape), part_of(4, 0, None)[1]]
            + [pl.BlockSpec(memory_space=pl.ANY)] * page,
            out_specs=three_here,
            scratch_shapes=(pltpu.VMEM((page_rows, D), bf),),
            input_output_aliases={5: 0} if page else {},
            compiler_params=pltpu.CompilerParams(vmem_limit_bytes=58 * 1024 * 1024),
            cost_estimate=pl.CostEstimate(flops=rows * 2 * D * D, bytes_accessed=1 << 20, transcendentals=0),
        )(*args)

    page_got, got, dmix = stage(
        (siblings, [pair_page[1], pair_wo[1]]),
        (place.to_groups, d_slots),
        (partial(run_window_bwd, 0), (dv1, mix, att, bias, w_one)),
    )
    d_rd = sum(x.astype(f32) for x in [pick(d_slots, place.group)] + list(got)).astype(bf)
    for bit in range(2, nq.bit_length() - 1):
        d_rd = (d_rd.astype(f32) + place.hop(d_rd, 1 << bit).astype(f32)).astype(bf)
    second, corner, first, own_page = place.square_terms(
        place.chip_terms([(pair_page[0], page_got[0]), (pair_wo[0], page_got[1])])
    )
    rds, second, corner, dmix = stage(
        (place.group_hops, d_rd),
        (partial(place.outer_hop, 1), second.astype(bf)),
        (partial(place.outer_hop, 1), corner.astype(bf)),
        (partial(run_window_bwd, 1), (dv1, mix, att, bias, w_one, dmix)),
    )
    own_page = own_page + second.astype(f32)
    first = (first + corner.astype(f32)).astype(bf)
    d_rd = jnp.transpose(place.in_order([d_rd] + list(rds)), (1, 2, 0, 3)).reshape(3, slots, D)

    def run_query_back(args):
        return simple(
            partial(query_back, 2 * r, D // nz),
            "query_back",
            (*args[:6], part_of(3, 1, args[6]), part_of(4, 1, args[7]), *args[8:]),
            [((slots, D), bf), ((7, 2 * r * nz, D), bf), ((1, D), f32), ((1, D), f32)],
            scratch=(pltpu.VMEM((3, slots, D), bf),),
        )

    def run_window_grads(args):
        return run_grads(
            window_grads,
            "window_grads",
            [],
            [act_block, act_block, three_block, act_block, whole((1, D))],
            [],
            args,
            4,
            (pltpu.VMEM((4, D, D), f32),),
            2 * rows * 4 * D * D,
        )

    first, (pair_window,) = stage(
        (partial(place.outer_hop, 0), first), (run_window_grads, (dv1, x, dmix, att, g_window))
    )
    own_page = place.inner_square((own_page + first.astype(f32)).astype(bf))
    page_sum = lax.psum_scatter(own_page.reshape(nz, 4 * r, D), "dp", scatter_dimension=0).reshape(4, r, D)
    window_got, (x_grad, d_late, dg_slots, dg_reader) = stage(
        (place.sibling, pair_window[1]),
        (
            run_query_back,
            (chip_id, xs, s1, ds2, d_rd, g_reader, w_two, w_one, mix_q, att_q, own_live, g_slots),
        ),
    )
    keep_late, give_late = chip_halves(d_late, r)
    second, corner, first, own_window = place.square_terms(place.chip_terms([(pair_window[0], window_got)]))
    second, late_got = tie(second.astype(bf), place.sibling(give_late))
    late = (keep_late.astype(f32) + late_got.astype(f32)).astype(bf)

    def run_window_end(args):
        return call(
            window_end,
            "window_end",
            (sds((rows, D), bf), sds((1, D), f32)),
            [act_block, act_block, three_block, whole((1, D)), part_of(4, 0, None)[1]],
            (act_block, whole((1, D))),
            (MICRO,),
            args,
            scratch=(pltpu.VMEM((1, D), f32),),
            flops=2 * rows * 3 * D * D,
        )

    second, corner, late_passed, (v_grad, dg_window) = stage(
        (partial(place.outer_hop, 1), second),
        (partial(place.outer_hop, 1), corner.astype(bf)),
        (place.send_terms, late),
        (run_window_end, (dv1, x, dmix, g_window, w_one)),
    )
    own_window = own_window + second.astype(f32)
    first = (first + corner.astype(f32)).astype(bf)
    late_sum = place.own_terms(late) + sum(y.astype(f32) for y in late_passed)
    own_gains = jnp.concatenate([dg_window, dg_page, dg_vmlp])
    query_gains = jnp.concatenate([dg_slots, dg_reader, dg_qmlp])
    first, chip_gains = stage(
        (partial(place.outer_hop, 0), first),
        (lambda x: [place.hop(x, mask) for mask in range(1, nq)], own_gains),
    )
    own_window = place.inner_square((own_window + first.astype(f32)).astype(bf))
    gain_rows = jnp.concatenate([own_gains + sum(chip_gains), query_gains]).reshape(6, nz, nq, 2, r)
    gain_rows = pick(gain_rows, place.chip, 2)
    gain_rows = pick(gain_rows, core, 2) + place.sibling(pick(gain_rows, 1 - core, 2))
    gain_rows = jnp.swapaxes(gain_rows, 0, 1).reshape(nz, 1, 1, 6 * r).astype(bf)
    gain_rows = jnp.pad(gain_rows, ((0, 0), (0, 0), (0, r - 1), (0, D - 6 * r)))
    own_window = jnp.concatenate([own_window, gain_rows], axis=1)
    window_passed = place.send_terms(own_window)
    grad_win = place.own_terms(own_window) + sum(y.astype(f32) for y in window_passed)
    both = grad_win[4, 0, : 6 * r].reshape(6, r)

    visual_out = roll_out(v3.reshape(MICRO, height, WIN, D), place, bands)
    visual_grad = roll_out(v_grad.reshape(MICRO, height, WIN, D), place, bands)
    query_out = place.owned_rows(q_out)
    query_grad = place.owned_rows(x_grad)

    grad_page = page_sum.astype(f32)
    grad_up = net_sum[:4].astype(f32)
    grad_down = net_sum[4:].reshape(4 * r, D).astype(f32)
    grad_qup = jnp.concatenate([early_sum[k] for k in range(4)], axis=1)
    grad_ro = early_sum[4]
    grad_qdown = early_sum[5:].reshape(4 * r, D)
    grad_sq = jnp.concatenate([late_sum[k] for k in range(3)], axis=1)
    grad_so = late_sum[3]
    grad_rd = jnp.concatenate([late_sum[4 + k] for k in range(3)], axis=1)

    def wide(units):
        return jnp.concatenate([units[k] for k in range(units.shape[0])], axis=1)

    return (
        visual_out,
        query_out,
        visual_grad,
        query_grad,
        both[0],
        wide(grad_win[:3]),
        grad_win[3],
        both[3],
        grad_sq,
        grad_so,
        both[4],
        both[1],
        jnp.concatenate([grad_rd[:, :D], wide(grad_page[:2])], axis=1),
        grad_ro,
        jnp.concatenate([grad_page[2], grad_rd[:, D:]], axis=1),
        grad_page[3],
        both[2],
        wide(grad_up),
        grad_down,
        both[5],
        grad_qup,
        grad_qdown,
    )


def solution(mesh):
    page = P("dp", "fsdp", None, None)
    slot = P("dp", "fsdp", None)
    gain = P(("dp", "fsdp"))
    matrix = P(("dp", "fsdp"), None)
    weights = (
        gain,
        matrix,
        matrix,
        gain,
        matrix,
        matrix,
        gain,
        gain,
        matrix,
        matrix,
        matrix,
        matrix,
        gain,
        matrix,
        matrix,
        gain,
        matrix,
        matrix,
    )
    return jax.shard_map(
        local,
        mesh=mesh,
        in_specs=(page, slot, P("dp"), P("dp", None)) + weights + (page, slot),
        out_specs=(page, slot, page, slot) + weights,
        check_vma=False,
    )
```

time: 750 us -> 668 us (0.89)
  waiting for transfers between devices: 207 us -> 145 us
  Pallas kernels: 218 us -> 262 us
  local copies, waits for them, and re-layouts: 110 us -> 72.8 us
  other arithmetic: 97.6 us -> 62.5 us
  starting transfers between devices: 79.2 us -> 102 us
  between operations: 24.7 us -> 15.6 us
    ppermute x39 -> x38, waiting for transfers between devices: 116 us -> 40.3 us  [hop(): return lax.ppermute(x, 'fsdp', route)]
    pallas_call x15 -> x18, Pallas kernels: 146 us -> 198 us  [call(): pl.pallas_call(body, name=name, out_shape=out_shape, grid=grid, in_specs=...]
    ppermute x5 -> x20, waiting for transfers between devices: 39.2 us -> 89.3 us  [the longest x18 89.3 us: across(): return lax.ppermute(x, 'dp', [(z, z ^ mask) for z in range(self.nz)])]
    reduce_scatter x4 -> x3, waiting for transfers between devices: 33.6 us -> 5.12 us  [the longest x1 5.12 us: local(): lax.psum_scatter(own_page.reshape(nz, 4 * r, D), 'dp', scatter_dimension=0)]
    ppermute x5 -> x20, starting transfers between devices: 19.6 us -> 46.8 us  [the longest x18 41.9 us: across(): return lax.ppermute(x, 'dp', [(z, z ^ mask) for z in range(self.nz)])]
    concatenate x26 -> x13, other arithmetic: 23.3 us -> 8.29 us  [the longest x4 4.04 us: parts(): return jnp.concatenate(blocks, axis=-3)]
    ppermute x29 -> x33, starting transfers between devices: 20.4 us -> 6.6 us  [sibling(): return lax.ppermute(x, 'fsdp', [(f, f ^ 1) for f in range(self.nf)])]
    optimization_barrier x0 -> x8, local copies, waits for them, and re-layouts: none -> 13 us  [tie(): return lax.optimization_barrier(arrays)]
  transfers between devices with their start and end apart: 81 -> 96, of which waited for: 36 -> 26; matrix products, arithmetic and copies ran while one was open for 26% -> 14% of each run, Pallas kernels for 29% -> 38%
where the time goes in v1:
time: 668 us; the launch traced here: 660 us
  Pallas kernels  262 us (39%)
  waiting for transfers between devices  145 us (22%)
  starting transfers between devices  102 us (15%)
  local copies, waits for them, and re-layouts  72.8 us (11%)
  other arithmetic  62.5 us (9%)
  between operations  15.6 us (2%)
    pallas_call x18, Pallas kernels, call(): pl.pallas_call(body, name=name, out_shape=out_shape, grid=grid, in_specs=...  198 us
    ppermute x18, waiting for transfers between devices, across(): return lax.ppermute(x, 'dp', [(z, z ^ mask) for z in range(self.nz)])  89.3 us
    ppermute x38, starting transfers between devices, hop(): return lax.ppermute(x, 'fsdp', route)  48.9 us
    ppermute x18, starting transfers between devices, across(): return lax.ppermute(x, 'dp', [(z, z ^ mask) for z in range(self.nz)])  41.9 us
    ppermute x38, waiting for transfers between devices, hop(): return lax.ppermute(x, 'fsdp', route)  40.3 us
    pallas_call x4, Pallas kernels, place_units(): pl.pallas_call(body, name='place_units', grid=(nz,), out_shape=tuple(shap...  34.1 us
    pallas_call x2, Pallas kernels, run_window_bwd(): pl.pallas_call(window_bwd, name='window_bwd', out_shape=sds((3, rows, D),...  29.3 us
    unnamed x174, local copies, waits for them, and re-layouts  22.8 us
  transfers between devices with their start and end apart: 96, of which 26 were waited for; matrix products, arithmetic and copies ran while one was open for 14% of the time, Pallas kernels for 38%

profile of v1, /device:TPU:0, one launch (start us, length us, event | category | flops | bytes accessed | tf_op | source)
XLA Modules:
  0.0 660.4 jit_solution(12131557087006728827)
XLA Ops:
  21.7 8.5 %collective-permute-done = bf16[9,24,768]{2,1,0:T(8,128)(2,1)S(1)} collective-permute-done((bf16[9,24,768]{2,1,0:T(8,128)(2,1)}, bf16[9,24,768]{2,1,0:T(8,128)(2,1)S(1)}, u32[]{:S(2)}, u32[]{:S(2)}) %collective-permute-start) | collective-permute-done | bytes 331808 | tf_op jit(solution)/shard_map/ppermute | solution.py:660
  30.1 13.5 %collective-permute-done.1 = bf16[9,24,768]{2,1,0:T(8,128)(2,1)S(1)} collective-permute-done((bf16[9,24,768]{2,1,0:T(8,128)(2,1)}, bf16[9,24,768]{2,1,0:T(8,128)(2,1)S(1)}, u32[]{:S(2)}, u32[]{:S(2)}) %collective-permute-start.1) | collective-permute-done | bytes 331808 | tf_op jit(solution)/shard_map/ppermute | solution.py:660
  63.1 11.9 %collective-permute-done.6 = bf16[7,24,768]{2,1,0:T(8,128)(2,1)S(1)} collective-permute-done((bf16[7,24,768]{2,1,0:T(8,128)(2,1)S(1)}, bf16[7,24,768]{2,1,0:T(8,128)(2,1)S(1)}, u32[]{:S(2)}, u32[]{:S(2)}) %collective-permute-start.6) | collective-permute-done | bytes 258080 | tf_op jit(solution)/shard_map/ppermute | solution.py:660
  94.8 14.0 %collective-permute-done.11 = bf16[8,24,768]{2,1,0:T(8,128)(2,1)S(1)} collective-permute-done((bf16[8,24,768]{2,1,0:T(8,128)(2,1)}, bf16[8,24,768]{2,1,0:T(8,128)(2,1)S(1)}, u32[]{:S(2)}, u32[]{:S(2)}) %collective-permute-start.11) | collective-permute-done | bytes 294944 | tf_op jit(solution)/shard_map/ppermute | solution.py:660
  110.4 13.5 %collective-permute-done.14.args_2_ = bf16[4,7,24,768]{3,2,1,0:T(8,128)(2,1)S(1)} collective-permute-done((bf16[4,7,24,768]{3,2,1,0:T(8,128)(2,1)S(1)}, bf16[4,7,24,768]{3,2,1,0:T(8,128)(2,1)S(1)}, u32[]{:S(2)}, u32[]{:S(2)}) %collective-permute-start.14) | collective-permute-done | bytes 1032224 | tf_op jit(solution)/shard_map/ppermute | solution.py:657
  164.6 8.8 %place_units.4 = (bf16[8,16,48,768]{3,2,1,0:T(8,128)(2,1)}, f32[16,8,768]{2,1,0:T(8,128)}) custom-call(s32[3]{0:T(128)} %pad_add_fusion.table_ref, bf16[4,9,24,768]{3,2,1,0:T(8,128)(2,1)} %copy-done.2, bf16[4,9,24,768]{3,2,1,0:T(8,128)(2,1)} %copy-done.15, bf16[4,9,24,768]{3,2,1,0:T(8,128)(2,1)} %copy-done.16, ...), custom_call_target="tpu_custom_call" | custom-call | bytes 21233664 | tf_op jit(solution)/shard_map/place_units/pallas_call | solution.py:613
  180.9 16.5 %window_fwd.1 = (bf16[3,864,768]{2,1,0:T(8,128)(2,1)}, bf16[864,768]{1,0:T(8,128)(2,1)}, f32[864,768]{1,0:T(8,128)}) custom-call(bf16[864,768]{1,0:T(8,128)(2,1)} %roll_in.2.x_ref, f32[3,144,144]{2,1,0:T(8,128)} %compare_select_fusion.bias_ref, f32[1,768]{1,0:T(1,128)} %squeeze.286.gw_ref, bf16[8,768,768]{2,1,0:T(8,128)(2,1)} %bitcast.429), custom_call_target="tpu_custom_call" | custom-call | flops 4076863488 | bytes 1048576 | tf_op jit(solution)/shard_map/window_fwd/pallas_call | solution.py:108
  241.3 8.3 %place_units.6 = (bf16[4,16,48,768]{3,2,1,0:T(8,128)(2,1)}, bf16[16,192,768]{2,1,0:T(8,128)(2,1)}) custom-call(s32[3]{0:T(128)} %pad_add_fusion.table_ref, bf16[4,8,24,768]{3,2,1,0:T(8,128)(2,1)} %copy-done.4, bf16[4,8,24,768]{3,2,1,0:T(8,128)(2,1)} %collective-permute-done.25.args_1_, bf16[4,8,24,768]{3,2,1,0:T(8,128)(2,1)} %collective-permute-done.26.args_2_, ...), custom_call_target="tpu_custom_call" | custom-call | bytes 18874368 | tf_op jit(solution)/shard_map/place_units/pallas_call | solution.py:613
  249.6 8.0 %write_fwd.1 = (bf16[864,768]{1,0:T(8,128)(2,1)}, f32[864,768]{1,0:T(8,128)}) custom-call(f32[864,768]{1,0:T(8,128)} %get-tuple-element.598.x_ref.v1_ref, bf16[3,864,768]{2,1,0:T(8,128)(2,1)} %page_units.1.k_ref.v_ref.wq_ref, bf16[2,128,768]{2,1,0:T(8,128)(2,1)} %get-tuple-element.528.wk_ref, bf16[2,128,768]{2,1,0:T(8,128)(2,1)} %get-tuple-element.529.wv_ref, ...), custom_call_target="tpu_custom_call" | custom-call | flops 1019215872 | bytes 1048576 | tf_op jit(solution)/shard_map/write_fwd/pallas_call | solution.py:108
  267.5 27.7 %mlp_both.2 = (f32[864,768]{1,0:T(8,128)}, f32[864,768]{1,0:T(8,128)}, bf16[16,2,24,768]{3,2,1,0:T(8,128)(2,1)}, bf16[16,2,24,768]{3,2,1,0:T(8,128)(2,1)}, bf16[...) custom-call(s32[1]{0:T(128)} %bitcast.31.core_ref, f32[864,768]{1,0:T(8,128)} %get-tuple-element.501.x_ref, ...), custom_call_target="tpu_custom_call" | custom-call | flops 12230590464 | bytes 1048576 | tf_op jit(solution)/shard_map/mlp_both/pallas_call | solution.py:108
  296.8 9.2 %collective-permute-done.42 = bf16[9,24,768]{2,1,0:T(8,128)(2,1)S(1)} collective-permute-done((bf16[9,24,768]{2,1,0:T(8,128)(2,1)S(1)}, bf16[9,24,768]{2,1,0:T(8,128)(2,1)S(1)}, u32[]{:S(2)}, u32[]{:S(2)}) %collective-permute-start.42) | collective-permute-done | bytes 331808 | tf_op jit(solution)/shard_map/ppermute | solution.py:660
  311.7 30.9 %mlp_both.3 = (bf16[864,768]{1,0:T(8,128)(2,1)}, f32[864,768]{1,0:T(8,128)}, f32[1,768]{1,0:T(1,128)}, bf16[16,2,24,768]{3,2,1,0:T(8,128)(2,1)}, bf16[16,2,24,76...) custom-call(s32[1]{0:T(128)} %bitcast.31.core_ref, ...), custom_call_target="tpu_custom_call" | custom-call | flops 12230590464 | bytes 1048576 | tf_op jit(solution)/shard_map/mlp_both/pallas_call | solution.py:108
  344.9 14.8 %write_bwd.1 = (bf16[864,768]{1,0:T(8,128)(2,1)}, bf16[2,128,768]{2,1,0:T(8,128)(2,1)}, bf16[2,128,768]{2,1,0:T(8,128)(2,1)}, bf16[16,1,24,768]{3,2,1,0:T(8,128)(2,1)}, bf16[16,1,24,768]{3,2,1,0:T(8,128)(2,1)}) custom-call(s32[1]{0:T(128)} %bitcast.31.core_ref, f32[864,768]{1,0:T(8,128)} %get-tuple-element.599.dv2_ref, ...), custom_call_target="tpu_custom_call" | custom-call | flops 2038431744 | bytes 1048576 | tf_op jit(solution)/shard_map/write_bwd/pallas_call | solution.py:108
  386.9 9.1 %place_units.7 = (bf16[5,16,48,768]{3,2,1,0:T(8,128)(2,1)}, bf16[16,192,768]{2,1,0:T(8,128)(2,1)}) custom-call(s32[3]{0:T(128)} %pad_add_fusion.table_ref, bf16[4,9,24,768]{3,2,1,0:T(8,128)(2,1)} %copy-done.3, bf16[4,9,24,768]{3,2,1,0:T(8,128)(2,1)} %copy-done.17, bf16[4,9,24,768]{3,2,1,0:T(8,128)(2,1)} %copy-done.18, bf16[4,9,24,768]{3,2,1,0:T(8,128)(2,1)} %copy-done.19, ...), custom_call_target="tpu_custom_call" | custom-call | bytes 21233664 | tf_op jit(solution)/shard_map/place_units/pallas_call | solution.py:613
  396.0 13.3 %query_mlp.1 = (bf16[128,768]{1,0:T(8,128)(2,1)}, f32[128,768]{1,0:T(8,128)}, bf16[128,768]{1,0:T(8,128)(2,1)}, bf16[5,192,768]{2,1,0:T(8,128)(2,1)}, bf16[768,768]{1,0:T(8,128)(2,1)}, /*index=5*/f32[1,768]{1,0:T(1,128)}) custom-call(s32[1]{0:T(128)} %bitcast.101.chip_ref, f32[128,768]{1,0:T(8,128)} %get-tuple-element.662.x_ref.s1_ref, ...), custom_call_target="tpu_custom_call" | custom-call | flops 1073741824 | bytes 1048576 | tf_op jit(solution)/shard_map/query_mlp/pallas_call | solution.py:108
  424.8 8.6 %read_bwd.1 = (bf16[2,128,768]{2,1,0:T(8,128)(2,1)}, bf16[864,768]{1,0:T(8,128)(2,1)}, bf16[864,768]{1,0:T(8,128)(2,1)}) custom-call(bf16[2,128,768]{2,1,0:T(8,128)(2,1)} %get-tuple-element.582.rq_ref, bf16[3,864,768]{2,1,0:T(8,128)(2,1)} %page_units.1.k_ref.v_ref.wq_ref, bf16[3,864,768]{2,1,0:T(8,128)(2,1)} %page_units.1.k_ref.v_ref.wq_ref, ...), custom_call_target="tpu_custom_call" | custom-call | flops 1698693120 | bytes 1048576 | tf_op jit(solution)/shard_map/read_bwd/pallas_call | solution.py:108
  441.7 15.4 %page_bwd.1 = (f32[864,768]{1,0:T(8,128)}, f32[1,768]{1,0:T(1,128)}, bf16[16,3,24,768]{3,2,1,0:T(8,128)(2,1)}, bf16[16,3,24,768]{3,2,1,0:T(8,128)(2,1)}) custom-call(s32[1]{0:T(128)} %bitcast.31.core_ref, f32[864,768]{1,0:T(8,128)} %get-tuple-element.598.x_ref.v1_ref, f32[864,768]{1,0:T(8,128)} %get-tuple-element.599.dv2_ref, ...), custom_call_target="tpu_custom_call" | custom-call | flops 6115295232 | bytes 1048576 | tf_op jit(solution)/shard_map/page_bwd/pallas_call | solution.py:108
  469.7 14.8 %window_bwd.2.refs_0_ = bf16[3,864,768]{2,1,0:T(8,128)(2,1)} custom-call(f32[864,768]{1,0:T(8,128)} %get-tuple-element.683.dv1_ref, bf16[3,864,768]{2,1,0:T(8,128)(2,1)} %get-tuple-element.636.mix_ref, bf16[864,768]{1,0:T(8,128)(2,1)} %get-tuple-element.647.att_ref, f32[3,144,144]{2,1,0:T(8,128)} %compare_select_fusion.bias_ref, bf16[8,768,768]{2,1,0:T(8,128)(2,1)} %bitcast.430), custom_call_target="tpu_custom_call" | custom-call | flops 1019215872 | bytes 1048576 | tf_op jit(solution)/shard_map/window_bwd/pallas_call | solution.py:1308
  502.9 14.5 %window_bwd.3.dmix_ref = bf16[3,864,768]{2,1,0:T(8,128)(2,1)} custom-call(f32[864,768]{1,0:T(8,128)} %get-tuple-element.683.dv1_ref, bf16[3,864,768]{2,1,0:T(8,128)(2,1)} %get-tuple-element.636.mix_ref, bf16[864,768]{1,0:T(8,128)(2,1)} %get-tuple-element.647.att_ref, f32[3,144,144]{2,1,0:T(8,128)} %compare_select_fusion.bias_ref, ...), custom_call_target="tpu_custom_call", output_to_operand_aliasing={{}: (5, {})} | custom-call | flops 1019215872 | bytes 1048576 | tf_op jit(solution)/shard_map/window_bwd/pallas_call | solution.py:1308
  522.3 11.4 %window_grads.1 = (bf16[16,4,24,768]{3,2,1,0:T(8,128)(2,1)}, bf16[16,4,24,768]{3,2,1,0:T(8,128)(2,1)}) custom-call(s32[1]{0:T(128)} %bitcast.31.core_ref, f32[864,768]{1,0:T(8,128)} %get-tuple-element.683.dv1_ref, bf16[864,768]{1,0:T(8,128)(2,1)} %roll_in.2.x_ref, bf16[3,864,768]{2,1,0:T(8,128)(2,1)} %window_bwd.3.dmix_ref, ...), custom_call_target="tpu_custom_call" | custom-call | flops 4076863488 | bytes 1048576 | tf_op jit(solution)/shard_map/window_grads/pallas_call | solution.py:108
  554.5 11.7 %query_back.1 = (bf16[128,768]{1,0:T(8,128)(2,1)}, bf16[7,192,768]{2,1,0:T(8,128)(2,1)}, f32[1,768]{1,0:T(1,128)}, f32[1,768]{1,0:T(1,128)}) custom-call(s32[1]{0:T(128)} %bitcast.101.chip_ref, bf16[128,768]{1,0:T(8,128)(2,1)} %get-tuple-element.661.x_ref, f32[128,768]{1,0:T(8,128)} %get-tuple-element.662.x_ref.s1_ref, ...), custom_call_target="tpu_custom_call" | custom-call | flops 1073741824 | bytes 1048576 | tf_op jit(solution)/shard_map/query_back/pallas_call | solution.py:108
  589.3 9.2 %window_end.1 = (bf16[864,768]{1,0:T(8,128)(2,1)}, f32[1,768]{1,0:T(1,128)}) custom-call(f32[864,768]{1,0:T(8,128)} %get-tuple-element.683.dv1_ref, bf16[864,768]{1,0:T(8,128)(2,1)} %roll_in.2.x_ref, bf16[3,864,768]{2,1,0:T(8,128)(2,1)} %window_bwd.3.dmix_ref, f32[1,768]{1,0:T(1,128)} %get-tuple-element.686.gw_ref, bf16[8,768,768]{2,1,0:T(8,128)(2,1)} %bitcast.433), custom_call_target="tpu_custom_call" | custom-call | flops 3057647616 | bytes 1048576 | tf_op jit(solution)/shard_map/window_end/pallas_call | solution.py:108
  598.6 9.4 %collective-permute-done.81 = bf16[7,24,768]{2,1,0:T(8,128)(2,1)S(1)} collective-permute-done((bf16[7,24,768]{2,1,0:T(8,128)(2,1)S(1)}, bf16[7,24,768]{2,1,0:T(8,128)(2,1)S(1)}, u32[]{:S(2)}, u32[]{:S(2)}) %collective-permute-start.81) | collective-permute-done | bytes 258080 | tf_op jit(solution)/shard_map/ppermute | solution.py:660
  642.8 8.8 %collective-permute-done.91 = bf16[5,24,768]{2,1,0:T(8,128)(2,1)S(1)} collective-permute-done((bf16[5,24,768]{2,1,0:T(8,128)(2,1)S(1)}, bf16[5,24,768]{2,1,0:T(8,128)(2,1)S(1)}, u32[]{:S(2)}, u32[]{:S(2)}) %collective-permute-start.91) | collective-permute-done | bytes 184352 | tf_op jit(solution)/shard_map/ppermute | solution.py:660
  (539 shorter events, 333.2 us)
Async XLA Ops:
  7.2 536.7 %reduce-scatter.6.cloned.1.call-start = ((), (), s32[]{:S(2)}) async-start(), calls=%async_computation.4 | async-start | bytes 1658880 | tf_op jit(solution)/shard_map/reduce_scatter | solution.py:1264
  12.7 31.0 %collective-permute-start.4 = (bf16[2,36,6,768]{3,0,2,1:T(2,128)(2,1)S(1)}, bf16[2,36,6,768]{3,0,2,1:T(2,128)(2,1)S(1)}, u32[]{:S(2)}, u32[]{:S(2)}) collective-permute-start(bf16[2,36,6,768]{3,0,2,1:T(2,128)(2,1)S(1)} %slice.279), channel_id=1, source_target_pairs={{1,0},{2,1},{3,2},{4,3},{5,4},{6,5},{7,6},{0,7},{9,8},{10,9},{11,1... | collective-permute-start | bytes 1990664 | tf_op jit(solution)/shard_map/ppermute | solution.py:801
  45.7 29.2 %collective-permute-start.8 = (bf16[4,9,24,768]{3,2,1,0:T(8,128)(2,1)S(1)}, bf16[4,9,24,768]{3,2,1,0:T(8,128)(2,1)S(1)}, u32[]{:S(2)}, u32[]{:S(2)}) collective-permute-start(bf16[4,9,24,768]{3,2,1,0:T(8,128)(2,1)S(1)} %pad_maximum_fusion.4.args_0_), channel_id=1, source_target_pairs={{0,2},{1,5},{2,0},{3,7},{4,6},{5,1},{6,4},{7,3},{8,10},{9,13},{10,... | collective-permute-start | bytes 3981320 | tf_op jit(solution)/shard_map/ppermute | solution.py:657
  45.8 29.2 %collective-permute-start.9 = (bf16[4,9,24,768]{3,2,1,0:T(8,128)(2,1)S(1)}, bf16[4,9,24,768]{3,2,1,0:T(8,128)(2,1)S(1)}, u32[]{:S(2)}, u32[]{:S(2)}) collective-permute-start(bf16[4,9,24,768]{3,2,1,0:T(8,128)(2,1)S(1)} %pad_maximum_fusion.4.args_0_), channel_id=1, source_target_pairs={{0,4},{1,3},{2,6},{3,1},{4,0},{5,7},{6,2},{7,5},{8,12},{9,11},{10,... | collective-permute-start | bytes 3981320 | tf_op jit(solution)/shard_map/ppermute | solution.py:657
  76.7 32.6 %collective-permute-start.13 = (bf16[4,7,24,768]{3,2,1,0:T(8,128)(2,1)S(1)}, bf16[4,7,24,768]{3,2,1,0:T(8,128)(2,1)S(1)}, u32[]{:S(2)}, u32[]{:S(2)}) collective-permute-start(bf16[4,7,24,768]{3,2,1,0:T(8,128)(2,1)S(1)} %pad_maximum_fusion.11.args_0_), channel_id=1, source_target_pairs={{0,2},{1,5},{2,0},{3,7},{4,6},{5,1},{6,4},{7,3},{8,10},{9,13},{10,... | collective-permute-start | bytes 3096584 | tf_op jit(solution)/shard_map/ppermute | solution.py:657
  88.2 41.5 %collective-permute-start.15 = (bf16[4,9,24,768]{3,2,1,0:T(8,128)(2,1)}, bf16[4,9,24,768]{3,2,1,0:T(8,128)(2,1)}, u32[]{:S(2)}, u32[]{:S(2)}) collective-permute-start(bf16[4,9,24,768]{3,2,1,0:T(8,128)(2,1)} %copy-done.15), channel_id=1, source_target_pairs={{0,4},{1,3},{2,6},{3,1},{4,0},{5,7},{6,2},{7,5},{8,12},{9,11},{10,... | collective-permute-start | bytes 3981320 | tf_op jit(solution)/shard_map/ppermute | solution.py:657
  94.8 34.8 %collective-permute-start.16 = (bf16[4,9,24,768]{3,2,1,0:T(8,128)(2,1)S(1)}, bf16[4,9,24,768]{3,2,1,0:T(8,128)(2,1)}, u32[]{:S(2)}, u32[]{:S(2)}) collective-permute-start(bf16[4,9,24,768]{3,2,1,0:T(8,128)(2,1)S(1)} %pad_maximum_fusion.4.args_0_), channel_id=1, source_target_pairs={{0,1},{1,0},{2,3},{3,2},{4,5},{5,4},{6,7},{7,6},{8,9},{9,8},{10,11... | collective-permute-start | bytes 3981320 | tf_op jit(solution)/shard_map/ppermute | solution.py:652
  152.6 44.9 %collective-permute-start.25 = (bf16[4,8,24,768]{3,2,1,0:T(8,128)(2,1)S(1)}, bf16[4,8,24,768]{3,2,1,0:T(8,128)(2,1)}, u32[]{:S(2)}, u32[]{:S(2)}) collective-permute-start(bf16[4,8,24,768]{3,2,1,0:T(8,128)(2,1)S(1)} %pad_maximum_fusion.7.args_0_), channel_id=1, source_target_pairs={{0,2},{1,5},{2,0},{3,7},{4,6},{5,1},{6,4},{7,3},{8,10},{9,13},{10,... | collective-permute-start | bytes 3538952 | tf_op jit(solution)/shard_map/ppermute | solution.py:657
  160.6 36.9 %collective-permute-start.26 = (bf16[4,8,24,768]{3,2,1,0:T(8,128)(2,1)S(1)}, bf16[4,8,24,768]{3,2,1,0:T(8,128)(2,1)}, u32[]{:S(2)}, u32[]{:S(2)}) collective-permute-start(bf16[4,8,24,768]{3,2,1,0:T(8,128)(2,1)S(1)} %pad_maximum_fusion.7.args_0_), channel_id=1, source_target_pairs={{0,4},{1,3},{2,6},{3,1},{4,0},{5,7},{6,2},{7,5},{8,12},{9,11},{10,... | collective-permute-start | bytes 3538952 | tf_op jit(solution)/shard_map/ppermute | solution.py:657
  162.5 34.9 %collective-permute-start.27 = (bf16[4,7,24,768]{3,2,1,0:T(8,128)(2,1)}, bf16[4,7,24,768]{3,2,1,0:T(8,128)(2,1)S(1)}, u32[]{:S(2)}, u32[]{:S(2)}) collective-permute-start(bf16[4,7,24,768]{3,2,1,0:T(8,128)(2,1)} %copy-done.35), channel_id=1, source_target_pairs={{0,1},{1,0},{2,3},{3,2},{4,5},{5,4},{6,7},{7,6},{8,9},{9,8},{10,11... | collective-permute-start | bytes 3096584 | tf_op jit(solution)/shard_map/ppermute | solution.py:652
  162.5 34.9 %collective-permute-start.28 = (bf16[4,7,24,768]{3,2,1,0:T(8,128)(2,1)}, bf16[4,7,24,768]{3,2,1,0:T(8,128)(2,1)}, u32[]{:S(2)}, u32[]{:S(2)}) collective-permute-start(bf16[4,7,24,768]{3,2,1,0:T(8,128)(2,1)} %copy-done.36), channel_id=1, source_target_pairs={{0,1},{1,0},{2,3},{3,2},{4,5},{5,4},{6,7},{7,6},{8,9},{9,8},{10,11... | collective-permute-start | bytes 3096584 | tf_op jit(solution)/shard_map/ppermute | solution.py:652
  163.0 34.4 %collective-permute-start.29 = (bf16[4,7,24,768]{3,2,1,0:T(8,128)(2,1)}, bf16[4,7,24,768]{3,2,1,0:T(8,128)(2,1)}, u32[]{:S(2)}, u32[]{:S(2)}) collective-permute-start(bf16[4,7,24,768]{3,2,1,0:T(8,128)(2,1)} %collective-permute-done.20.args_3_), channel_id=1, source_target_pairs={{0,1},{1,0},{2,3},{3,2},{4,5},{5,4},{6,7},{7,6},{8,9},{9,8},{10,11... | collective-permute-start | bytes 3096584 | tf_op jit(solution)/shard_map/ppermute | solution.py:652
  257.7 39.1 %collective-permute-start.40 = (bf16[9,24,768]{2,1,0:T(8,128)(2,1)S(1)}, bf16[9,24,768]{2,1,0:T(8,128)(2,1)S(1)}, u32[]{:S(2)}, u32[]{:S(2)}) collective-permute-start(bf16[9,24,768]{2,1,0:T(8,128)(2,1)S(1)} %copy-done.52), channel_id=1, source_target_pairs={{0,8},{8,0},{16,24},{24,16},{1,9},{9,1},{17,25},{25,17},{2,10},{10... | collective-permute-start | bytes 995336 | tf_op jit(solution)/shard_map/ppermute | solution.py:660
  262.4 34.4 %collective-permute-start.41 = (bf16[9,24,768]{2,1,0:T(8,128)(2,1)S(1)}, bf16[9,24,768]{2,1,0:T(8,128)(2,1)S(1)}, u32[]{:S(2)}, u32[]{:S(2)}) collective-permute-start(bf16[9,24,768]{2,1,0:T(8,128)(2,1)S(1)} %copy-done.52), channel_id=1, source_target_pairs={{0,16},{8,24},{16,0},{24,8},{1,17},{9,25},{17,1},{25,9},{2,18},{10... | collective-permute-start | bytes 995336 | tf_op jit(solution)/shard_map/ppermute | solution.py:660
  263.9 31.3 %collective-permute-start.37 = (f32[128,195]{0,1:T(8,128)S(1)}, f32[128,195]{0,1:T(8,128)S(1)}, u32[]{:S(2)}, u32[]{:S(2)}) collective-permute-start(f32[128,195]{0,1:T(8,128)S(1)} %get-tuple-element.850), channel_id=1, source_target_pairs={{0,2},{1,3},{2,0},{3,1},{4,6},{5,7},{6,4},{7,5},{8,10},{9,11},{10,... | collective-permute-start | bytes 299528 | tf_op jit(solution)/shard_map/ppermute | solution.py:657
  265.5 31.2 %collective-permute-start.38 = (f32[128,195]{0,1:T(8,128)S(1)}, f32[128,195]{0,1:T(8,128)S(1)}, u32[]{:S(2)}, u32[]{:S(2)}) collective-permute-start(f32[128,195]{0,1:T(8,128)S(1)} %get-tuple-element.849), channel_id=1, source_target_pairs={{0,4},{1,5},{2,6},{3,7},{4,0},{5,1},{6,2},{7,3},{8,12},{9,13},{10,... | collective-permute-start | bytes 299528 | tf_op jit(solution)/shard_map/ppermute | solution.py:657
  265.9 30.8 %collective-permute-start.39 = (f32[128,195]{0,1:T(8,128)S(1)}, f32[128,195]{0,1:T(8,128)S(1)}, u32[]{:S(2)}, u32[]{:S(2)}) collective-permute-start(f32[128,195]{0,1:T(8,128)S(1)} %get-tuple-element.848), channel_id=1, source_target_pairs={{0,6},{1,7},{2,4},{3,5},{4,2},{5,3},{6,0},{7,1},{8,14},{9,15},{10,... | collective-permute-start | bytes 299528 | tf_op jit(solution)/shard_map/ppermute | solution.py:657
  306.1 36.5 %collective-permute-start.46 = (bf16[4,9,24,768]{3,2,1,0:T(8,128)(2,1)S(1)}, bf16[4,9,24,768]{3,2,1,0:T(8,128)(2,1)S(1)}, u32[]{:S(2)}, u32[]{:S(2)}) collective-permute-start(bf16[4,9,24,768]{3,2,1,0:T(8,128)(2,1)S(1)} %pad_maximum_fusion.5.args_0_), channel_id=1, source_target_pairs={{0,2},{1,5},{2,0},{3,7},{4,6},{5,1},{6,4},{7,3},{8,10},{9,13},{10,... | collective-permute-start | bytes 3981320 | tf_op jit(solution)/shard_map/ppermute | solution.py:657
  307.9 34.8 %collective-permute-start.47 = (bf16[4,9,24,768]{3,2,1,0:T(8,128)(2,1)S(1)}, bf16[4,9,24,768]{3,2,1,0:T(8,128)(2,1)S(1)}, u32[]{:S(2)}, u32[]{:S(2)}) collective-permute-start(bf16[4,9,24,768]{3,2,1,0:T(8,128)(2,1)S(1)} %pad_maximum_fusion.5.args_0_), channel_id=1, source_target_pairs={{0,4},{1,3},{2,6},{3,1},{4,0},{5,7},{6,2},{7,5},{8,12},{9,11},{10,... | collective-permute-start | bytes 3981320 | tf_op jit(solution)/shard_map/ppermute | solution.py:657
  308.2 34.4 %collective-permute-start.43 = (bf16[128,201]{0,1:T(8,128)(2,1)S(1)}, bf16[128,201]{0,1:T(8,128)(2,1)S(1)}, u32[]{:S(2)}, u32[]{:S(2)}) collective-permute-start(bf16[128,201]{0,1:T(8,128)(2,1)S(1)} %get-tuple-element.499), channel_id=1, source_target_pairs={{0,2},{1,3},{2,0},{3,1},{4,6},{5,7},{6,4},{7,5},{8,10},{9,11},{10,... | collective-permute-start | bytes 154376 | tf_op jit(solution)/shard_map/ppermute | solution.py:657
  309.8 32.8 %collective-permute-start.44 = (bf16[128,201]{0,1:T(8,128)(2,1)S(1)}, bf16[128,201]{0,1:T(8,128)(2,1)S(1)}, u32[]{:S(2)}, u32[]{:S(2)}) collective-permute-start(bf16[128,201]{0,1:T(8,128)(2,1)S(1)} %get-tuple-element.499), channel_id=1, source_target_pairs={{0,4},{1,5},{2,6},{3,7},{4,0},{5,1},{6,2},{7,3},{8,12},{9,13},{10,... | collective-permute-start | bytes 154376 | tf_op jit(solution)/shard_map/ppermute | solution.py:657
  310.3 32.3 %collective-permute-start.45 = (bf16[128,201]{0,1:T(8,128)(2,1)S(1)}, bf16[128,201]{0,1:T(8,128)(2,1)S(1)}, u32[]{:S(2)}, u32[]{:S(2)}) collective-permute-start(bf16[128,201]{0,1:T(8,128)(2,1)S(1)} %get-tuple-element.499), channel_id=1, source_target_pairs={{0,6},{1,7},{2,4},{3,5},{4,2},{5,3},{6,0},{7,1},{8,14},{9,15},{10,... | collective-permute-start | bytes 154376 | tf_op jit(solution)/shard_map/ppermute | solution.py:657
  461.1 89.4 %reduce-scatter.8.cloned.1.call-start = ((), (), s32[]{:S(2)}) async-start(), calls=%async_computation.5 | async-start | bytes 1474560 | tf_op jit(solution)/shard_map/reduce_scatter | solution.py:1298
  502.9 72.0 %reduce-scatter.4.cloned.1.call-start = ((), (), s32[]{:S(2)}) async-start(), calls=%async_computation.3 | async-start | bytes 737280 | tf_op jit(solution)/shard_map/reduce_scatter | solution.py:1369
  (156 other events, 1937.7 us)
Sparse Core Ops, SparseCore 0:
  461.2 35.4 reduce-scatter.5
  503.0 32.7 reduce-scatter.7
  549.9 24.9 reduce-scatter.3

commit v2 on v1

--- a/solution.py
+++ b/solution.py
@@ -71,37 +71,52 @@
     return jnp.where(mask, stacked[:rows], stacked[rows:])
 
 
-def pair_forward(q2, k2, v2, bias):
-    mask = low_lanes(q2.shape[0])
-    s = dot_t(twofold(q2, mask), k2) * SCALE
+def groups_of_pairs(q_rows, k_rows):
+    together = max(1, min(PAIRS, 700000 // (2 * q_rows * k_rows)))
+    return [range(p, min(p + together, PAIRS)) for p in range(0, PAIRS, together)]
+
+
+def lanes(p):
+    return slice(p * 2 * HEAD, (p + 1) * 2 * HEAD)
+
+
+def scaled(q2, mask):
+    return twofold(q2 * jnp.asarray(SCALE, bf), mask)
+
+
+def pairs_forward(q, k, v, bias):
+    mask = low_lanes(q[0].shape[0])
+    s = [dot_t(scaled(q2, mask), k2) for q2, k2 in zip(q, k)]
     if bias is not None:
-        s = s + bias
-    m = jnp.max(s, axis=-1, keepdims=True)
-    e = jnp.exp(s - m)
-    l = jnp.sum(e, axis=-1, keepdims=True)
-    out = dot(e.astype(bf), v2) / l
-    return onefold(out, mask), m, l
-
-
-def pair_backward(q2, k2, v2, d2, a2, bias, lse=None):
-    mask = low_lanes(q2.shape[0])
-    qs = twofold(q2, mask)
-    ds = twofold(d2, mask)
-    s = dot_t(qs, k2) * SCALE
+        s = [x + bias for x in s]
+    m = [jnp.max(x, axis=-1, keepdims=True) for x in s]
+    e = [jnp.exp(x - top) for x, top in zip(s, m)]
+    l = [jnp.sum(x, axis=-1, keepdims=True) for x in e]
+    out = [dot(x.astype(bf), v2) for x, v2 in zip(e, v)]
+    return [(onefold(x / total, mask), top, total) for x, top, total in zip(out, m, l)]
+
+
+def pairs_backward(q, k, v, d, a, bias, lse=None):
+    mask = low_lanes(q[0].shape[0])
+    qs = [scaled(q2, mask) for q2 in q]
+    ds = [twofold(d2, mask) for d2 in d]
+    s = [dot_t(q2, k2) for q2, k2 in zip(qs, k)]
+    dp = [dot_t(d2, v2) for d2, v2 in zip(ds, v)]
+    corr = [
+        jnp.sum(d2.astype(f32) * twofold(a2, mask).astype(f32), axis=-1, keepdims=True) for d2, a2 in zip(ds, a)
+    ]
     if bias is not None:
-        s = s + bias
+        s = [x + bias for x in s]
     if lse is None:
-        e = jnp.exp(s - jnp.max(s, axis=-1, keepdims=True))
-        p = e * (1.0 / jnp.sum(e, axis=-1, keepdims=True))
+        e = [jnp.exp(x - jnp.max(x, axis=-1, keepdims=True)) for x in s]
+        p = [x * (1.0 / jnp.sum(x, axis=-1, keepdims=True)) for x in e]
     else:
-        p = jnp.exp(s - lse)
-    corr = jnp.sum(ds.astype(f32) * twofold(a2, mask).astype(f32), axis=-1, keepdims=True)
-    dp = dot_t(ds, v2)
-    dsc = (p * (dp - corr)).astype(bf)
-    dq = onefold(dot(dsc, k2), mask) * SCALE
-    dk = t_dot(dsc, qs) * SCALE
-    dv = t_dot(p.astype(bf), ds)
-    return dq, dk, dv
+        p = [jnp.exp(x - y) for x, y in zip(s, lse)]
+    dsc = [(x * (y - c)).astype(bf) for x, y, c in zip(p, dp, corr)]
+    dq = [onefold(dot(x, k2), mask) * SCALE for x, k2 in zip(dsc, k)]
+    dk = [t_dot(x, q2) for x, q2 in zip(dsc, qs)]
+    dv = [t_dot(x.astype(bf), d2) for x, d2 in zip(p, ds)]
+    return list(zip(dq, dk, dv))
 
 
 def call(body, name, out_shape, in_specs, out_specs, grid, args, scratch=(), flops=0):
@@ -145,10 +160,11 @@
         at = pl.ds(pl.multiple_of(w * PATCH, 16), PATCH)
         bias = bias_ref[w]
         bias = jnp.concatenate([bias, bias], axis=0)
-        for p in range(PAIRS):
-            c = slice(p * 128, p * 128 + 128)
-            out = pair_forward(mix_ref[0, at, c], mix_ref[1, at, c], mix_ref[2, at, c], bias)[0]
-            att_ref[at, c] = out.astype(bf)
+        for group in groups_of_pairs(PATCH, PATCH):
+            cs = [lanes(p) for p in group]
+            outs = pairs_forward(*([mix_ref[u, at, c] for c in cs] for u in range(3)), bias)
+            for c, (out, _, _) in zip(cs, outs):
+                att_ref[at, c] = out.astype(bf)
         return carry
 
     lax.fori_loop(0, rows // PATCH, window, 0)
@@ -165,21 +181,23 @@
     slots = rq_ref.shape[1]
     lane = lax.broadcasted_iota(jnp.int32, (slots, 128), 1)
     acc = jnp.zeros((slots, 128), f32)
-    for p in range(PAIRS):
-        c = slice(p * 128, p * 128 + 128)
-        out, m, l = pair_forward(rq_ref[0, :, c], k_ref[0, :, c], v_ref[0, :, c], None)
-        o_ref[0, :, c] = out
-        lse = m + jnp.log(l)
-        acc = jnp.where(lane == 2 * p, lse[:slots], acc)
-        acc = jnp.where(lane == 2 * p + 1, lse[slots:], acc)
+    for group in groups_of_pairs(slots, k_ref.shape[1]):
+        cs = [lanes(p) for p in group]
+        outs = pairs_forward(*([ref[0, :, c] for c in cs] for ref in (rq_ref, k_ref, v_ref)), None)
+        for p, c, (out, m, l) in zip(group, cs, outs):
+            o_ref[0, :, c] = out
+            lse = m + jnp.log(l)
+            acc = jnp.where(lane == 2 * p, lse[:slots], acc)
+            acc = jnp.where(lane == 2 * p + 1, lse[slots:], acc)
     lse_ref[0] = acc
 
 
 def write_fwd(v1_ref, wq_ref, wk_ref, wv_ref, bias_ref, wo_ref, wr_ref, v2_ref):
-    for p in range(PAIRS):
-        c = slice(p * 128, p * 128 + 128)
-        out = pair_forward(wq_ref[0, :, c], wk_ref[0, :, c], wv_ref[0, :, c], bias_ref[0])[0]
-        wr_ref[:, c] = out.astype(bf)
+    for group in groups_of_pairs(wq_ref.shape[1], wk_ref.shape[1]):
+        cs = [lanes(p) for p in group]
+        outs = pairs_forward(*([ref[0, :, c] for c in cs] for ref in (wq_ref, wk_ref, wv_ref)), bias_ref[0])
+        for c, (out, _, _) in zip(cs, outs):
+            wr_ref[:, c] = out.astype(bf)
     v2_ref[...] = v1_ref[...] + dot(wr_ref[...], wo_ref[0])
 
 
@@ -216,7 +234,7 @@
     else:
         span = 2 * rows_of_core
         for i in range(d_down.shape[0] // span):
-            emit(core_ref, d_down[i * span : (i + 1) * span], outs[2], outs[3], i)
+            emit(core_ref, d_down[i * span : (i + 1) * span], outs[2], outs[3], (i, 0))
 
     @pl.when(j == 0)
     def _():
@@ -259,28 +277,27 @@
     def _():
         emit_unit(core_ref, acc_ref[...], outs, 0)
 
-    for p in range(PAIRS):
-        c = slice(p * 128, p * 128 + 128)
-        dq, dk, dv = pair_backward(
-            wq_ref[0, :, c], wk_ref[0, :, c], wv_ref[0, :, c], dwr[:, c], wr_ref[:, c], bias_ref[0]
-        )
-        dwq_ref[:, c] = dq.astype(bf)
-        dwk_ref[0, :, c] = dk.astype(bf)
-        dwv_ref[0, :, c] = dv.astype(bf)
+    for group in groups_of_pairs(wq_ref.shape[1], wk_ref.shape[1]):
+        cs = [lanes(p) for p in group]
+        parts = ([ref[0, :, c] for c in cs] for ref in (wq_ref, wk_ref, wv_ref))
+        grads = pairs_backward(*parts, [dwr[:, c] for c in cs], [wr_ref[:, c] for c in cs], bias_ref[0])
+        for c, (dq, dk, dv) in zip(cs, grads):
+            dwq_ref[:, c] = dq.astype(bf)
+            dwk_ref[0, :, c] = dk.astype(bf)
+            dwv_ref[0, :, c] = dv.astype(bf)
 
 
 def read_bwd(rq_ref, k_ref, v_ref, d_ref, r_ref, lse_ref, dq_ref, dk_ref, dv_ref):
     slots = rq_ref.shape[1]
     lse = lse_ref[0]
-    for p in range(PAIRS):
-        c = slice(p * 128, p * 128 + 128)
-        both = jnp.concatenate([lse[:, 2 * p : 2 * p + 1], lse[:, 2 * p + 1 : 2 * p + 2]], axis=0)
-        dq, dk, dv = pair_backward(
-            rq_ref[0, :, c], k_ref[0, :, c], v_ref[0, :, c], d_ref[0, :, c], r_ref[0, :, c], None, both
-        )
-        dq_ref[0, :, c] = dq.astype(bf)
-        dk_ref[:, c] = dk.astype(bf)
-        dv_ref[:, c] = dv.astype(bf)
+    for group in groups_of_pairs(slots, k_ref.shape[1]):
+        cs = [lanes(p) for p in group]
+        both = [jnp.concatenate([lse[:, 2 * p + k : 2 * p + k + 1] for k in range(2)], axis=0) for p in group]
+        parts = ([ref[0, :, c] for c in cs] for ref in (rq_ref, k_ref, v_ref, d_ref, r_ref))
+        for c, (dq, dk, dv) in zip(cs, pairs_backward(*parts, None, both)):
+            dq_ref[0, :, c] = dq.astype(bf)
+            dk_ref[:, c] = dk.astype(bf)
+            dv_ref[:, c] = dv.astype(bf)
 
 
 def emit(core_ref, rows, keep_ref, give_ref, at):
@@ -295,10 +312,12 @@
     if len(outs) == 1:
         outs[0][u] = unit.astype(bf)
         return
-    chips = outs[0].shape[0]
-    span = unit.shape[0] // chips
-    for i in range(chips):
-        emit(core_ref, unit[i * span : (i + 1) * span], outs[0], outs[1], (i, u))
+    nq, nz = outs[0].shape[:2]
+    span = unit.shape[0] // (nq * nz)
+    for z in range(nz):
+        for q in range(nq):
+            i = z * nq + q
+            emit(core_ref, unit[i * span : (i + 1) * span], outs[0], outs[1], (q, z, u))
 
 
 def page_bwd(core_ref, v1_ref, dv2_ref, dk_ref, dv_ref, dwq_ref, gp_ref, wp_ref, dv1_ref, dg_ref, *refs):
@@ -339,14 +358,13 @@
         at = pl.ds(pl.multiple_of(w * PATCH, 16), PATCH)
         bias = bias_ref[w]
         bias = jnp.concatenate([bias, bias], axis=0)
-        for p in range(PAIRS):
-            c = slice(p * 128, p * 128 + 128)
-            dq, dk, dv = pair_backward(
-                mix_ref[0, at, c], mix_ref[1, at, c], mix_ref[2, at, c], datt_ref[at, c], att_ref[at, c], bias
-            )
-            dmix_ref[0, at, c] = dq.astype(bf)
-            dmix_ref[1, at, c] = dk.astype(bf)
-            dmix_ref[2, at, c] = dv.astype(bf)
+        for group in groups_of_pairs(PATCH, PATCH):
+            cs = [lanes(p) for p in group]
+            parts = ([mix_ref[u, at, c] for c in cs] for u in range(3))
+            grads = pairs_backward(*parts, [datt_ref[at, c] for c in cs], [att_ref[at, c] for c in cs], bias)
+            for c, grad in zip(cs, grads):
+                for u in range(3):
+                    dmix_ref[u, at, c] = grad[u].astype(bf)
         return carry
 
     lax.fori_loop(0, rows // PATCH, window, 0)
@@ -399,10 +417,11 @@
     xn = (normalise(x)[0] * g_ref[...]).astype(bf)
     for u in range(3):
         mix_ref[u] = dot(xn, w_ref[u]).astype(bf)
-    for p in range(PAIRS):
-        c = slice(p * 128, p * 128 + 128)
-        out = pair_forward(mix_ref[0, :, c], mix_ref[1, :, c], mix_ref[2, :, c], bias_ref[...])[0]
-        att_ref[:, c] = out.astype(bf)
+    for group in groups_of_pairs(x.shape[0], x.shape[0]):
+        cs = [lanes(p) for p in group]
+        outs = pairs_forward(*([mix_ref[u, :, c] for c in cs] for u in range(3)), bias_ref[...])
+        for c, (out, _, _) in zip(cs, outs):
+            att_ref[:, c] = out.astype(bf)
     s1_ref[...] = x + dot(att_ref[...], w_ref[3])
 
 
@@ -415,10 +434,19 @@
     return dot(x, jnp.where(row == at, 1.0, 0.0).astype(bf)).astype(bf)
 
 
+def emit_chip(core_ref, unit, outs, u, r):
+    if len(outs) == 1:
+        outs[0][u] = unit.astype(bf)
+        return
+    for z in range(unit.shape[0] // (2 * r)):
+        emit(core_ref, unit[z * 2 * r : (z + 1) * 2 * r], outs[0], outs[1], (z, u))
+
+
 def query_mlp(
     span,
     step,
     chip_ref,
+    core_ref,
     s1_ref,
     read_ref,
     wo_ref,
@@ -429,11 +457,11 @@
     out_ref,
     ds2_ref,
     dread_ref,
-    dw_ref,
-    ddown_ref,
     dg_ref,
+    *outs,
 ):
     chip = chip_ref[0]
+    split = len(outs) // 2
     reading = read_ref[...]
     s2 = s1_ref[...] + dot(reading, wo_ref[0])
     hat, inv = normalise(s2)
@@ -449,10 +477,14 @@
         dpre = (dot_t(cot, down) * slope).astype(bf)
         part = dot_t(dpre, up)
         dxn = part if dxn is None else dxn + part
-        dw_ref[k] = t_dot(x_own, dpre).astype(bf)
+        emit_chip(core_ref, t_dot(x_own, dpre), outs[:split], k, span // 2)
         act_own = own_columns(act, chip, 4 * span, 4 * step)
         rows = act_own.shape[1]
-        ddown_ref[k * rows : (k + 1) * rows] = t_dot(act_own, cot).astype(bf)
+        d_down = t_dot(act_own, cot)
+        if split == 1:
+            outs[1][0, k * rows : (k + 1) * rows] = d_down.astype(bf)
+        else:
+            emit(core_ref, d_down, outs[2], outs[3], (k, 0))
     out_ref[...] = y.astype(bf)
     dx, dg = norm_back(dxn, hat, inv, g_ref[...])
     ds2 = cot.astype(f32) + dx
@@ -460,13 +492,14 @@
     dg_ref[...] = dg
     d2b = ds2.astype(bf)
     dread_ref[...] = dot_t(d2b, wo_ref[0]).astype(bf)
-    dw_ref[4] = t_dot(own_columns(reading, chip, span, step), d2b).astype(bf)
+    emit_chip(core_ref, t_dot(own_columns(reading, chip, span, step), d2b), outs[:split], 4, span // 2)
 
 
 def query_back(
     span,
     step,
     chip_ref,
+    core_ref,
     x_ref,
     s1_ref,
     ds2_ref,
@@ -479,11 +512,11 @@
     bias_ref,
     gs_ref,
     out_ref,
-    dw_ref,
     dgs_ref,
     dgr_ref,
-    dmix_ref,
+    *refs,
 ):
+    outs, dmix_ref = refs[:-1], refs[-1]
     chip = chip_ref[0]
     hat, inv = normalise(s1_ref[...])
     rn_own = own_columns((hat * gr_ref[...]).astype(bf), chip, span, step)
@@ -491,18 +524,18 @@
     dx, dg = norm_back(drn, hat, inv, gr_ref[...])
     dgr_ref[...] = dg
     for u in range(3):
-        dw_ref[4 + u] = t_dot(rn_own, d_ref[u]).astype(bf)
+        emit_chip(core_ref, t_dot(rn_own, d_ref[u]), outs, 4 + u, span // 2)
     ds1 = ds2_ref[...] + dx
     d1b = ds1.astype(bf)
     datt = dot_t(d1b, ws_ref[3]).astype(bf)
-    dw_ref[3] = t_dot(own_columns(att_ref[...], chip, span, step), d1b).astype(bf)
-    for p in range(PAIRS):
-        c = slice(p * 128, p * 128 + 128)
-        grads = pair_backward(
-            mix_ref[0, :, c], mix_ref[1, :, c], mix_ref[2, :, c], datt[:, c], att_ref[:, c], bias_ref[...]
-        )
-        for u in range(3):
-            dmix_ref[u, :, c] = grads[u].astype(bf)
+    emit_chip(core_ref, t_dot(own_columns(att_ref[...], chip, span, step), d1b), outs, 3, span // 2)
+    for group in groups_of_pairs(datt.shape[0], datt.shape[0]):
+        cs = [lanes(p) for p in group]
+        parts = ([mix_ref[u, :, c] for c in cs] for u in range(3))
+        grads = pairs_backward(*parts, [datt[:, c] for c in cs], [att_ref[:, c] for c in cs], bias_ref[...])
+        for c, grad in zip(cs, grads):
+            for u in range(3):
+                dmix_ref[u, :, c] = grad[u].astype(bf)
     hat, inv = normalise(x_ref[...].astype(f32))
     xn_own = own_columns((hat * gs_ref[...]).astype(bf), chip, span, step)
     dxn = dot_t(dmix_ref[0], ws_ref[0]) + dot_t(dmix_ref[1], ws_ref[1]) + dot_t(dmix_ref[2], ws_ref[2])
@@ -510,7 +543,7 @@
     dgs_ref[...] = dg
     out_ref[...] = (ds1 + dx).astype(bf)
     for u in range(3):
-        dw_ref[u] = t_dot(xn_own, dmix_ref[u]).astype(bf)
+        emit_chip(core_ref, t_dot(xn_own, dmix_ref[u]), outs, u, span // 2)
 
 
 def simple(body, name, args, outs, scratch=()):
@@ -584,10 +617,9 @@
 
         @pl.when(now == 0)
         def _():
-            for k, there in targets():
-                for m in range(nz):
-                    at = jnp.bitwise_xor(z, m)
-                    pltpu.make_async_copy(refs[k].at[m], there.at[at], sem.at[k, at]).start()
+            for to in range(nz):
+                for k, there in targets():
+                    pltpu.make_async_copy(refs[k].at[jnp.bitwise_xor(z, to)], there.at[to], sem.at[k, to]).start()
 
         for k, there in targets():
             pltpu.make_async_copy(refs[k].at[0], there.at[now], sem.at[k, now]).wait()
@@ -697,11 +729,15 @@
         return jnp.transpose(now, (3, 2, 1, 0, 4, 5))
 
     def chip_terms(self, pairs):
-        def parts(i):
+        def parts(i, kind=f32):
             blocks = []
-            for keep, other in pairs:
-                shape = (self.nz, 4) + (() if self.nq == 4 else (self.nq // 4,)) + keep.shape[2:]
-                blocks.append(pick(keep.reshape(shape), i, 1).astype(f32) + pick(other.reshape(shape), i, 1).astype(f32))
+            for pair in pairs:
+                along = []
+                for keep, other in pair if isinstance(pair[0], (tuple, list)) else [pair]:
+                    shape = (4,) + (() if self.nq == 4 else (self.nq // 4,)) + keep.shape[1:]
+                    block = pick(keep.reshape(shape), i).astype(f32) + pick(other.reshape(shape), i).astype(f32)
+                    along.append((block if self.nq == 4 else jnp.swapaxes(block, 0, 1)).astype(kind))
+                blocks.append(along[0] if len(along) == 1 else jnp.concatenate(along))
             return jnp.concatenate(blocks, axis=-3)
 
         return parts
@@ -710,7 +746,7 @@
         x = x.reshape((-1, self.nz, self.nq, 2, r, x.shape[-1]))
 
         def rows(which):
-            return jnp.moveaxis(pick(x, which, 3), 0, 2)
+            return jnp.transpose(pick(x, which, 3), (2, 1, 0, 3, 4))
 
         return rows(self.core), rows(1 - self.core)
 
@@ -718,7 +754,8 @@
         bit = (self.nq.bit_length() - 1) - 2
         here = (self.chip >> bit) % 4
         first = jnp.where(self.even, 1, 2)
-        return [parts(here ^ mask) for mask in (3 - first, jnp.full_like(first, 3), first, jnp.zeros_like(first))]
+        masks = (3 - first, jnp.full_like(first, 3), first, jnp.zeros_like(first))
+        return [parts(here ^ mask, kind) for mask, kind in zip(masks, (bf, bf, f32, f32))]
 
     def outer_hop(self, which, x):
         bit = (self.nq.bit_length() - 1) - 2
@@ -805,40 +842,81 @@
     half = WIN // 2
     pages, height = x.shape[:2]
     if bands > 1:
-        x = jnp.concatenate([x[:, :, half:], beside], axis=2)
+        x = jnp.concatenate([x[:, :, half:], beside.reshape(pages, height, half, D)], axis=2)
         route = [(f // bands * bands + (f + 1) % bands, f) for f in range(place.nf)]
         below = lax.ppermute(x[:, :half], "fsdp", route)
         return jnp.concatenate([x[:, half:], below], axis=1).reshape(-1, D)
 
-    def body(x_ref, b_ref, out_ref, tall_ref):
+    def body(x_ref, b_ref, out_ref, tall_ref, side_ref):
+        side_ref[...] = b_ref[...].astype(f32)
         for to in range(height):
             row = (to + half) % height
             tall_ref[to * WIN : to * WIN + half] = x_ref[0, row].astype(f32)[half:]
-            tall_ref[to * WIN + half : (to + 1) * WIN] = b_ref[0, row].astype(f32)
+            tall_ref[to * WIN + half : (to + 1) * WIN] = side_ref[row * half : (row + 1) * half]
         out_ref[...] = tall_ref[...].astype(bf)
 
     return call(
         body,
         "roll_in",
         sds((pages * height * WIN, D), bf),
-        [per_page((1, height, WIN, D), 0), per_page((1, height, half, D), 0)],
+        [per_page((1, height, WIN, D), 0), per_page((height * half, D), 0)],
         per_page((height * WIN, D), 0),
         (pages,),
         (x, beside),
-        scratch=(pltpu.VMEM((height * WIN, D), f32),),
+        scratch=(pltpu.VMEM((height * WIN, D), f32), pltpu.VMEM((height * half, D), f32)),
         flops=1 << 20,
     )
 
 
-def roll_out(x, place, bands):
+def last_columns(x):
     half = WIN // 2
-    beside = lax.ppermute(x[:, :, half:], "fsdp", [(f, (f + bands) % place.nf) for f in range(place.nf)])
-    x = jnp.concatenate([beside, x[:, :, :half]], axis=2)
-    above = x[:, -half:]
+    height = x.shape[0] // MICRO // WIN
+
+    def body(x_ref, out_ref, tall_ref, side_ref):
+        tall_ref[...] = x_ref[...].astype(f32)
+        for row in range(height):
+            side_ref[row * half : (row + 1) * half] = tall_ref[row * WIN + half : (row + 1) * WIN]
+        out_ref[...] = side_ref[...].astype(bf)
+
+    return call(
+        body,
+        "last_columns",
+        sds((MICRO * height * half, D), bf),
+        [per_page((height * WIN, D), 0)],
+        per_page((height * half, D), 0),
+        (MICRO,),
+        (x,),
+        (pltpu.VMEM((height * WIN, D), f32), pltpu.VMEM((height * half, D), f32)),
+    )
+
+
+def roll_out(x, beside, place, bands):
+    half = WIN // 2
+    height = x.shape[0] // MICRO // WIN
+    shape = (MICRO, height, WIN, D)
     if bands > 1:
-        route = [(f, f // bands * bands + (f + 1) % bands) for f in range(place.nf)]
-        above = lax.ppermute(above, "fsdp", route)
-    return jnp.concatenate([above, x[:, :-half]], axis=1)
+        x = jnp.concatenate([beside.reshape(MICRO, height, half, D), x.reshape(shape)[:, :, :half]], axis=2)
+        rows = [(f, f // bands * bands + (f + 1) % bands) for f in range(place.nf)]
+        above = lax.ppermute(x[:, -half:], "fsdp", rows)
+        return jnp.concatenate([above, x[:, :-half]], axis=1)
+
+    def body(x_ref, b_ref, out_ref, tall_ref, side_ref):
+        tall_ref[...] = x_ref[...].astype(f32)
+        side_ref[...] = b_ref[...].astype(f32)
+        for row in range(height):
+            parts = [side_ref[row * half : (row + 1) * half], tall_ref[row * WIN : row * WIN + half]]
+            out_ref[0, (row + half) % height] = jnp.concatenate(parts, axis=0).astype(bf)
+
+    return call(
+        body,
+        "roll_out",
+        sds(shape, bf),
+        [per_page((height * WIN, D), 0), per_page((height * half, D), 0)],
+        per_page((1,) + shape[1:], 0),
+        (MICRO,),
+        (x, beside),
+        (pltpu.VMEM((height * WIN, D), f32), pltpu.VMEM((height * half, D), f32)),
+    )
 
 
 def local(
@@ -914,7 +992,6 @@
             out.append(jnp.pad(rows_left, ((0, 0), (0, 6), (0, 0))))
         return out
 
-    ends = jnp.stack([query_slots, query_cot])
     positions = (slot_order[:, :, None] * Q_DEV + jnp.arange(Q_DEV, dtype=jnp.int32)).reshape(MICRO, slots)
     live = jnp.where(positions < lengths[:, None], 0.0, -1e30).astype(f32).reshape(MICRO, 1, slots)
     own_live = pick(live, core)
@@ -932,38 +1009,6 @@
     def all_dp(block, got):
         return jnp.stack([block] + list(got))
 
-    got, ends_two, beside_x = stage(
-        (place.send_line, one),
-        (place.sibling, pick(ends, 1 - core, 1)),
-        (partial(roll_beside, place=place, bands=bands), visual[:, :, : WIN // 2]),
-    )
-    all_one = all_dp(one, got)
-    ends = jnp.swapaxes(ordered(even, pick(ends, core, 1), ends_two), 0, 1).reshape(2, 2 * Q_DEV, D)
-    got, (f_one, s_one) = stage((place.send_line, two), (squares, all_one))
-    all_two = all_dp(two, got)
-    x = roll_in(visual, beside_x, place, bands)
-    c_one, sib_one, sib_f_one, sib_s_one, ends_two = stage(
-        (place.second_hop, f_one),
-        (place.sibling, all_one),
-        (place.sibling, f_one),
-        (place.sibling, s_one),
-        (partial(spread, bit=0), ends),
-    )
-    ends = spread_order(ends, ends_two, 0)
-    got, (f_two, s_two) = stage((place.send_line, three), (squares, all_two))
-    all_three = all_dp(three, got)
-    c_two, ends_two, sib_c_one, sib_two, beside_cot = stage(
-        (place.second_hop, f_two),
-        (partial(spread, bit=1), ends),
-        (place.sibling, c_one),
-        (place.sibling, all_two),
-        (partial(roll_beside, place=place, bands=bands), visual_cot[:, :, : WIN // 2]),
-    )
-    ends = spread_order(ends, ends_two, 1)
-    for bit in range(2, nq.bit_length() - 1):
-        ends = spread_order(ends, spread(ends, bit), bit)
-    xs, xs_cot = ends[0], ends[1]
-
     act_block = per_page((page_rows, D), 0)
     three_block = per_page((3, page_rows, D), 1)
 
@@ -971,7 +1016,7 @@
         return full, pl.BlockSpec((size, D, D), lambda *_: (index, 0, 0), pipeline_mode=pl.Buffered(1))
 
     def run_first(args):
-        sib_c, x, xs = args
+        sib_c, x = args
         w_one, gain_all = assemble(one, [all_one, f_one, s_one, c_one], [sib_one, sib_f_one, sib_s_one, sib_c], 8, 0)
         gain_all = gain_all[:, :2, : 6 * r].reshape(nz * nq * 2, 6, r)
         gain_all = jnp.transpose(gain_all, (1, 0, 2)).reshape(6, 1, D)
@@ -985,27 +1030,55 @@
             (x, bias, gain_all[0], w_one),
             flops=2 * rows * 4 * D * D,
         )
-        heard = simple(
+        return w_one, gain_all, windows
+
+    roll = partial(roll_beside, place=place, bands=bands)
+    ends = jnp.stack([query_slots, query_cot])
+    got, beside_x, ends_two = stage(
+        (place.send_line, one),
+        (roll, visual[:, :, : WIN // 2].reshape(-1, D)),
+        (place.sibling, pick(ends, 1 - core, 1)),
+    )
+    all_one = all_dp(one, got)
+    ends = jnp.swapaxes(ordered(even, pick(ends, core, 1), ends_two), 0, 1).reshape(2, 2 * Q_DEV, D)
+    got, (f_one, s_one) = stage((place.send_line, two), (squares, all_one))
+    c_one, ends_two, sib_one, sib_f_one, sib_s_one, x = stage(
+        (place.second_hop, f_one),
+        (partial(spread, bit=0), ends),
+        (place.sibling, all_one),
+        (place.sibling, f_one),
+        (place.sibling, s_one),
+        (lambda args: roll_in(*args, place, bands), (visual, beside_x)),
+    )
+    ends = spread_order(ends, ends_two, 0)
+    sib_c_one, ends_two, got = tie(place.sibling(c_one), spread(ends, 1), got)
+    ends = spread_order(ends, ends_two, 1)
+    for bit in range(2, nq.bit_length() - 1):
+        ends = spread_order(ends, spread(ends, bit), bit)
+    xs, xs_cot = ends[0], ends[1]
+    all_two = all_dp(two, got)
+    got, (f_two, s_two), first = stage(
+        (place.send_line, three), (squares, all_two), (run_first, (sib_c_one, x))
+    )
+    all_three = all_dp(three, got)
+    c_two, sib_two, sib_f_two, sib_s_two = stage(
+        (place.second_hop, f_two),
+        (place.sibling, all_two),
+        (place.sibling, f_two),
+        (place.sibling, s_two),
+    )
+    sib_c_two, all_three = tie(place.sibling(c_two), all_three)
+    w_one, gain_all, (mix, att, v1) = first
+    g_window, g_slots, g_reader, g_page, g_vmlp, g_qmlp = (gain_all[k] for k in range(6))
+
+    def run_second(args):
+        sib_c, v1, xs = args
+        mix_q, att_q, s1 = simple(
             slots_fwd,
             "slots_fwd",
-            (xs, gain_all[1], part_of(4, 1, w_one), own_live),
+            (xs, g_slots, part_of(4, 1, w_one), own_live),
             [((3, slots, D), bf), ((slots, D), bf), ((slots, D), f32)],
         )
-        return w_one, gain_all, windows, heard
-
-    (f_three, s_three), sib_f_two, sib_s_two, sib_c_two, first = stage(
-        (squares, all_three),
-        (place.sibling, f_two),
-        (place.sibling, s_two),
-        (place.sibling, c_two),
-        (run_first, (sib_c_one, x, xs)),
-    )
-    cot = roll_in(visual_cot, beside_cot, place, bands)
-    w_one, gain_all, (mix, att, v1), (mix_q, att_q, s1) = first
-    g_window, g_slots, g_reader, g_page, g_vmlp, g_qmlp = (gain_all[k] for k in range(6))
-
-    def run_second(args):
-        sib_c, v1, s1 = args
         (w_two,) = assemble(two, [all_two, f_two, s_two, c_two], [sib_two, sib_f_two, sib_s_two, sib_c], 7, 0)
         (rd_own,) = simple(
             normed_units, "slots_units", (s1, g_reader, part_of(3, 1, w_two)), [((3, slots, D), bf)]
@@ -1020,16 +1093,14 @@
             (v1, g_page, w_two),
             flops=2 * rows * 3 * D * D,
         )
-        return w_two, rd_own, pk
-
-    c_three, sib_three, sib_f_three, sib_s_three, (w_two, rd_own, pk) = stage(
-        (place.second_hop, f_three),
-        (place.sibling, all_three),
-        (place.sibling, f_three),
-        (place.sibling, s_three),
-        (run_second, (sib_c_two, v1, s1)),
-    )
-    rd_two, sib_c_three = stage((place.sibling, rd_own), (place.sibling, c_three))
+        return w_two, rd_own, pk, mix_q, att_q, s1
+
+    got, (f_three, s_three), (w_two, rd_own, pk, mix_q, att_q, s1) = stage(
+        (place.send_line, four), (squares, all_three), (run_second, (sib_c_two, v1, xs))
+    )
+    rd_two = place.sibling(rd_own)
+    rd_two, got = tie(rd_two, got)
+    all_four = all_dp(four, got)
     rd = jnp.swapaxes(ordered(even, rd_own, rd_two), 0, 1)
     rq, wk, wv = rd[0], rd[1], rd[2]
     slot_block = per_page((1, slots, D), 0)
@@ -1037,17 +1108,6 @@
 
     def of_pk(u):
         return pl.BlockSpec((1, page_rows, D), lambda p: (u, p, 0))
-
-    o_part, lse_part = call(
-        read_fwd,
-        "read_fwd",
-        (sds((MICRO, slots, D), f32), sds((MICRO, slots, 128), f32)),
-        [slot_block, of_pk(0), of_pk(1)],
-        (slot_block, stat_block),
-        (MICRO,),
-        (rq, pk, pk),
-        flops=2 * rows * slots * D * 4,
-    )
 
     def merge(terms):
         width = terms[0].shape[-1] // (HEAD + 1) * HEAD
@@ -1059,6 +1119,25 @@
         out = sum(t[..., :width] * jnp.repeat(share, HEAD, axis=-1) for t, share in zip(terms, shares))
         return jnp.concatenate([out, top + jnp.log(total)], axis=-1)
 
+    def run_read(args):
+        return call(
+            read_fwd,
+            "read_fwd",
+            (sds((MICRO, slots, D), f32), sds((MICRO, slots, 128), f32)),
+            [slot_block, of_pk(0), of_pk(1)],
+            (slot_block, stat_block),
+            (MICRO,),
+            args,
+            flops=2 * rows * slots * D * 4,
+        )
+
+    c_three, sib_three, sib_f_three, sib_s_three, (o_part, lse_part) = stage(
+        (place.second_hop, f_three),
+        (place.sibling, all_three),
+        (place.sibling, f_three),
+        (place.sibling, s_three),
+        (run_read, (rq, pk, pk)),
+    )
     terms = jnp.concatenate([o_part, lse_part[..., :HEADS]], axis=-1)
     live_block = per_page((1, 1, slots), 0)
 
@@ -1074,9 +1153,20 @@
             flops=2 * rows * D * D,
         )
 
-    terms_two, (writing, v2), (w_up, w_down) = stage(
+    terms_two, sib_c_three, beside_cot, (writing, v2) = stage(
         (place.sibling, pick(terms, 1 - core)),
+        (place.sibling, c_three),
+        (roll, visual_cot[:, :, : WIN // 2].reshape(-1, D)),
         (run_write, (v1, pk, wk, wv, live, w_two)),
+    )
+    terms = merge([pick(terms, core), terms_two])
+    blocks = jnp.concatenate(
+        [terms[:, :D].reshape(slots, GROUPS, GCOLS), terms[:, D:].reshape(slots, GROUPS, GHEADS)], axis=-1
+    )
+    blocks = jnp.swapaxes(blocks, 0, 1)
+    got, cot, (w_up, w_down) = stage(
+        (place.to_groups, blocks),
+        (lambda args: roll_in(*args, place, bands), (visual_cot, beside_cot)),
         (
             lambda sib_c: assemble(
                 three, [all_three, f_three, s_three, c_three], [sib_three, sib_f_three, sib_s_three, sib_c], 4, 1
@@ -1084,12 +1174,7 @@
             sib_c_three,
         ),
     )
-    terms = merge([pick(terms, core), terms_two])
-    blocks = jnp.concatenate(
-        [terms[:, :D].reshape(slots, GROUPS, GCOLS), terms[:, D:].reshape(slots, GROUPS, GHEADS)], axis=-1
-    )
-    blocks = jnp.swapaxes(blocks, 0, 1)
-    chunk = 384
+    chunk = D
     steps = 2 * D // chunk
     per_unit = D // chunk
 
@@ -1097,12 +1182,14 @@
         return pl.BlockSpec(shape, lambda j: (0,) * len(shape), pipeline_mode=pl.Buffered(1))
 
     smem = pl.BlockSpec(memory_space=pltpu.SMEM)
-    zq = nz * nq
     if fast:
-        up_shapes = [sds((zq, 2, r, D), bf)] * 2
-        up_outs = [pl.BlockSpec((zq, 1, r, chunk), lambda j: (0, j // per_unit, 0, j % per_unit))] * 2
-        down_shapes = [sds((zq // 2, 4 * r, D), bf)] * 2
-        down_outs = [pl.BlockSpec((chunk // (8 * r), 4 * r, D), lambda j: (j, 0, 0))] * 2
+        up_shapes = [sds((nq, nz, 2, r, D), bf)] * 2
+        up_outs = [pl.BlockSpec((nq, nz, 1, r, chunk), lambda j: (0, 0, j // per_unit, 0, j % per_unit))] * 2
+        several = chunk // (8 * r)
+        down_shapes = [sds((nq, nz // 2, 4 * r, D), bf)] * 2
+        down_outs = [
+            pl.BlockSpec((several, 1, 4 * r, D), lambda j: (j % (nq // several), j // (nq // several), 0, 0))
+        ] * 2
     else:
         up_shapes = [sds((2, D, D), bf)]
         up_outs = [pl.BlockSpec((1, D, chunk), lambda j: (j // per_unit, 0, j % per_unit))]
@@ -1135,17 +1222,17 @@
         )
         count = len(outs)
         if fast:
-            up = [y.reshape(nz, nq, 2, r, D) for y in out[count : count + 2]]
-            down = [y.reshape(nz // 2, nq, 4, r, D) for y in out[count + 2 :]]
+            up = out[count : count + 2]
+            down = [y.reshape(nq, nz // 2, 4, r, D) for y in out[count + 2 :]]
         else:
             up = place.halves(out[count], r)
             d = out[count + 1].reshape(nz // 2, nq, 2, 4, r, D)
-            down = [pick(d, which, 2) for which in (core, 1 - core)]
+            down = [jnp.swapaxes(pick(d, which, 2), 0, 1) for which in (core, 1 - core)]
         return tuple(out[:count]) + (list(up), list(down))
 
     def run_grads(body, name, shapes, specs, outs, args, units, scratch, flops):
         if fast:
-            unit_shapes = [sds((zq, units, r, D), bf)] * 2
+            unit_shapes = [sds((nq, nz, units, r, D), bf)] * 2
         else:
             unit_shapes = [sds((units, D, D), bf)]
         unit_outs = [whole(y.shape) for y in unit_shapes]
@@ -1162,23 +1249,25 @@
         )
         count = len(outs)
         if fast:
-            pair = [y.reshape(nz, nq, units, r, D) for y in out[count:]]
+            pair = list(out[count:])
         else:
             pair = list(place.halves(out[count], r))
         return tuple(out[:count]) + (pair,)
 
-    got = stage((place.to_groups, blocks))[0]
     reading = merge([pick(blocks, place.group)] + list(got))
     for bit in range(2, nq.bit_length() - 1):
         reading = merge([reading, place.hop(reading, 1 << bit)])
     message = jnp.concatenate([reading[:, :GCOLS].astype(bf)] + split_three(reading[:, GCOLS:]), axis=-1)
-    got, (y, dxn, up_one, down_one) = stage(
-        (place.send_line, four), (partial(run_mlp, False), (v2, g_vmlp, w_up, w_down, cot))
-    )
-    all_four = all_dp(four, got)
-    reads, (f_four, s_four), (v3, dv2, dg_vmlp, up_two, down_two) = stage(
+    reads, (f_four, s_four), (y, dxn, up_one, down_one) = stage(
         (place.group_hops, message),
         (squares, all_four),
+        (partial(run_mlp, False), (v2, g_vmlp, w_up, w_down, cot)),
+    )
+    c_four, sib_four, sib_f_four, sib_s_four, (v3, dv2, dg_vmlp, up_two, down_two) = stage(
+        (place.second_hop, f_four),
+        (place.sibling, all_four),
+        (place.sibling, f_four),
+        (place.sibling, s_four),
         (partial(run_mlp, True), (v2, g_vmlp, w_up, w_down, cot, y, dxn)),
     )
     reads = place.in_order([message] + list(reads))
@@ -1198,24 +1287,17 @@
             4 * rows * D * D,
         )
 
-    c_four, sib_four, sib_f_four, sib_s_four, (dwq, dwk, dwv, pair_wo) = stage(
-        (place.second_hop, f_four),
-        (place.sibling, all_four),
-        (place.sibling, f_four),
-        (place.sibling, s_four),
-        (run_write_bwd, (dv2, writing, pk, wk, wv, live, w_two)),
-    )
-    sib_c_four, *net_got = stage(
+    sib_c_four, *net_got, (dwq, dwk, dwv, pair_wo) = stage(
         (place.sibling, c_four),
         (place.sibling, up_one[1]),
         (place.sibling, up_two[1]),
         (place.sibling, down_one[1]),
         (place.sibling, down_two[1]),
-    )
-    keep_down = jnp.concatenate([down_one[0], down_two[0]])
-    down_got = jnp.concatenate([net_got[2], net_got[3]])
+        (run_write_bwd, (dv2, writing, pk, wk, wv, live, w_two)),
+    )
+    down_pairs = [(down_one[0], net_got[2]), (down_two[0], net_got[3])]
     second, corner, first, own_net = place.square_terms(
-        place.chip_terms([(up_one[0], net_got[0]), (up_two[0], net_got[1]), (keep_down, down_got)])
+        place.chip_terms([(up_one[0], net_got[0]), (up_two[0], net_got[1]), down_pairs])
     )
 
     def run_query(args):
@@ -1227,18 +1309,22 @@
         return simple(
             partial(query_mlp, 2 * r, D // nz),
             "query_mlp",
-            (chip_id, s1, read_q, part_of(1, 4, units), g_qmlp, (units, up_block), w_down, xs_cot),
-            [
-                ((slots, D), bf),
-                ((slots, D), f32),
-                ((slots, D), bf),
-                ((5, 2 * r * nz, D), bf),
-                ((8 * r * nz, D), bf),
-                ((1, D), f32),
-            ],
-        )
-
-    second, corner, (q_out, ds2, d_read, d_early, d_qdown, dg_qmlp) = stage(
+            (chip_id, core_id, s1, read_q, part_of(1, 4, units), g_qmlp, (units, up_block), w_down, xs_cot),
+            [((slots, D), bf), ((slots, D), f32), ((slots, D), bf), ((1, D), f32)]
+            + chip_shapes(5, r)
+            + chip_shapes(1, 4 * r),
+        )
+
+    def chip_shapes(k, r):
+        return [((nz, k, r, D), bf)] * 2 if fast else [((k, nz * 2 * r, D), bf)]
+
+    def chip_pair(outs, r):
+        if fast:
+            return list(outs)
+        x = outs[0].reshape(-1, nz, 2, r, D)
+        return [jnp.swapaxes(pick(x, which, 2), 0, 1) for which in (core, 1 - core)]
+
+    second, corner, (q_out, ds2, d_read, dg_qmlp, *d_early) = stage(
         (partial(place.outer_hop, 1), second.astype(bf)),
         (partial(place.outer_hop, 1), corner.astype(bf)),
         (run_query, (s1, read_q)),
@@ -1246,14 +1332,9 @@
     own_net = own_net + second.astype(f32)
     first = (first + corner.astype(f32)).astype(bf)
 
-    def chip_halves(x, r):
-        x = x.reshape(x.shape[0], nz, 2, r, D)
-        return [jnp.swapaxes(pick(x, which, 2), 0, 1) for which in (core, 1 - core)]
-
-    tall = [y.reshape(nz, 4, r, D) for y in chip_halves(d_qdown[None], 4 * r)]
-    keep_early, give_early = (
-        jnp.concatenate([a, b], axis=1) for a, b in zip(chip_halves(d_early, r), tall)
-    )
+    count = len(d_early) // 2
+    pairs = zip(chip_pair(d_early[:count], r), chip_pair(d_early[count:], 4 * r))
+    keep_early, give_early = (jnp.concatenate([a, b.reshape(nz, 4, r, D)], axis=1) for a, b in pairs)
     three_parts = jnp.concatenate([d_read, read_q, lse_page], axis=-1)
     parts_two, early_got = stage((place.sibling, three_parts), (place.sibling, give_early))
     three_parts = ordered(even, three_parts, parts_two)
@@ -1276,9 +1357,7 @@
             flops=2 * rows * slots * D * 10,
         )
 
-    first, (drq, dk, dv) = stage(
-        (partial(place.outer_hop, 0), first), (run_read_bwd, (rq, pk, pk, d_read_all, read_all, lse_all))
-    )
+    drq, dk, dv = run_read_bwd((rq, pk, pk, d_read_all, read_all, lse_all))
 
     def run_page_bwd(args):
         return run_grads(
@@ -1294,11 +1373,13 @@
         )
 
     d_slots = jnp.stack([drq, dwk, dwv], axis=1)
+    slots_two, first, (dv1, dg_page, pair_page) = stage(
+        (place.sibling, pick(d_slots, 1 - core)),
+        (partial(place.outer_hop, 0), first),
+        (run_page_bwd, (v1, dv2, dk, dv, dwq, g_page, w_two)),
+    )
     own_net = place.inner_square((own_net + first.astype(f32)).astype(bf))
     net_sum = lax.psum_scatter(own_net.reshape(nz, 8 * r, D), "dp", scatter_dimension=0).reshape(8, r, D)
-    slots_two, (dv1, dg_page, pair_page) = stage(
-        (place.sibling, pick(d_slots, 1 - core)), (run_page_bwd, (v1, dv2, dk, dv, dwq, g_page, w_two))
-    )
     d_slots = (pick(d_slots, core).astype(f32) + slots_two.astype(f32)).astype(bf)
     d_slots = jnp.transpose(d_slots.reshape(3, slots, GROUPS, GCOLS), (2, 0, 1, 3))
 
@@ -1344,8 +1425,8 @@
         return simple(
             partial(query_back, 2 * r, D // nz),
             "query_back",
-            (*args[:6], part_of(3, 1, args[6]), part_of(4, 1, args[7]), *args[8:]),
-            [((slots, D), bf), ((7, 2 * r * nz, D), bf), ((1, D), f32), ((1, D), f32)],
+            (*args[:7], part_of(3, 1, args[7]), part_of(4, 1, args[8]), *args[9:]),
+            [((slots, D), bf), ((1, D), f32), ((1, D), f32)] + chip_shapes(7, r),
             scratch=(pltpu.VMEM((3, slots, D), bf),),
         )
 
@@ -1365,19 +1446,22 @@
     first, (pair_window,) = stage(
         (partial(place.outer_hop, 0), first), (run_window_grads, (dv1, x, dmix, att, g_window))
     )
+    pair_window, net_sum, early_sum = tie(pair_window, net_sum, early_sum)
     own_page = place.inner_square((own_page + first.astype(f32)).astype(bf))
-    page_sum = lax.psum_scatter(own_page.reshape(nz, 4 * r, D), "dp", scatter_dimension=0).reshape(4, r, D)
-    window_got, (x_grad, d_late, dg_slots, dg_reader) = stage(
-        (place.sibling, pair_window[1]),
+    (window_got,) = stage((place.sibling, pair_window[1]))
+    second, corner, first, own_window = place.square_terms(place.chip_terms([(pair_window[0], window_got)]))
+    second, corner, page_passed, (x_grad, dg_slots, dg_reader, *d_late) = stage(
+        (partial(place.outer_hop, 1), second.astype(bf)),
+        (partial(place.outer_hop, 1), corner.astype(bf)),
+        (place.send_terms, own_page),
         (
             run_query_back,
-            (chip_id, xs, s1, ds2, d_rd, g_reader, w_two, w_one, mix_q, att_q, own_live, g_slots),
+            (chip_id, core_id, xs, s1, ds2, d_rd, g_reader, w_two, w_one, mix_q, att_q, own_live, g_slots),
         ),
     )
-    keep_late, give_late = chip_halves(d_late, r)
-    second, corner, first, own_window = place.square_terms(place.chip_terms([(pair_window[0], window_got)]))
-    second, late_got = tie(second.astype(bf), place.sibling(give_late))
-    late = (keep_late.astype(f32) + late_got.astype(f32)).astype(bf)
+    own_window = own_window + second.astype(f32)
+    first = (first + corner.astype(f32)).astype(bf)
+    keep_late, give_late = chip_pair(d_late, r)
 
     def run_window_end(args):
         return call(
@@ -1392,38 +1476,54 @@
             flops=2 * rows * 3 * D * D,
         )
 
-    second, corner, late_passed, (v_grad, dg_window) = stage(
-        (partial(place.outer_hop, 1), second),
-        (partial(place.outer_hop, 1), corner.astype(bf)),
-        (place.send_terms, late),
-        (run_window_end, (dv1, x, dmix, g_window, w_one)),
-    )
-    own_window = own_window + second.astype(f32)
-    first = (first + corner.astype(f32)).astype(bf)
-    late_sum = place.own_terms(late) + sum(y.astype(f32) for y in late_passed)
+    def run_ends(args):
+        v3, *rest = args
+        v_grad, dg_window = run_window_end(rest)
+        return v_grad, dg_window, last_columns(v3), last_columns(v_grad)
+
+    first, late_got, (v_grad, dg_window, side_out, side_grad) = stage(
+        (partial(place.outer_hop, 0), first),
+        (place.sibling, give_late),
+        (run_ends, (v3, dv1, x, dmix, g_window, w_one)),
+    )
+    own_window = place.inner_square((own_window + first.astype(f32)).astype(bf))
+    late = (keep_late.astype(f32) + late_got.astype(f32)).astype(bf)
+    last = jnp.concatenate([own_window, late], axis=1)
+
+    def right(x):
+        return lax.ppermute(x, "fsdp", [(f, (f + bands) % nf) for f in range(nf)])
+
     own_gains = jnp.concatenate([dg_window, dg_page, dg_vmlp])
     query_gains = jnp.concatenate([dg_slots, dg_reader, dg_qmlp])
-    first, chip_gains = stage(
-        (partial(place.outer_hop, 0), first),
-        (lambda x: [place.hop(x, mask) for mask in range(1, nq)], own_gains),
-    )
-    own_window = place.inner_square((own_window + first.astype(f32)).astype(bf))
+    (chip_gains,) = stage((lambda x: [place.hop(x, mask) for mask in range(1, nq)], own_gains))
     gain_rows = jnp.concatenate([own_gains + sum(chip_gains), query_gains]).reshape(6, nz, nq, 2, r)
     gain_rows = pick(gain_rows, place.chip, 2)
-    gain_rows = pick(gain_rows, core, 2) + place.sibling(pick(gain_rows, 1 - core, 2))
-    gain_rows = jnp.swapaxes(gain_rows, 0, 1).reshape(nz, 1, 1, 6 * r).astype(bf)
-    gain_rows = jnp.pad(gain_rows, ((0, 0), (0, 0), (0, r - 1), (0, D - 6 * r)))
-    own_window = jnp.concatenate([own_window, gain_rows], axis=1)
-    window_passed = place.send_terms(own_window)
-    grad_win = place.own_terms(own_window) + sum(y.astype(f32) for y in window_passed)
-    both = grad_win[4, 0, : 6 * r].reshape(6, r)
-
-    visual_out = roll_out(v3.reshape(MICRO, height, WIN, D), place, bands)
-    visual_grad = roll_out(v_grad.reshape(MICRO, height, WIN, D), place, bands)
+    last_terms = [pick(last, place.z ^ m) for m in range(1, nz)]
+    count = max(nz // 2, 1)
+    passed_one, side_out, side_grad, gains_two = stage(
+        (lambda xs: [place.across(x, m + 1) for m, x in enumerate(xs)], last_terms[:count]),
+        (right, side_out),
+        (right, side_grad),
+        (place.sibling, pick(gain_rows, 1 - core, 2)),
+    )
+    gain_rows = jnp.swapaxes(pick(gain_rows, core, 2) + gains_two, 0, 1)
+    passed_two, gains_passed, visual_out, visual_grad = stage(
+        (lambda xs: [place.across(x, m + 1 + count) for m, x in enumerate(xs)], last_terms[count:]),
+        (place.send_terms, gain_rows),
+        (lambda args: roll_out(*args, place, bands), (v3, side_out)),
+        (lambda args: roll_out(*args, place, bands), (v_grad, side_grad)),
+    )
+    last_sum = place.own_terms(last) + sum(y.astype(f32) for y in list(passed_one) + list(passed_two))
+    grad_win, late_sum = last_sum[:4], last_sum[4:]
+    both = place.own_terms(gain_rows) + sum(gains_passed)
+    q_out, x_grad, net_sum, early_sum, own_page, page_passed, _ = tie(
+        q_out, x_grad, net_sum, early_sum, own_page, page_passed, passed_one
+    )
+    grad_page = place.own_terms(own_page) + sum(y.astype(f32) for y in page_passed)
+
     query_out = place.owned_rows(q_out)
     query_grad = place.owned_rows(x_grad)
 
-    grad_page = page_sum.astype(f32)
     grad_up = net_sum[:4].astype(f32)
     grad_down = net_sum[4:].reshape(4 * r, D).astype(f32)
     grad_qup = jnp.concatenate([early_sum[k] for k in range(4)], axis=1)

time: 668 us -> 591 us (0.88)
  waiting for transfers between devices: 145 us -> 117 us
  local copies, waits for them, and re-layouts: 72.8 us -> 49.6 us
  Pallas kernels: 262 us -> 250 us
    ppermute x18 -> x21, waiting for transfers between devices: 89.3 us -> 59.1 us  [across(): return lax.ppermute(x, 'dp', [(z, z ^ mask) for z in range(self.nz)])]
    ppermute x38, starting transfers between devices: 48.9 us -> 39.2 us  [hop(): return lax.ppermute(x, 'fsdp', route)]
    ppermute x38, waiting for transfers between devices: 40.3 us -> 49.6 us  [hop(): return lax.ppermute(x, 'fsdp', route)]
    optimization_barrier x8 -> x4, local copies, waits for them, and re-layouts: 13 us -> 5.77 us  [tie(): return lax.optimization_barrier(arrays)]
    pallas_call x18 -> x22, Pallas kernels: 198 us -> 191 us  [call(): pl.pallas_call(body, name=name, out_shape=out_shape, grid=grid, in_specs=...]
    unnamed x174 -> x175, local copies, waits for them, and re-layouts: 22.8 us -> 18.2 us
    ppermute x18 -> x21, starting transfers between devices: 41.9 us -> 45.7 us  [across(): return lax.ppermute(x, 'dp', [(z, z ^ mask) for z in range(self.nz)])]
  transfers between devices with their start and end apart: 96 -> 98, of which waited for: 26 -> 20; matrix products, arithmetic and copies ran while one was open for 14% -> 9% of each run, Pallas kernels for 38% -> 41%
where the time goes in v2:
time: 591 us; the launch traced here: 587 us
  Pallas kernels  250 us (42%)
  waiting for transfers between devices  117 us (20%)
  starting transfers between devices  98.4 us (17%)
  other arithmetic  56.7 us (10%)
  local copies, waits for them, and re-layouts  49.6 us (8%)
  between operations  16.2 us (3%)
    pallas_call x22, Pallas kernels, call(): pl.pallas_call(body, name=name, out_shape=out_shape, grid=grid, in_specs=...  191 us
    ppermute x21, waiting for transfers between devices, across(): return lax.ppermute(x, 'dp', [(z, z ^ mask) for z in range(self.nz)])  59.1 us
    ppermute x38, waiting for transfers between devices, hop(): return lax.ppermute(x, 'fsdp', route)  49.6 us
    ppermute x21, starting transfers between devices, across(): return lax.ppermute(x, 'dp', [(z, z ^ mask) for z in range(self.nz)])  45.7 us
    ppermute x38, starting transfers between devices, hop(): return lax.ppermute(x, 'fsdp', route)  39.2 us
    pallas_call x4, Pallas kernels, place_units(): pl.pallas_call(body, name='place_units', grid=(nz,), out_shape=tuple(shap...  35.2 us
    pallas_call x2, Pallas kernels, run_window_bwd(): pl.pallas_call(window_bwd, name='window_bwd', out_shape=sds((3, rows, D),...  23 us
    unnamed x175, local copies, waits for them, and re-layouts  18.2 us
  transfers between devices with their start and end apart: 98, of which 20 were waited for; matrix products, arithmetic and copies ran while one was open for 9% of the time, Pallas kernels for 41%

profile of v2, /device:TPU:0, one launch (start us, length us, event | category | flops | bytes accessed | tf_op | source)
XLA Modules:
  0.0 587.1 jit_solution(16482126626608608570)
XLA Ops:
  20.7 8.5 %collective-permute-done = bf16[9,24,768]{2,1,0:T(8,128)(2,1)S(1)} collective-permute-done((bf16[9,24,768]{2,1,0:T(8,128)(2,1)}, bf16[9,24,768]{2,1,0:T(8,128)(2,1)S(1)}, u32[]{:S(2)}, u32[]{:S(2)}) %collective-permute-start) | collective-permute-done | bytes 331808 | tf_op jit(solution)/shard_map/ppermute | solution.py:692
  29.2 13.5 %collective-permute-done.1 = bf16[9,24,768]{2,1,0:T(8,128)(2,1)S(1)} collective-permute-done((bf16[9,24,768]{2,1,0:T(8,128)(2,1)}, bf16[9,24,768]{2,1,0:T(8,128)(2,1)S(1)}, u32[]{:S(2)}, u32[]{:S(2)}) %collective-permute-start.1) | collective-permute-done | bytes 331808 | tf_op jit(solution)/shard_map/ppermute | solution.py:692
  61.8 11.8 %collective-permute-done.6 = bf16[7,24,768]{2,1,0:T(8,128)(2,1)S(1)} collective-permute-done((bf16[7,24,768]{2,1,0:T(8,128)(2,1)}, bf16[7,24,768]{2,1,0:T(8,128)(2,1)S(1)}, u32[]{:S(2)}, u32[]{:S(2)}) %collective-permute-start.6) | collective-permute-done | bytes 258080 | tf_op jit(solution)/shard_map/ppermute | solution.py:692
  80.6 11.2 %collective-permute-done.10.args_3_ = bf16[4,9,24,768]{3,2,1,0:T(8,128)(2,1)} collective-permute-done((bf16[4,9,24,768]{3,2,1,0:T(8,128)(2,1)}, bf16[4,9,24,768]{3,2,1,0:T(8,128)(2,1)}, u32[]{:S(2)}, u32[]{:S(2)}) %collective-permute-start.10) | collective-permute-done | bytes 1327136 | tf_op jit(solution)/shard_map/ppermute | solution.py:689
  108.1 7.6 %collective-permute-start.17 = (bf16[8,24,768]{2,1,0:T(8,128)(2,1)}, bf16[8,24,768]{2,1,0:T(8,128)(2,1)}, u32[]{:S(2)}, u32[]{:S(2)}) collective-permute-start(bf16[8,24,768]{2,1,0:T(8,128)(2,1)} %get-tuple-element.453), channel_id=1, source_target_pairs={{0,8},{8,0},{16,24},{24,16},{1,9},{9,1},{17,25},{25,17},{2,10},{10... | collective-permute-start | bytes 884744 | tf_op jit(solution)/shard_map/ppermute | solution.py:692
  118.1 8.9 %place_units.4 = (bf16[8,16,48,768]{3,2,1,0:T(8,128)(2,1)}, f32[16,8,768]{2,1,0:T(8,128)}) custom-call(s32[3]{0:T(128)} %pad_add_fusion.table_ref, bf16[4,9,24,768]{3,2,1,0:T(8,128)(2,1)} %copy-done.3, bf16[4,9,24,768]{3,2,1,0:T(8,128)(2,1)} %collective-permute-done.8.args_1_, bf16[4,9,24,768]{3,2,1,0:T(8,128)(2,1)} %collective-permute-done.9.args_2_, ...), custom_call_target="tpu_custom_call" | custom-call | bytes 21233664 | tf_op jit(solution)/shard_map/place_units/pallas_call | solution.py:645
  129.5 15.3 %window_fwd.1 = (bf16[3,864,768]{2,1,0:T(8,128)(2,1)}, bf16[864,768]{1,0:T(8,128)(2,1)}, f32[864,768]{1,0:T(8,128)}) custom-call(bf16[864,768]{1,0:T(8,128)(2,1)} %roll_in.2.x_ref, f32[3,144,144]{2,1,0:T(8,128)} %compare_select_fusion.bias_ref, f32[1,768]{1,0:T(1,128)} %squeeze.289.gw_ref, bf16[8,768,768]{2,1,0:T(8,128)(2,1)} %bitcast.388), custom_call_target="tpu_custom_call" | custom-call | flops 4076863488 | bytes 1048576 | tf_op jit(solution)/shard_map/window_fwd/pallas_call | solution.py:123
  147.1 12.5 %collective-permute-done.22.args_3_ = bf16[4,7,24,768]{3,2,1,0:T(8,128)(2,1)} collective-permute-done((bf16[4,7,24,768]{3,2,1,0:T(8,128)(2,1)S(1)}, bf16[4,7,24,768]{3,2,1,0:T(8,128)(2,1)}, u32[]{:S(2)}, u32[]{:S(2)}) %collective-permute-start.22) | collective-permute-done | bytes 1032224 | tf_op jit(solution)/shard_map/ppermute | solution.py:689
  173.6 7.8 %place_units.5 = bf16[7,16,48,768]{3,2,1,0:T(8,128)(2,1)} custom-call(s32[3]{0:T(128)} %pad_add_fusion.table_ref, bf16[4,7,24,768]{3,2,1,0:T(8,128)(2,1)} %copy-done.5, bf16[4,7,24,768]{3,2,1,0:T(8,128)(2,1)} %copy-done.28, bf16[4,7,24,768]{3,2,1,0:T(8,128)(2,1)} %collective-permute-done.21.args_2_, bf16[4,7,24,768]{3,2,1,0:T(8,128)(2,1)} %collective-permute-done.22.args_3_, ...), custom_call_target="tpu_custom_call" | custom-call | bytes 16515072 | tf_op jit(solution)/shard_map/place_units/pallas_call | solution.py:645
  190.0 7.7 %page_units.1.k_ref.v_ref.wq_ref = bf16[3,864,768]{2,1,0:T(8,128)(2,1)} custom-call(f32[864,768]{1,0:T(8,128)} %get-tuple-element.650.x_ref.v1_ref, f32[1,768]{1,0:T(1,128)} %get-tuple-element.655.g_ref.gp_ref, bf16[7,768,768]{2,1,0:T(8,128)(2,1)} %bitcast.383), custom_call_target="tpu_custom_call" | custom-call | flops 3057647616 | bytes 1048576 | tf_op jit(solution)/shard_map/page_units/pallas_call | solution.py:123
  222.9 8.4 %write_fwd.1 = (bf16[864,768]{1,0:T(8,128)(2,1)}, f32[864,768]{1,0:T(8,128)}) custom-call(f32[864,768]{1,0:T(8,128)} %get-tuple-element.650.x_ref.v1_ref, bf16[3,864,768]{2,1,0:T(8,128)(2,1)} %page_units.1.k_ref.v_ref.wq_ref, bf16[2,128,768]{2,1,0:T(8,128)(2,1)} %get-tuple-element.597.wk_ref, bf16[2,128,768]{2,1,0:T(8,128)(2,1)} %get-tuple-element.598.wv_ref, ...), custom_call_target="tpu_custom_call" | custom-call | flops 1019215872 | bytes 1048576 | tf_op jit(solution)/shard_map/write_fwd/pallas_call | solution.py:123
  240.6 8.7 %place_units.6 = (bf16[4,16,48,768]{3,2,1,0:T(8,128)(2,1)}, bf16[16,192,768]{2,1,0:T(8,128)(2,1)}) custom-call(s32[3]{0:T(128)} %pad_add_fusion.table_ref, bf16[4,8,24,768]{3,2,1,0:T(8,128)(2,1)} %copy-done.4, bf16[4,8,24,768]{3,2,1,0:T(8,128)(2,1)} %collective-permute-done.30.args_1_, bf16[4,8,24,768]{3,2,1,0:T(8,128)(2,1)} %collective-permute-done.31.args_2_, ...), custom_call_target="tpu_custom_call" | custom-call | bytes 18874368 | tf_op jit(solution)/shard_map/place_units/pallas_call | solution.py:645
  254.8 22.5 %mlp_both.2 = (f32[864,768]{1,0:T(8,128)}, f32[864,768]{1,0:T(8,128)}, bf16[4,4,2,24,768]{4,3,2,1,0:T(8,128)(2,1)}, bf16[4,4,2,24,768]{4,3,2,1,0:T(8,128)(2,1)},...) custom-call(s32[1]{0:T(128)} %bitcast.26.core_ref, f32[864,768]{1,0:T(8,128)} %get-tuple-element.568.x_ref, ...), custom_call_target="tpu_custom_call" | custom-call | flops 12230590464 | bytes 1048576 | tf_op jit(solution)/shard_map/mlp_both/pallas_call | solution.py:123
  285.8 25.6 %mlp_both.3 = (bf16[864,768]{1,0:T(8,128)(2,1)}, f32[864,768]{1,0:T(8,128)}, f32[1,768]{1,0:T(1,128)}, bf16[4,4,2,24,768]{4,3,2,1,0:T(8,128)(2,1)}, bf16[4,4,2,2...) custom-call(s32[1]{0:T(128)} %bitcast.26.core_ref, ...), custom_call_target="tpu_custom_call" | custom-call | flops 12230590464 | bytes 1048576 | tf_op jit(solution)/shard_map/mlp_both/pallas_call | solution.py:123
  314.5 13.2 %write_bwd.1 = (bf16[864,768]{1,0:T(8,128)(2,1)}, bf16[2,128,768]{2,1,0:T(8,128)(2,1)}, bf16[2,128,768]{2,1,0:T(8,128)(2,1)}, bf16[4,4,1,24,768]{4,3,2,1,0:T(8,128)(2,1)}, bf16[4,4,1,24,768]{4,3,2,1,0:T(8,128)(2,1)}) custom-call(s32[1]{0:T(128)} %bitcast.26.core_ref, f32[864,768]{1,0:T(8,128)} %get-tuple-element.651.dv2_ref, ...), custom_call_target="tpu_custom_call" | custom-call | flops 2038431744 | bytes 1048576 | tf_op jit(solution)/shard_map/write_bwd/pallas_call | solution.py:123
  345.3 9.8 %place_units.7 = (bf16[5,16,48,768]{3,2,1,0:T(8,128)(2,1)}, bf16[16,192,768]{2,1,0:T(8,128)(2,1)}) custom-call(s32[3]{0:T(128)} %pad_add_fusion.table_ref, bf16[4,9,24,768]{3,2,1,0:T(8,128)(2,1)} %copy-done.2, bf16[4,9,24,768]{3,2,1,0:T(8,128)(2,1)} %copy-done.18, bf16[4,9,24,768]{3,2,1,0:T(8,128)(2,1)} %copy-done.19, bf16[4,9,24,768]{3,2,1,0:T(8,128)(2,1)} %copy-done.20, ...), custom_call_target="tpu_custom_call" | custom-call | bytes 21233664 | tf_op jit(solution)/shard_map/place_units/pallas_call | solution.py:645
  355.1 13.1 %query_mlp.1 = (bf16[128,768]{1,0:T(8,128)(2,1)}, f32[128,768]{1,0:T(8,128)}, bf16[128,768]{1,0:T(8,128)(2,1)}, f32[1,768]{1,0:T(1,128)}, bf16[4,5,24,768]{3,2,1...) custom-call(s32[1]{0:T(128)} %bitcast.98.chip_ref, ...), custom_call_target="tpu_custom_call" | custom-call | flops 1073741824 | bytes 1048576 | tf_op jit(solution)/shard_map/query_mlp/pallas_call | solution.py:123
  388.3 15.3 %page_bwd.1 = (f32[864,768]{1,0:T(8,128)}, f32[1,768]{1,0:T(1,128)}, bf16[4,4,3,24,768]{4,3,2,1,0:T(8,128)(2,1)}, bf16[4,4,3,24,768]{4,3,2,1,0:T(8,128)(2,1)}) custom-call(s32[1]{0:T(128)} %bitcast.26.core_ref, f32[864,768]{1,0:T(8,128)} %get-tuple-element.650.x_ref.v1_ref, f32[864,768]{1,0:T(8,128)} %get-tuple-element.651.dv2_ref, ...), custom_call_target="tpu_custom_call" | custom-call | flops 6115295232 | bytes 1048576 | tf_op jit(solution)/shard_map/page_bwd/pallas_call | solution.py:123
  413.9 11.4 %window_bwd.2.refs_0_ = bf16[3,864,768]{2,1,0:T(8,128)(2,1)} custom-call(f32[864,768]{1,0:T(8,128)} %get-tuple-element.746.dv1_ref, bf16[3,864,768]{2,1,0:T(8,128)(2,1)} %get-tuple-element.687.mix_ref, bf16[864,768]{1,0:T(8,128)(2,1)} %get-tuple-element.698.att_ref, f32[3,144,144]{2,1,0:T(8,128)} %compare_select_fusion.bias_ref, bf16[8,768,768]{2,1,0:T(8,128)(2,1)} %bitcast.390), custom_call_target="tpu_custom_call" | custom-call | flops 1019215872 | bytes 1048576 | tf_op jit(solution)/shard_map/window_bwd/pallas_call | solution.py:1389
  435.6 11.6 %window_bwd.3.dmix_ref = bf16[3,864,768]{2,1,0:T(8,128)(2,1)} custom-call(f32[864,768]{1,0:T(8,128)} %get-tuple-element.746.dv1_ref, bf16[3,864,768]{2,1,0:T(8,128)(2,1)} %get-tuple-element.687.mix_ref, bf16[864,768]{1,0:T(8,128)(2,1)} %get-tuple-element.698.att_ref, f32[3,144,144]{2,1,0:T(8,128)} %compare_select_fusion.bias_ref, ...), custom_call_target="tpu_custom_call", output_to_operand_aliasing={{}: (5, {})} | custom-call | flops 1019215872 | bytes 1048576 | tf_op jit(solution)/shard_map/window_bwd/pallas_call | solution.py:1389
  456.1 11.6 %window_grads.1 = (bf16[4,4,4,24,768]{4,3,2,1,0:T(8,128)(2,1)}, bf16[4,4,4,24,768]{4,3,2,1,0:T(8,128)(2,1)}) custom-call(s32[1]{0:T(128)} %bitcast.26.core_ref, f32[864,768]{1,0:T(8,128)} %get-tuple-element.746.dv1_ref, bf16[864,768]{1,0:T(8,128)(2,1)} %roll_in.2.x_ref, bf16[3,864,768]{2,1,0:T(8,128)(2,1)} %window_bwd.3.dmix_ref, ...), custom_call_target="tpu_custom_call" | custom-call | flops 4076863488 | bytes 1048576 | tf_op jit(solution)/shard_map/window_grads/pallas_call | solution.py:123
  485.9 10.1 %query_back.1 = (bf16[128,768]{1,0:T(8,128)(2,1)}, f32[1,768]{1,0:T(1,128)}, f32[1,768]{1,0:T(1,128)}, bf16[4,7,24,768]{3,2,1,0:T(8,128)(2,1)}, bf16[4,7,24,768]{3,2,1,0:T(8,128)(2,1)}) custom-call(s32[1]{0:T(128)} %bitcast.98.chip_ref, s32[1]{0:T(128)} %bitcast.26.core_ref, bf16[128,768]{1,0:T(8,128)(2,1)} %get-tuple-element.724.x_ref, ...), custom_call_target="tpu_custom_call" | custom-call | flops 1073741824 | bytes 1048576 | tf_op jit(solution)/shard_map/query_back/pallas_call | solution.py:123
  499.3 9.0 %window_end.1 = (bf16[864,768]{1,0:T(8,128)(2,1)}, f32[1,768]{1,0:T(1,128)}) custom-call(f32[864,768]{1,0:T(8,128)} %get-tuple-element.746.dv1_ref, bf16[864,768]{1,0:T(8,128)(2,1)} %roll_in.2.x_ref, bf16[3,864,768]{2,1,0:T(8,128)(2,1)} %window_bwd.3.dmix_ref, f32[1,768]{1,0:T(1,128)} %get-tuple-element.749.gw_ref, bf16[8,768,768]{2,1,0:T(8,128)(2,1)} %bitcast.393), custom_call_target="tpu_custom_call" | custom-call | flops 3057647616 | bytes 1048576 | tf_op jit(solution)/shard_map/window_end/pallas_call | solution.py:123
  528.0 15.9 %collective-permute-done.85 = bf16[11,24,768]{2,1,0:T(8,128)(2,1)} collective-permute-done((bf16[11,24,768]{2,1,0:T(8,128)(2,1)}, bf16[11,24,768]{2,1,0:T(8,128)(2,1)}, u32[]{:S(2)}, u32[]{:S(2)}) %collective-permute-start.85) | collective-permute-done | bytes 405536 | tf_op jit(solution)/shard_map/ppermute | solution.py:692
  (529 shorter events, 279.8 us)
Async XLA Ops:
  7.2 447.9 %reduce-scatter.5.cloned.1.call-start = ((), (), s32[]{:S(2)}) async-start(), calls=%async_computation.3 | async-start | bytes 1658880 | tf_op jit(solution)/shard_map/reduce_scatter | solution.py:1345
  11.8 31.0 %collective-permute-start.3 = (bf16[432,768]{1,0:T(8,128)(2,1)S(1)}, bf16[432,768]{1,0:T(8,128)(2,1)S(1)}, u32[]{:S(2)}, u32[]{:S(2)}) collective-permute-start(bf16[432,768]{1,0:T(8,128)(2,1)S(1)} %reshape.592), channel_id=1, source_target_pairs={{1,0},{2,1},{3,2},{4,3},{5,4},{6,5},{7,6},{0,7},{9,8},{10,9},{11,1... | collective-permute-start | bytes 1990664 | tf_op jit(solution)/shard_map/ppermute | solution.py:838
  44.2 29.5 %collective-permute-start.8 = (bf16[4,9,24,768]{3,2,1,0:T(8,128)(2,1)S(1)}, bf16[4,9,24,768]{3,2,1,0:T(8,128)(2,1)}, u32[]{:S(2)}, u32[]{:S(2)}) collective-permute-start(bf16[4,9,24,768]{3,2,1,0:T(8,128)(2,1)S(1)} %pad_maximum_fusion.args_0_), channel_id=1, source_target_pairs={{0,2},{1,5},{2,0},{3,7},{4,6},{5,1},{6,4},{7,3},{8,10},{9,13},{10,... | collective-permute-start | bytes 3981320 | tf_op jit(solution)/shard_map/ppermute | solution.py:689
  44.3 29.4 %collective-permute-start.9 = (bf16[4,9,24,768]{3,2,1,0:T(8,128)(2,1)S(1)}, bf16[4,9,24,768]{3,2,1,0:T(8,128)(2,1)}, u32[]{:S(2)}, u32[]{:S(2)}) collective-permute-start(bf16[4,9,24,768]{3,2,1,0:T(8,128)(2,1)S(1)} %pad_maximum_fusion.args_0_), channel_id=1, source_target_pairs={{0,4},{1,3},{2,6},{3,1},{4,0},{5,7},{6,2},{7,5},{8,12},{9,11},{10,... | collective-permute-start | bytes 3981320 | tf_op jit(solution)/shard_map/ppermute | solution.py:689
  104.7 40.0 %collective-permute-start.20 = (bf16[4,7,24,768]{3,2,1,0:T(8,128)(2,1)S(1)}, bf16[4,7,24,768]{3,2,1,0:T(8,128)(2,1)S(1)}, u32[]{:S(2)}, u32[]{:S(2)}) collective-permute-start(bf16[4,7,24,768]{3,2,1,0:T(8,128)(2,1)S(1)} %pad_maximum_fusion.5.args_0_), channel_id=1, source_target_pairs={{0,2},{1,5},{2,0},{3,7},{4,6},{5,1},{6,4},{7,3},{8,10},{9,13},{10,... | collective-permute-start | bytes 3096584 | tf_op jit(solution)/shard_map/ppermute | solution.py:689
  106.1 38.7 %collective-permute-start.21 = (bf16[4,7,24,768]{3,2,1,0:T(8,128)(2,1)S(1)}, bf16[4,7,24,768]{3,2,1,0:T(8,128)(2,1)}, u32[]{:S(2)}, u32[]{:S(2)}) collective-permute-start(bf16[4,7,24,768]{3,2,1,0:T(8,128)(2,1)S(1)} %pad_maximum_fusion.5.args_0_), channel_id=1, source_target_pairs={{0,4},{1,3},{2,6},{3,1},{4,0},{5,7},{6,2},{7,5},{8,12},{9,11},{10,... | collective-permute-start | bytes 3096584 | tf_op jit(solution)/shard_map/ppermute | solution.py:689
  108.1 36.7 %collective-permute-start.17 = (bf16[8,24,768]{2,1,0:T(8,128)(2,1)}, bf16[8,24,768]{2,1,0:T(8,128)(2,1)}, u32[]{:S(2)}, u32[]{:S(2)}) collective-permute-start(bf16[8,24,768]{2,1,0:T(8,128)(2,1)} %get-tuple-element.453), channel_id=1, source_target_pairs={{0,8},{8,0},{16,24},{24,16},{1,9},{9,1},{17,25},{25,17},{2,10},{10... | collective-permute-start | bytes 884744 | tf_op jit(solution)/shard_map/ppermute | solution.py:692
  115.7 29.1 %collective-permute-start.18 = (bf16[8,24,768]{2,1,0:T(8,128)(2,1)}, bf16[8,24,768]{2,1,0:T(8,128)(2,1)}, u32[]{:S(2)}, u32[]{:S(2)}) collective-permute-start(bf16[8,24,768]{2,1,0:T(8,128)(2,1)} %get-tuple-element.453), channel_id=1, source_target_pairs={{0,16},{8,24},{16,0},{24,8},{1,17},{9,25},{17,1},{25,9},{2,18},{10... | collective-permute-start | bytes 884744 | tf_op jit(solution)/shard_map/ppermute | solution.py:692
  116.6 28.1 %collective-permute-start.19 = (bf16[8,24,768]{2,1,0:T(8,128)(2,1)}, bf16[8,24,768]{2,1,0:T(8,128)(2,1)}, u32[]{:S(2)}, u32[]{:S(2)}) collective-permute-start(bf16[8,24,768]{2,1,0:T(8,128)(2,1)} %get-tuple-element.453), channel_id=1, source_target_pairs={{0,24},{8,16},{16,8},{24,0},{1,25},{9,17},{17,9},{25,1},{2,26},{10... | collective-permute-start | bytes 884744 | tf_op jit(solution)/shard_map/ppermute | solution.py:692
  164.7 33.0 %collective-permute-start.30 = (bf16[4,8,24,768]{3,2,1,0:T(8,128)(2,1)S(1)}, bf16[4,8,24,768]{3,2,1,0:T(8,128)(2,1)}, u32[]{:S(2)}, u32[]{:S(2)}) collective-permute-start(bf16[4,8,24,768]{3,2,1,0:T(8,128)(2,1)S(1)} %pad_maximum_fusion.3.args_0_), channel_id=1, source_target_pairs={{0,2},{1,5},{2,0},{3,7},{4,6},{5,1},{6,4},{7,3},{8,10},{9,13},{10,... | collective-permute-start | bytes 3538952 | tf_op jit(solution)/shard_map/ppermute | solution.py:689
  165.1 32.7 %collective-permute-start.31 = (bf16[4,8,24,768]{3,2,1,0:T(8,128)(2,1)S(1)}, bf16[4,8,24,768]{3,2,1,0:T(8,128)(2,1)}, u32[]{:S(2)}, u32[]{:S(2)}) collective-permute-start(bf16[4,8,24,768]{3,2,1,0:T(8,128)(2,1)S(1)} %pad_maximum_fusion.3.args_0_), channel_id=1, source_target_pairs={{0,4},{1,3},{2,6},{3,1},{4,0},{5,7},{6,2},{7,5},{8,12},{9,11},{10,... | collective-permute-start | bytes 3538952 | tf_op jit(solution)/shard_map/ppermute | solution.py:689
  169.2 28.5 %collective-permute-start.27 = (bf16[9,24,768]{2,1,0:T(8,128)(2,1)}, bf16[9,24,768]{2,1,0:T(8,128)(2,1)S(1)}, u32[]{:S(2)}, u32[]{:S(2)}) collective-permute-start(bf16[9,24,768]{2,1,0:T(8,128)(2,1)} %get-tuple-element.479), channel_id=1, source_target_pairs={{0,8},{8,0},{16,24},{24,16},{1,9},{9,1},{17,25},{25,17},{2,10},{10... | collective-permute-start | bytes 995336 | tf_op jit(solution)/shard_map/ppermute | solution.py:692
  170.3 27.4 %collective-permute-start.28 = (bf16[9,24,768]{2,1,0:T(8,128)(2,1)}, bf16[9,24,768]{2,1,0:T(8,128)(2,1)S(1)}, u32[]{:S(2)}, u32[]{:S(2)}) collective-permute-start(bf16[9,24,768]{2,1,0:T(8,128)(2,1)} %get-tuple-element.479), channel_id=1, source_target_pairs={{0,16},{8,24},{16,0},{24,8},{1,17},{9,25},{17,1},{25,9},{2,18},{10... | collective-permute-start | bytes 995336 | tf_op jit(solution)/shard_map/ppermute | solution.py:692
  249.5 34.3 %collective-permute-start.46 = (bf16[4,9,24,768]{3,2,1,0:T(8,128)(2,1)S(1)}, bf16[4,9,24,768]{3,2,1,0:T(8,128)(2,1)S(1)}, u32[]{:S(2)}, u32[]{:S(2)}) collective-permute-start(bf16[4,9,24,768]{3,2,1,0:T(8,128)(2,1)S(1)} %pad_maximum_fusion.1.args_0_), channel_id=1, source_target_pairs={{0,2},{1,5},{2,0},{3,7},{4,6},{5,1},{6,4},{7,3},{8,10},{9,13},{10,... | collective-permute-start | bytes 3981320 | tf_op jit(solution)/shard_map/ppermute | solution.py:689
  250.2 33.6 %collective-permute-start.47 = (bf16[4,9,24,768]{3,2,1,0:T(8,128)(2,1)S(1)}, bf16[4,9,24,768]{3,2,1,0:T(8,128)(2,1)S(1)}, u32[]{:S(2)}, u32[]{:S(2)}) collective-permute-start(bf16[4,9,24,768]{3,2,1,0:T(8,128)(2,1)S(1)} %pad_maximum_fusion.1.args_0_), channel_id=1, source_target_pairs={{0,4},{1,3},{2,6},{3,1},{4,0},{5,7},{6,2},{7,5},{8,12},{9,11},{10,... | collective-permute-start | bytes 3981320 | tf_op jit(solution)/shard_map/ppermute | solution.py:689
  251.3 31.2 %collective-permute-start.43 = (bf16[128,201]{0,1:T(8,128)(2,1)S(1)}, bf16[128,201]{0,1:T(8,128)(2,1)S(1)}, u32[]{:S(2)}, u32[]{:S(2)}) collective-permute-start(bf16[128,201]{0,1:T(8,128)(2,1)S(1)} %get-tuple-element.546), channel_id=1, source_target_pairs={{0,2},{1,3},{2,0},{3,1},{4,6},{5,7},{6,4},{7,5},{8,10},{9,11},{10,... | collective-permute-start | bytes 154376 | tf_op jit(solution)/shard_map/ppermute | solution.py:689
  253.3 29.3 %collective-permute-start.44 = (bf16[128,201]{0,1:T(8,128)(2,1)S(1)}, bf16[128,201]{0,1:T(8,128)(2,1)S(1)}, u32[]{:S(2)}, u32[]{:S(2)}) collective-permute-start(bf16[128,201]{0,1:T(8,128)(2,1)S(1)} %get-tuple-element.546), channel_id=1, source_target_pairs={{0,4},{1,5},{2,6},{3,7},{4,0},{5,1},{6,2},{7,3},{8,12},{9,13},{10,... | collective-permute-start | bytes 154376 | tf_op jit(solution)/shard_map/ppermute | solution.py:689
  253.6 30.1 %collective-permute-start.45 = (bf16[128,201]{0,1:T(8,128)(2,1)S(1)}, bf16[128,201]{0,1:T(8,128)(2,1)S(1)}, u32[]{:S(2)}, u32[]{:S(2)}) collective-permute-start(bf16[128,201]{0,1:T(8,128)(2,1)S(1)} %get-tuple-element.546), channel_id=1, source_target_pairs={{0,6},{1,7},{2,4},{3,5},{4,2},{5,3},{6,0},{7,1},{8,14},{9,15},{10,... | collective-permute-start | bytes 154376 | tf_op jit(solution)/shard_map/ppermute | solution.py:689
  283.8 27.6 %collective-permute-start.48 = (bf16[4,9,24,768]{3,2,1,0:T(8,128)(2,1)S(1)}, bf16[4,9,24,768]{3,2,1,0:T(8,128)(2,1)S(1)}, u32[]{:S(2)}, u32[]{:S(2)}) collective-permute-start(bf16[4,9,24,768]{3,2,1,0:T(8,128)(2,1)S(1)} %collective-permute-done.46.args_1_), channel_id=1, source_target_pairs={{0,4},{1,3},{2,6},{3,1},{4,0},{5,7},{6,2},{7,5},{8,12},{9,11},{10,... | collective-permute-start | bytes 3981320 | tf_op jit(solution)/shard_map/ppermute | solution.py:689
  285.3 26.1 %collective-permute-start.49 = (bf16[4,9,24,768]{3,2,1,0:T(8,128)(2,1)S(1)}, bf16[4,9,24,768]{3,2,1,0:T(8,128)(2,1)}, u32[]{:S(2)}, u32[]{:S(2)}) collective-permute-start(bf16[4,9,24,768]{3,2,1,0:T(8,128)(2,1)S(1)} %pad_maximum_fusion.1.args_0_), channel_id=1, source_target_pairs={{0,1},{1,0},{2,3},{3,2},{4,5},{5,4},{6,7},{7,6},{8,9},{9,8},{10,11... | collective-permute-start | bytes 3981320 | tf_op jit(solution)/shard_map/ppermute | solution.py:684
  285.3 26.1 %collective-permute-start.50 = (bf16[4,9,24,768]{3,2,1,0:T(8,128)(2,1)S(1)}, bf16[4,9,24,768]{3,2,1,0:T(8,128)(2,1)}, u32[]{:S(2)}, u32[]{:S(2)}) collective-permute-start(bf16[4,9,24,768]{3,2,1,0:T(8,128)(2,1)S(1)} %collective-permute-done.46.args_1_), channel_id=1, source_target_pairs={{0,1},{1,0},{2,3},{3,2},{4,5},{5,4},{6,7},{7,6},{8,9},{9,8},{10,11... | collective-permute-start | bytes 3981320 | tf_op jit(solution)/shard_map/ppermute | solution.py:684
  337.0 31.2 %collective-permute-start.57 = (bf16[4,8,24,768]{3,2,1,0:T(8,128)(2,1)}, bf16[4,8,24,768]{3,2,1,0:T(8,128)(2,1)}, u32[]{:S(2)}, u32[]{:S(2)}) collective-permute-start(bf16[4,8,24,768]{3,2,1,0:T(8,128)(2,1)} %maximum_maximum_fusion), channel_id=1, source_target_pairs={{0,4},{1,3},{2,6},{3,1},{4,0},{5,7},{6,2},{7,5},{8,12},{9,11},{10,... | collective-permute-start | bytes 3538952 | tf_op jit(solution)/shard_map/ppermute | solution.py:689
  337.6 30.6 %collective-permute-start.58 = (bf16[4,8,24,768]{3,2,1,0:T(8,128)(2,1)}, bf16[4,8,24,768]{3,2,1,0:T(8,128)(2,1)}, u32[]{:S(2)}, u32[]{:S(2)}) collective-permute-start(bf16[4,8,24,768]{3,2,1,0:T(8,128)(2,1)} %maximum_maximum_fusion.1), channel_id=1, source_target_pairs={{0,4},{1,3},{2,6},{3,1},{4,0},{5,7},{6,2},{7,5},{8,12},{9,11},{10,... | collective-permute-start | bytes 3538952 | tf_op jit(solution)/shard_map/ppermute | solution.py:689
  388.2 79.6 %reduce-scatter.3.cloned.1.call-start = ((), (), s32[]{:S(2)}) async-start(), calls=%async_computation.2 | async-start | bytes 1474560 | tf_op jit(solution)/shard_map/reduce_scatter | solution.py:1382
  (161 other events, 1775.3 us)
Sparse Core Ops, SparseCore 0:
  388.3 34.3 reduce-scatter.4
  424.9 27.9 reduce-scatter.2

commit v3 on v2

--- a/solution.py
+++ b/solution.py
@@ -289,10 +289,16 @@
 
 def read_bwd(rq_ref, k_ref, v_ref, d_ref, r_ref, lse_ref, dq_ref, dk_ref, dv_ref):
     slots = rq_ref.shape[1]
-    lse = lse_ref[0]
+    lse = lse_ref[0].astype(f32)
+
+    def of_head(h):
+        at = h // GHEADS * 3 * GHEADS + h % GHEADS
+        hi, mid, lo = (lse[:, at + k * GHEADS : at + k * GHEADS + 1] for k in range(3))
+        return (hi + mid) + lo
+
     for group in groups_of_pairs(slots, k_ref.shape[1]):
         cs = [lanes(p) for p in group]
-        both = [jnp.concatenate([lse[:, 2 * p + k : 2 * p + k + 1] for k in range(2)], axis=0) for p in group]
+        both = [jnp.concatenate([of_head(2 * p), of_head(2 * p + 1)], axis=0) for p in group]
         parts = ([ref[0, :, c] for c in cs] for ref in (rq_ref, k_ref, v_ref, d_ref, r_ref))
         for c, (dq, dk, dv) in zip(cs, pairs_backward(*parts, None, both)):
             dq_ref[0, :, c] = dq.astype(bf)
@@ -456,13 +462,17 @@
     cot_ref,
     out_ref,
     ds2_ref,
-    dread_ref,
+    message_ref,
     dg_ref,
     *outs,
 ):
     chip = chip_ref[0]
-    split = len(outs) // 2
-    reading = read_ref[...]
+    reads = [read_ref[k] for k in range(GROUPS)]
+    reading = jnp.concatenate([x[:, :GCOLS] for x in reads], axis=-1)
+    sums = [x[:, GCOLS:] for x in reads] + [jnp.zeros((reading.shape[0], 128 - 3 * HEADS), bf)]
+    message_ref[:, D : 2 * D] = reading
+    message_ref[:, 2 * D :] = jnp.concatenate(sums, axis=-1)
+    split = 2 if len(outs) == 2 and len(outs[0].shape) == 4 else 1
     s2 = s1_ref[...] + dot(reading, wo_ref[0])
     hat, inv = normalise(s2)
     xn = (hat * g_ref[...]).astype(bf)
@@ -484,14 +494,17 @@
         if split == 1:
             outs[1][0, k * rows : (k + 1) * rows] = d_down.astype(bf)
         else:
-            emit(core_ref, d_down, outs[2], outs[3], (k, 0))
+            part = rows // 8
+            for t in range(4):
+                both = [d_down[(4 * c + t) * part : (4 * c + t + 1) * part] for c in range(2)]
+                emit(core_ref, jnp.concatenate(both, axis=0), outs[0], outs[1], (k, 5 + t))
     out_ref[...] = y.astype(bf)
     dx, dg = norm_back(dxn, hat, inv, g_ref[...])
     ds2 = cot.astype(f32) + dx
     ds2_ref[...] = ds2
     dg_ref[...] = dg
     d2b = ds2.astype(bf)
-    dread_ref[...] = dot_t(d2b, wo_ref[0]).astype(bf)
+    message_ref[:, :D] = dot_t(d2b, wo_ref[0]).astype(bf)
     emit_chip(core_ref, t_dot(own_columns(reading, chip, span, step), d2b), outs[:split], 4, span // 2)
 
 
@@ -546,6 +559,78 @@
         emit_chip(core_ref, t_dot(xn_own, dmix_ref[u]), outs, u, span // 2)
 
 
+def gain_grad(gain_ref, *pairs):
+    total = sum(jnp.sum(grad * weight.astype(f32), axis=-1, keepdims=True) for grad, weight in pairs)
+    return total / gain_ref[...].astype(f32)
+
+
+def own_sum(z, own_ref, passed, u):
+    total = own_ref[z, u].astype(f32)
+    for ref in passed:
+        total = total + ref[u].astype(f32)
+    return total
+
+
+def finish_most(
+    nz,
+    z_ref,
+    net_ref,
+    early_ref,
+    up_ref,
+    qup_ref,
+    slots_ref,
+    reader_ref,
+    writer_ref,
+    gp_ref,
+    gv_ref,
+    gs_ref,
+    gr_ref,
+    gq_ref,
+    page_ref,
+    late_ref,
+    *refs,
+):
+    page, late = refs[: nz - 1], refs[nz - 1 : 2 * nz - 2]
+    outs = refs[2 * nz - 2 :]
+    d_up, d_down, d_qup, d_ro, d_qdown, d_reader, d_writer, d_wo, d_sq, d_so, d_gp, d_gv, d_gs, d_gr, d_gq = outs
+    z = z_ref[0]
+
+    def units(ref, start, count):
+        return jnp.concatenate([ref[start + k].astype(f32) for k in range(count)], axis=-1)
+
+    up = units(net_ref, 0, 4)
+    d_up[...] = up
+    d_gv[...] = gain_grad(gv_ref, (up, up_ref[...]))
+    qup = units(early_ref, 0, 4)
+    d_qup[...] = qup
+    d_gq[...] = gain_grad(gq_ref, (qup, qup_ref[...]))
+    d_ro[...] = early_ref[4].astype(f32)
+    for k in range(4):
+        d_down[k] = net_ref[4 + k].astype(f32)
+        d_qdown[k] = early_ref[5 + k].astype(f32)
+    read_k, read_v, write_q, out = (own_sum(z, page_ref, page, u) for u in range(4))
+    sq = jnp.concatenate([own_sum(z, late_ref, late, u) for u in range(3)], axis=-1)
+    so, read_q, write_k, write_v = (own_sum(z, late_ref, late, u) for u in range(3, 7))
+    d_wo[...] = out
+    d_sq[...] = sq
+    d_so[...] = so
+    d_reader[...] = jnp.concatenate([read_q, read_k, read_v], axis=-1)
+    d_writer[...] = jnp.concatenate([write_q, write_k, write_v], axis=-1)
+    d_gs[...] = gain_grad(gs_ref, (sq, slots_ref[...]))
+    reader, writer = reader_ref[...], writer_ref[...]
+    d_gp[...] = gain_grad(gp_ref, (read_k, reader[:, D : 2 * D]), (read_v, reader[:, 2 * D :]), (write_q, writer[:, :D]))
+    d_gr[...] = gain_grad(gr_ref, (read_q, reader[:, :D]), (write_k, writer[:, D : 2 * D]), (write_v, writer[:, 2 * D :]))
+
+
+def finish_windows(z_ref, gain_ref, qkv_ref, own_ref, *refs):
+    passed, (d_qkv, d_out, d_gain) = refs[:-3], refs[-3:]
+    z = z_ref[0]
+    qkv = jnp.concatenate([own_sum(z, own_ref, passed, u) for u in range(3)], axis=-1)
+    d_qkv[...] = qkv
+    d_out[...] = own_sum(z, own_ref, passed, 3)
+    d_gain[...] = gain_grad(gain_ref, (qkv, qkv_ref[...]))
+
+
 def simple(body, name, args, outs, scratch=()):
     arrays = [a[0] if isinstance(a, tuple) else a for a in args]
     specs = [
@@ -596,6 +681,45 @@
                 out_ref[k] = w[...]
 
     return simple(body, "pack_rows", arrays + (gains,), [((n, r, D), bf) for n in (9, 7, 8, 9)])
+
+
+def net_terms(place, ups, downs):
+    nq, nz, _, r, _ = ups[0][0].shape
+    half = nz // 2
+    table = jnp.stack([place.core, place.chip]).astype(jnp.int32)
+
+    def body(table_ref, *refs):
+        outs = refs[8:]
+        z = pl.program_id(0)
+        first = jnp.where(table_ref[0] == 0, 1, 2)
+        masks = (3 - first, 3, first, 0)
+        for mask, out_ref in zip(masks, outs):
+            at = jnp.bitwise_xor(table_ref[1], mask)
+            for k in range(2):
+                a, b = refs[2 * k], refs[2 * k + 1]
+                for u in range(2):
+                    out_ref[0, 2 * k + u] = (a[at, 0, u].astype(f32) + b[at, 0, u].astype(f32)).astype(bf)
+            for k in range(2):
+                a, b = refs[4 + 2 * k], refs[5 + 2 * k]
+
+                @pl.when(z // half == k)
+                def _():
+                    for u in range(4):
+                        out_ref[0, 4 + u] = (a[at, 0, u].astype(f32) + b[at, 0, u].astype(f32)).astype(bf)
+
+    def down_block(k):
+        return pl.BlockSpec((nq, 1, 4, r, D), lambda z: (0, jnp.clip(z - k * half, 0, half - 1), 0, 0, 0))
+
+    up_block = pl.BlockSpec((nq, 1, 2, r, D), lambda z: (0, z, 0, 0, 0))
+    return call(
+        body,
+        "net_terms",
+        (sds((nz, 8, r, D), bf),) * 4,
+        [pl.BlockSpec(memory_space=pltpu.SMEM)] + [up_block] * 4 + [down_block(0)] * 2 + [down_block(1)] * 2,
+        (pl.BlockSpec((1, 8, r, D), lambda z: (z, 0, 0, 0)),) * 4,
+        (nz,),
+        (table, *ups[0], *ups[1], *downs[0], *downs[1]),
+    )
 
 
 def place_units(place, pieces, plain, tall):
@@ -1061,24 +1185,27 @@
         (place.send_line, three), (squares, all_two), (run_first, (sib_c_one, x))
     )
     all_three = all_dp(three, got)
-    c_two, sib_two, sib_f_two, sib_s_two = stage(
+    w_one, gain_all, (mix, att, v1) = first
+    g_window, g_slots, g_reader, g_page, g_vmlp, g_qmlp = (gain_all[k] for k in range(6))
+
+    def run_slots(args):
+        return simple(
+            slots_fwd,
+            "slots_fwd",
+            (args[0], g_slots, part_of(4, 1, args[1]), own_live),
+            [((3, slots, D), bf), ((slots, D), bf), ((slots, D), f32)],
+        )
+
+    c_two, sib_two, sib_f_two, sib_s_two, (mix_q, att_q, s1) = stage(
         (place.second_hop, f_two),
         (place.sibling, all_two),
         (place.sibling, f_two),
         (place.sibling, s_two),
+        (run_slots, (xs, w_one)),
     )
     sib_c_two, all_three = tie(place.sibling(c_two), all_three)
-    w_one, gain_all, (mix, att, v1) = first
-    g_window, g_slots, g_reader, g_page, g_vmlp, g_qmlp = (gain_all[k] for k in range(6))
-
     def run_second(args):
-        sib_c, v1, xs = args
-        mix_q, att_q, s1 = simple(
-            slots_fwd,
-            "slots_fwd",
-            (xs, g_slots, part_of(4, 1, w_one), own_live),
-            [((3, slots, D), bf), ((slots, D), bf), ((slots, D), f32)],
-        )
+        sib_c, v1, s1 = args
         (w_two,) = assemble(two, [all_two, f_two, s_two, c_two], [sib_two, sib_f_two, sib_s_two, sib_c], 7, 0)
         (rd_own,) = simple(
             normed_units, "slots_units", (s1, g_reader, part_of(3, 1, w_two)), [((3, slots, D), bf)]
@@ -1093,10 +1220,10 @@
             (v1, g_page, w_two),
             flops=2 * rows * 3 * D * D,
         )
-        return w_two, rd_own, pk, mix_q, att_q, s1
-
-    got, (f_three, s_three), (w_two, rd_own, pk, mix_q, att_q, s1) = stage(
-        (place.send_line, four), (squares, all_three), (run_second, (sib_c_two, v1, xs))
+        return w_two, rd_own, pk
+
+    got, (f_three, s_three), (w_two, rd_own, pk) = stage(
+        (place.send_line, four), (squares, all_three), (run_second, (sib_c_two, v1, s1))
     )
     rd_two = place.sibling(rd_own)
     rd_two, got = tie(rd_two, got)
@@ -1271,8 +1398,6 @@
         (partial(run_mlp, True), (v2, g_vmlp, w_up, w_down, cot, y, dxn)),
     )
     reads = place.in_order([message] + list(reads))
-    lse_page = jnp.swapaxes(reads[..., GCOLS:], 0, 1).reshape(slots, 3 * HEADS)
-    read_q = jnp.swapaxes(reads[..., :GCOLS], 0, 1).reshape(slots, D)
 
     def run_write_bwd(args):
         return run_grads(
@@ -1296,23 +1421,24 @@
         (run_write_bwd, (dv2, writing, pk, wk, wv, live, w_two)),
     )
     down_pairs = [(down_one[0], net_got[2]), (down_two[0], net_got[3])]
-    second, corner, first, own_net = place.square_terms(
-        place.chip_terms([(up_one[0], net_got[0]), (up_two[0], net_got[1]), down_pairs])
-    )
+    up_pairs = [(up_one[0], net_got[0]), (up_two[0], net_got[1])]
+    if fast:
+        second, corner, first, own_net = net_terms(place, up_pairs, down_pairs)
+    else:
+        second, corner, first, own_net = place.square_terms(place.chip_terms(up_pairs + [down_pairs]))
 
     def run_query(args):
         units, w_down = assemble(
             four, [all_four, f_four, s_four, c_four], [sib_four, sib_f_four, sib_s_four, sib_c_four], 5, 1
         )
-        s1, read_q = args
+        s1, reads = args
         up_block = pl.BlockSpec((4, D, D), lambda *_: (0, 0, 0), pipeline_mode=pl.Buffered(1))
         return simple(
             partial(query_mlp, 2 * r, D // nz),
             "query_mlp",
-            (chip_id, core_id, s1, read_q, part_of(1, 4, units), g_qmlp, (units, up_block), w_down, xs_cot),
-            [((slots, D), bf), ((slots, D), f32), ((slots, D), bf), ((1, D), f32)]
-            + chip_shapes(5, r)
-            + chip_shapes(1, 4 * r),
+            (chip_id, core_id, s1, reads, part_of(1, 4, units), g_qmlp, (units, up_block), w_down, xs_cot),
+            [((slots, D), bf), ((slots, D), f32), ((slots, 2 * D + 128), bf), ((1, D), f32)]
+            + (chip_shapes(9, r) if fast else chip_shapes(5, r) + chip_shapes(1, 4 * r)),
         )
 
     def chip_shapes(k, r):
@@ -1324,40 +1450,40 @@
         x = outs[0].reshape(-1, nz, 2, r, D)
         return [jnp.swapaxes(pick(x, which, 2), 0, 1) for which in (core, 1 - core)]
 
-    second, corner, (q_out, ds2, d_read, dg_qmlp, *d_early) = stage(
+    second, corner, (q_out, ds2, message, dg_qmlp, *d_early) = stage(
         (partial(place.outer_hop, 1), second.astype(bf)),
         (partial(place.outer_hop, 1), corner.astype(bf)),
-        (run_query, (s1, read_q)),
-    )
-    own_net = own_net + second.astype(f32)
-    first = (first + corner.astype(f32)).astype(bf)
-
-    count = len(d_early) // 2
-    pairs = zip(chip_pair(d_early[:count], r), chip_pair(d_early[count:], 4 * r))
-    keep_early, give_early = (jnp.concatenate([a, b.reshape(nz, 4, r, D)], axis=1) for a, b in pairs)
-    three_parts = jnp.concatenate([d_read, read_q, lse_page], axis=-1)
-    parts_two, early_got = stage((place.sibling, three_parts), (place.sibling, give_early))
-    three_parts = ordered(even, three_parts, parts_two)
-    d_read_all, read_all = three_parts[..., :D], three_parts[..., D : 2 * D]
-    lse_all = join_three(three_parts[..., 2 * D :].reshape(MICRO, slots, GROUPS, 3 * GHEADS))
-    lse_all = jnp.pad(lse_all.reshape(MICRO, slots, HEADS), ((0, 0), (0, 0), (0, 128 - HEADS)))
+        (run_query, (s1, reads)),
+    )
+    own_net = own_net.astype(f32) + second.astype(f32)
+    first = (first.astype(f32) + corner.astype(f32)).astype(bf)
+
+    if fast:
+        keep_early, give_early = d_early
+    else:
+        pairs = zip(chip_pair(d_early[:1], r), chip_pair(d_early[1:], 4 * r))
+        keep_early, give_early = (jnp.concatenate([a, b.reshape(nz, 4, r, D)], axis=1) for a, b in pairs)
+    message_two, early_got = stage((place.sibling, message), (place.sibling, give_early))
+    message = ordered(even, message, message_two)
     early = (keep_early.astype(f32) + early_got.astype(f32)).astype(bf)
     early_sum = lax.psum_scatter(early.reshape(nz, 9 * r, D), "dp", scatter_dimension=0).reshape(9, r, D)
-    early_sum = early_sum.astype(f32)
 
     def run_read_bwd(args):
+        grad_block = pl.BlockSpec((1, slots, D), lambda p: (p, 0, 0))
+        read_block = pl.BlockSpec((1, slots, D), lambda p: (p, 0, 1))
+        sums_block = pl.BlockSpec((1, slots, 128), lambda p: (p, 0, 2 * D // 128))
         return call(
             read_bwd,
             "read_bwd",
             (sds((MICRO, slots, D), bf), sds((rows, D), bf), sds((rows, D), bf)),
-            [slot_block, of_pk(0), of_pk(1), slot_block, slot_block, stat_block],
+            [slot_block, of_pk(0), of_pk(1), grad_block, read_block, sums_block],
             (slot_block, act_block, act_block),
             (MICRO,),
             args,
             flops=2 * rows * slots * D * 10,
         )
 
-    drq, dk, dv = run_read_bwd((rq, pk, pk, d_read_all, read_all, lse_all))
+    drq, dk, dv = run_read_bwd((rq, pk, pk, message, message, message))
 
     def run_page_bwd(args):
         return run_grads(
@@ -1418,7 +1544,7 @@
         (partial(run_window_bwd, 1), (dv1, mix, att, bias, w_one, dmix)),
     )
     own_page = own_page + second.astype(f32)
-    first = (first + corner.astype(f32)).astype(bf)
+    first = (first.astype(f32) + corner.astype(f32)).astype(bf)
     d_rd = jnp.transpose(place.in_order([d_rd] + list(rds)), (1, 2, 0, 3)).reshape(3, slots, D)
 
     def run_query_back(args):
@@ -1443,25 +1569,30 @@
             2 * rows * 4 * D * D,
         )
 
-    first, (pair_window,) = stage(
-        (partial(place.outer_hop, 0), first), (run_window_grads, (dv1, x, dmix, att, g_window))
-    )
-    pair_window, net_sum, early_sum = tie(pair_window, net_sum, early_sum)
-    own_page = place.inner_square((own_page + first.astype(f32)).astype(bf))
-    (window_got,) = stage((place.sibling, pair_window[1]))
-    second, corner, first, own_window = place.square_terms(place.chip_terms([(pair_window[0], window_got)]))
-    second, corner, page_passed, (x_grad, dg_slots, dg_reader, *d_late) = stage(
-        (partial(place.outer_hop, 1), second.astype(bf)),
-        (partial(place.outer_hop, 1), corner.astype(bf)),
-        (place.send_terms, own_page),
+    def right(x):
+        return lax.ppermute(x, "fsdp", [(f, (f + bands) % nf) for f in range(nf)])
+
+    first, query_out, (x_grad, dg_slots, dg_reader, *d_late), side_out = stage(
+        (partial(place.outer_hop, 0), first),
+        (place.owned_rows, q_out),
         (
             run_query_back,
             (chip_id, core_id, xs, s1, ds2, d_rd, g_reader, w_two, w_one, mix_q, att_q, own_live, g_slots),
         ),
-    )
-    own_window = own_window + second.astype(f32)
-    first = (first + corner.astype(f32)).astype(bf)
+        (last_columns, v3),
+    )
+    own_page = place.inner_square((own_page + first.astype(f32)).astype(bf))
     keep_late, give_late = chip_pair(d_late, r)
+    late_got, page_passed, side_out, (pair_window,) = stage(
+        (place.sibling, give_late),
+        (place.send_terms, own_page),
+        (right, side_out),
+        (run_window_grads, (dv1, x, dmix, att, g_window)),
+    )
+    pair_window, net_sum, early_sum = tie(pair_window, net_sum, early_sum)
+    late = (keep_late.astype(f32) + late_got.astype(f32)).astype(bf)
+    (window_got,) = stage((place.sibling, pair_window[1]))
+    second, corner, first, own_window = place.square_terms(place.chip_terms([(pair_window[0], window_got)]))
 
     def run_window_end(args):
         return call(
@@ -1477,88 +1608,95 @@
         )
 
     def run_ends(args):
-        v3, *rest = args
+        v3, side_out, *rest = args
         v_grad, dg_window = run_window_end(rest)
-        return v_grad, dg_window, last_columns(v3), last_columns(v_grad)
-
-    first, late_got, (v_grad, dg_window, side_out, side_grad) = stage(
-        (partial(place.outer_hop, 0), first),
-        (place.sibling, give_late),
-        (run_ends, (v3, dv1, x, dmix, g_window, w_one)),
-    )
+        return v_grad, last_columns(v_grad), roll_out(v3, side_out, place, bands)
+
+    second, corner, late_passed, (v_grad, side_grad, visual_out) = stage(
+        (partial(place.outer_hop, 1), second.astype(bf)),
+        (partial(place.outer_hop, 1), corner.astype(bf)),
+        (place.send_terms, late),
+        (run_ends, (v3, side_out, dv1, x, dmix, g_window, w_one)),
+    )
+    own_window = own_window + second.astype(f32)
+    first = (first.astype(f32) + corner.astype(f32)).astype(bf)
+    first, query_grad = stage((partial(place.outer_hop, 0), first), (place.owned_rows, x_grad))
     own_window = place.inner_square((own_window + first.astype(f32)).astype(bf))
-    late = (keep_late.astype(f32) + late_got.astype(f32)).astype(bf)
-    last = jnp.concatenate([own_window, late], axis=1)
-
-    def right(x):
-        return lax.ppermute(x, "fsdp", [(f, (f + bands) % nf) for f in range(nf)])
-
-    own_gains = jnp.concatenate([dg_window, dg_page, dg_vmlp])
-    query_gains = jnp.concatenate([dg_slots, dg_reader, dg_qmlp])
-    (chip_gains,) = stage((lambda x: [place.hop(x, mask) for mask in range(1, nq)], own_gains))
-    gain_rows = jnp.concatenate([own_gains + sum(chip_gains), query_gains]).reshape(6, nz, nq, 2, r)
-    gain_rows = pick(gain_rows, place.chip, 2)
-    last_terms = [pick(last, place.z ^ m) for m in range(1, nz)]
-    count = max(nz // 2, 1)
-    passed_one, side_out, side_grad, gains_two = stage(
-        (lambda xs: [place.across(x, m + 1) for m, x in enumerate(xs)], last_terms[:count]),
-        (right, side_out),
+    z_id = place.z.astype(jnp.int32).reshape(1)
+
+    def column(gain):
+        return gain.reshape(r, 1)
+
+    def run_finish(args):
+        net_sum, early_sum, own_page, page_passed, late, late_passed = args
+        rows_of = [((r, 4 * D), f32), ((4, r, D), f32), ((r, 4 * D), f32), ((r, D), f32), ((4, r, D), f32)]
+        rows_of += [((r, 3 * D), f32)] * 2 + [((r, D), f32), ((r, 3 * D), f32), ((r, D), f32)] + [((r, 1), f32)] * 5
+        return simple(
+            partial(finish_most, nz),
+            "finish_most",
+            (
+                z_id,
+                net_sum,
+                early_sum,
+                visual_up,
+                query_up,
+                slots_qkv,
+                reader_qkv,
+                writer_qkv,
+                column(norm_page),
+                column(norm_visual_mlp),
+                column(norm_slots),
+                column(norm_reader),
+                column(norm_query_mlp),
+                own_page,
+                late,
+                *page_passed,
+                *late_passed,
+            ),
+            rows_of,
+        )
+
+    window_passed, side_grad, most = stage(
+        (place.send_terms, own_window),
         (right, side_grad),
-        (place.sibling, pick(gain_rows, 1 - core, 2)),
-    )
-    gain_rows = jnp.swapaxes(pick(gain_rows, core, 2) + gains_two, 0, 1)
-    passed_two, gains_passed, visual_out, visual_grad = stage(
-        (lambda xs: [place.across(x, m + 1 + count) for m, x in enumerate(xs)], last_terms[count:]),
-        (place.send_terms, gain_rows),
-        (lambda args: roll_out(*args, place, bands), (v3, side_out)),
-        (lambda args: roll_out(*args, place, bands), (v_grad, side_grad)),
-    )
-    last_sum = place.own_terms(last) + sum(y.astype(f32) for y in list(passed_one) + list(passed_two))
-    grad_win, late_sum = last_sum[:4], last_sum[4:]
-    both = place.own_terms(gain_rows) + sum(gains_passed)
-    q_out, x_grad, net_sum, early_sum, own_page, page_passed, _ = tie(
-        q_out, x_grad, net_sum, early_sum, own_page, page_passed, passed_one
-    )
-    grad_page = place.own_terms(own_page) + sum(y.astype(f32) for y in page_passed)
-
-    query_out = place.owned_rows(q_out)
-    query_grad = place.owned_rows(x_grad)
-
-    grad_up = net_sum[:4].astype(f32)
-    grad_down = net_sum[4:].reshape(4 * r, D).astype(f32)
-    grad_qup = jnp.concatenate([early_sum[k] for k in range(4)], axis=1)
-    grad_ro = early_sum[4]
-    grad_qdown = early_sum[5:].reshape(4 * r, D)
-    grad_sq = jnp.concatenate([late_sum[k] for k in range(3)], axis=1)
-    grad_so = late_sum[3]
-    grad_rd = jnp.concatenate([late_sum[4 + k] for k in range(3)], axis=1)
-
-    def wide(units):
-        return jnp.concatenate([units[k] for k in range(units.shape[0])], axis=1)
+        (run_finish, (net_sum, early_sum, own_page, page_passed, late, late_passed)),
+    )
+    visual_grad = roll_out(v_grad, side_grad, place, bands)
+    grad_win, grad_win_out, grad_gw = simple(
+        finish_windows,
+        "finish_windows",
+        (z_id, column(norm_window), window_qkv, own_window, *window_passed),
+        [((r, 3 * D), f32), ((r, D), f32), ((r, 1), f32)],
+    )
+    grad_up, grad_down, grad_qup, grad_ro, grad_qdown, grad_reader, grad_writer, grad_wo, grad_sq, grad_so = most[:10]
+    grad_gp, grad_gv, grad_gs, grad_gr, grad_gq = most[10:]
+
+    def gain(x):
+        return x.reshape(r)
 
     return (
         visual_out,
         query_out,
         visual_grad,
         query_grad,
-        both[0],
-        wide(grad_win[:3]),
-        grad_win[3],
-        both[3],
+        gain(grad_gw),
+        grad_win,
+        grad_win_out,
+        gain(grad_gs),
         grad_sq,
         grad_so,
-        both[4],
-        both[1],
-        jnp.concatenate([grad_rd[:, :D], wide(grad_page[:2])], axis=1),
+        gain(grad_gr),
+        gain(grad_gp),
+        grad_reader,
         grad_ro,
-        jnp.concatenate([grad_page[2], grad_rd[:, D:]], axis=1),
-        grad_page[3],
-        both[2],
-        wide(grad_up),
-        grad_down,
-        both[5],
+        grad_writer,
+        grad_wo,
+        gain(grad_gv),
+        grad_up,
+        grad_down.reshape(4 * r, D),
+        gain(grad_gq),
         grad_qup,
-        grad_qdown,
+        grad_qdown.reshape(4 * r, D),
     )
 
 

time: 591 us -> 575 us (0.973)
  other arithmetic: 56.7 us -> 41.6 us
  Pallas kernels: 250 us -> 263 us
  local copies, waits for them, and re-layouts: 49.6 us -> 39.8 us
    pallas_call x22 -> x25, Pallas kernels: 191 us -> 205 us  [call(): pl.pallas_call(body, name=name, out_shape=out_shape, grid=grid, in_specs=...]
    ppermute x21, waiting for transfers between devices: 59.1 us -> 49.7 us  [across(): return lax.ppermute(x, 'dp', [(z, z ^ mask) for z in range(self.nz)])]
    ppermute x38 -> x35, waiting for transfers between devices: 49.6 us -> 52.6 us  [hop(): return lax.ppermute(x, 'fsdp', route)]
    ppermute x38 -> x35, starting transfers between devices: 39.2 us -> 36.5 us  [hop(): return lax.ppermute(x, 'fsdp', route)]
    unnamed x175 -> x162, local copies, waits for them, and re-layouts: 18.2 us -> 17.8 us
  transfers between devices with their start and end apart: 98 -> 94, of which waited for: 20 -> 24; matrix products, arithmetic and copies ran while one was open for 9% -> 8% of each run, Pallas kernels for 41% -> 42%
where the time goes in v3:
time: 575 us; the launch traced here: 571 us
  Pallas kernels  263 us (46%)
  waiting for transfers between devices  114 us (20%)
  starting transfers between devices  97.7 us (17%)
  other arithmetic  41.6 us (7%)
  local copies, waits for them, and re-layouts  39.8 us (7%)
  between operations  15.7 us (3%)
    pallas_call x25, Pallas kernels, call(): pl.pallas_call(body, name=name, out_shape=out_shape, grid=grid, in_specs=...  205 us
    ppermute x35, waiting for transfers between devices, hop(): return lax.ppermute(x, 'fsdp', route)  52.6 us
    ppermute x21, waiting for transfers between devices, across(): return lax.ppermute(x, 'dp', [(z, z ^ mask) for z in range(self.nz)])  49.7 us
    ppermute x21, starting transfers between devices, across(): return lax.ppermute(x, 'dp', [(z, z ^ mask) for z in range(self.nz)])  49.1 us
    ppermute x35, starting transfers between devices, hop(): return lax.ppermute(x, 'fsdp', route)  36.5 us
    pallas_call x4, Pallas kernels, place_units(): pl.pallas_call(body, name='place_units', grid=(nz,), out_shape=tuple(shap...  35.1 us
    pallas_call x2, Pallas kernels, run_window_bwd(): pl.pallas_call(window_bwd, name='window_bwd', out_shape=sds((3, rows, D),...  22.9 us
    unnamed x162, local copies, waits for them, and re-layouts  17.8 us
  transfers between devices with their start and end apart: 94, of which 24 were waited for; matrix products, arithmetic and copies ran while one was open for 8% of the time, Pallas kernels for 42%

profile of v3, /device:TPU:0, one launch (start us, length us, event | category | flops | bytes accessed | tf_op | source)
XLA Modules:
  0.0 571.1 jit_solution(15572338764108436710)
XLA Ops:
  20.7 8.5 %collective-permute-done = bf16[9,24,768]{2,1,0:T(8,128)(2,1)S(1)} collective-permute-done((bf16[9,24,768]{2,1,0:T(8,128)(2,1)}, bf16[9,24,768]{2,1,0:T(8,128)(2,1)S(1)}, u32[]{:S(2)}, u32[]{:S(2)}) %collective-permute-start) | collective-permute-done | bytes 331808 | tf_op jit(solution)/shard_map/ppermute | solution.py:816
  29.2 13.5 %collective-permute-done.1 = bf16[9,24,768]{2,1,0:T(8,128)(2,1)S(1)} collective-permute-done((bf16[9,24,768]{2,1,0:T(8,128)(2,1)}, bf16[9,24,768]{2,1,0:T(8,128)(2,1)S(1)}, u32[]{:S(2)}, u32[]{:S(2)}) %collective-permute-start.1) | collective-permute-done | bytes 331808 | tf_op jit(solution)/shard_map/ppermute | solution.py:816
  61.8 11.8 %collective-permute-done.6 = bf16[7,24,768]{2,1,0:T(8,128)(2,1)S(1)} collective-permute-done((bf16[7,24,768]{2,1,0:T(8,128)(2,1)}, bf16[7,24,768]{2,1,0:T(8,128)(2,1)S(1)}, u32[]{:S(2)}, u32[]{:S(2)}) %collective-permute-start.6) | collective-permute-done | bytes 258080 | tf_op jit(solution)/shard_map/ppermute | solution.py:816
  80.6 11.2 %collective-permute-done.10.args_3_ = bf16[4,9,24,768]{3,2,1,0:T(8,128)(2,1)} collective-permute-done((bf16[4,9,24,768]{3,2,1,0:T(8,128)(2,1)}, bf16[4,9,24,768]{3,2,1,0:T(8,128)(2,1)}, u32[]{:S(2)}, u32[]{:S(2)}) %collective-permute-start.10) | collective-permute-done | bytes 1327136 | tf_op jit(solution)/shard_map/ppermute | solution.py:813
  107.8 7.6 %collective-permute-start.17 = (bf16[8,24,768]{2,1,0:T(8,128)(2,1)}, bf16[8,24,768]{2,1,0:T(8,128)(2,1)}, u32[]{:S(2)}, u32[]{:S(2)}) collective-permute-start(bf16[8,24,768]{2,1,0:T(8,128)(2,1)} %get-tuple-element.472), channel_id=1, source_target_pairs={{0,8},{8,0},{16,24},{24,16},{1,9},{9,1},{17,25},{25,17},{2,10},{10... | collective-permute-start | bytes 884744 | tf_op jit(solution)/shard_map/ppermute | solution.py:816
  117.8 8.8 %place_units.4 = (bf16[8,16,48,768]{3,2,1,0:T(8,128)(2,1)}, f32[16,8,768]{2,1,0:T(8,128)}) custom-call(s32[3]{0:T(128)} %pad_add_fusion.table_ref, bf16[4,9,24,768]{3,2,1,0:T(8,128)(2,1)} %copy-done.3, bf16[4,9,24,768]{3,2,1,0:T(8,128)(2,1)} %collective-permute-done.8.args_1_, bf16[4,9,24,768]{3,2,1,0:T(8,128)(2,1)} %collective-permute-done.9.args_2_, ...), custom_call_target="tpu_custom_call" | custom-call | bytes 21233664 | tf_op jit(solution)/shard_map/place_units/pallas_call | solution.py:769
  130.4 15.2 %window_fwd.1 = (bf16[3,864,768]{2,1,0:T(8,128)(2,1)}, bf16[864,768]{1,0:T(8,128)(2,1)}, f32[864,768]{1,0:T(8,128)}) custom-call(bf16[864,768]{1,0:T(8,128)(2,1)} %roll_in.2.x_ref, f32[3,144,144]{2,1,0:T(8,128)} %compare_select_fusion.bias_ref, f32[1,768]{1,0:T(1,128)} %squeeze.150.gw_ref, bf16[8,768,768]{2,1,0:T(8,128)(2,1)} %bitcast.254), custom_call_target="tpu_custom_call" | custom-call | flops 4076863488 | bytes 1048576 | tf_op jit(solution)/shard_map/window_fwd/pallas_call | solution.py:123
  169.8 7.9 %place_units.5 = bf16[7,16,48,768]{3,2,1,0:T(8,128)(2,1)} custom-call(s32[3]{0:T(128)} %pad_add_fusion.table_ref, bf16[4,7,24,768]{3,2,1,0:T(8,128)(2,1)} %copy-done.6, bf16[4,7,24,768]{3,2,1,0:T(8,128)(2,1)} %copy-done.30, bf16[4,7,24,768]{3,2,1,0:T(8,128)(2,1)} %collective-permute-done.21.args_2_, bf16[4,7,24,768]{3,2,1,0:T(8,128)(2,1)} %collective-permute-done.22.args_3_, ...), custom_call_target="tpu_custom_call" | custom-call | bytes 16515072 | tf_op jit(solution)/shard_map/place_units/pallas_call | solution.py:769
  181.5 7.8 %page_units.1.k_ref.v_ref.wq_ref = bf16[3,864,768]{2,1,0:T(8,128)(2,1)} custom-call(f32[864,768]{1,0:T(8,128)} %get-tuple-element.669.x_ref.v1_ref, f32[1,768]{1,0:T(1,128)} %get-tuple-element.674.g_ref.gp_ref, bf16[7,768,768]{2,1,0:T(8,128)(2,1)} %bitcast.249), custom_call_target="tpu_custom_call" | custom-call | flops 3057647616 | bytes 1048576 | tf_op jit(solution)/shard_map/page_units/pallas_call | solution.py:123
  205.1 7.4 %collective-permute-done.33.args_3_ = bf16[4,8,24,768]{3,2,1,0:T(8,128)(2,1)} collective-permute-done((bf16[4,8,24,768]{3,2,1,0:T(8,128)(2,1)}, bf16[4,8,24,768]{3,2,1,0:T(8,128)(2,1)}, u32[]{:S(2)}, u32[]{:S(2)}) %collective-permute-start.33) | collective-permute-done | bytes 1179680 | tf_op jit(solution)/shard_map/ppermute | solution.py:813
  217.7 8.4 %write_fwd.1 = (bf16[864,768]{1,0:T(8,128)(2,1)}, f32[864,768]{1,0:T(8,128)}) custom-call(f32[864,768]{1,0:T(8,128)} %get-tuple-element.669.x_ref.v1_ref, bf16[3,864,768]{2,1,0:T(8,128)(2,1)} %page_units.1.k_ref.v_ref.wq_ref, bf16[2,128,768]{2,1,0:T(8,128)(2,1)} %get-tuple-element.618.wk_ref, bf16[2,128,768]{2,1,0:T(8,128)(2,1)} %get-tuple-element.619.wv_ref, ...), custom_call_target="tpu_custom_call" | custom-call | flops 1019215872 | bytes 1048576 | tf_op jit(solution)/shard_map/write_fwd/pallas_call | solution.py:123
  233.6 8.8 %place_units.6 = (bf16[4,16,48,768]{3,2,1,0:T(8,128)(2,1)}, bf16[16,192,768]{2,1,0:T(8,128)(2,1)}) custom-call(s32[3]{0:T(128)} %pad_add_fusion.table_ref, bf16[4,8,24,768]{3,2,1,0:T(8,128)(2,1)} %copy-done.4, bf16[4,8,24,768]{3,2,1,0:T(8,128)(2,1)} %collective-permute-done.30.args_1_, bf16[4,8,24,768]{3,2,1,0:T(8,128)(2,1)} %collective-permute-done.31.args_2_, ...), custom_call_target="tpu_custom_call" | custom-call | bytes 18874368 | tf_op jit(solution)/shard_map/place_units/pallas_call | solution.py:769
  252.2 22.5 %mlp_both.2 = (f32[864,768]{1,0:T(8,128)}, f32[864,768]{1,0:T(8,128)}, bf16[4,4,2,24,768]{4,3,2,1,0:T(8,128)(2,1)}, bf16[4,4,2,24,768]{4,3,2,1,0:T(8,128)(2,1)},...) custom-call(s32[1]{0:T(128)} %bitcast.26.core_ref, f32[864,768]{1,0:T(8,128)} %get-tuple-element.590.x_ref, ...), custom_call_target="tpu_custom_call" | custom-call | flops 12230590464 | bytes 1048576 | tf_op jit(solution)/shard_map/mlp_both/pallas_call | solution.py:123
  283.6 25.6 %mlp_both.3 = (bf16[864,768]{1,0:T(8,128)(2,1)}, f32[864,768]{1,0:T(8,128)}, f32[1,768]{1,0:T(1,128)}, bf16[4,4,2,24,768]{4,3,2,1,0:T(8,128)(2,1)}, bf16[4,4,2,2...) custom-call(s32[1]{0:T(128)} %bitcast.26.core_ref, ...), custom_call_target="tpu_custom_call" | custom-call | flops 12230590464 | bytes 1048576 | tf_op jit(solution)/shard_map/mlp_both/pallas_call | solution.py:123
  312.4 13.1 %write_bwd.1 = (bf16[864,768]{1,0:T(8,128)(2,1)}, bf16[2,128,768]{2,1,0:T(8,128)(2,1)}, bf16[2,128,768]{2,1,0:T(8,128)(2,1)}, bf16[4,4,1,24,768]{4,3,2,1,0:T(8,128)(2,1)}, bf16[4,4,1,24,768]{4,3,2,1,0:T(8,128)(2,1)}) custom-call(s32[1]{0:T(128)} %bitcast.26.core_ref, f32[864,768]{1,0:T(8,128)} %get-tuple-element.670.dv2_ref, ...), custom_call_target="tpu_custom_call" | custom-call | flops 2038431744 | bytes 1048576 | tf_op jit(solution)/shard_map/write_bwd/pallas_call | solution.py:123
  335.6 9.7 %place_units.7 = (bf16[5,16,48,768]{3,2,1,0:T(8,128)(2,1)}, bf16[16,192,768]{2,1,0:T(8,128)(2,1)}) custom-call(s32[3]{0:T(128)} %pad_add_fusion.table_ref, bf16[4,9,24,768]{3,2,1,0:T(8,128)(2,1)} %copy-done.2, bf16[4,9,24,768]{3,2,1,0:T(8,128)(2,1)} %copy-done.17, bf16[4,9,24,768]{3,2,1,0:T(8,128)(2,1)} %copy-done.18, bf16[4,9,24,768]{3,2,1,0:T(8,128)(2,1)} %copy-done.20, ...), custom_call_target="tpu_custom_call" | custom-call | bytes 21233664 | tf_op jit(solution)/shard_map/place_units/pallas_call | solution.py:769
  345.3 13.4 %query_mlp.1 = (bf16[128,768]{1,0:T(8,128)(2,1)}, f32[128,768]{1,0:T(8,128)}, bf16[128,1664]{1,0:T(8,128)(2,1)}, f32[1,768]{1,0:T(1,128)}, bf16[4,9,24,768]{3,2,...) custom-call(s32[1]{0:T(128)} %bitcast.45.chip_ref, s32[1]{0:T(128)} %bitcast.26.core_ref, ...), custom_call_target="tpu_custom_call" | custom-call | flops 1073741824 | bytes 1048576 | tf_op jit(solution)/shard_map/query_mlp/pallas_call | solution.py:123
  367.8 7.7 %read_bwd.1 = (bf16[2,128,768]{2,1,0:T(8,128)(2,1)}, bf16[864,768]{1,0:T(8,128)(2,1)}, bf16[864,768]{1,0:T(8,128)(2,1)}) custom-call(bf16[2,128,768]{2,1,0:T(8,128)(2,1)} %get-tuple-element.526.rq_ref, bf16[3,864,768]{2,1,0:T(8,128)(2,1)} %page_units.1.k_ref.v_ref.wq_ref, bf16[3,864,768]{2,1,0:T(8,128)(2,1)} %page_units.1.k_ref.v_ref.wq_ref, ...), custom_call_target="tpu_custom_call" | custom-call | flops 1698693120 | bytes 1048576 | tf_op jit(solution)/shard_map/read_bwd/pallas_call | solution.py:123
  377.4 15.6 %page_bwd.1 = (f32[864,768]{1,0:T(8,128)}, f32[1,768]{1,0:T(1,128)}, bf16[4,4,3,24,768]{4,3,2,1,0:T(8,128)(2,1)}, bf16[4,4,3,24,768]{4,3,2,1,0:T(8,128)(2,1)}) custom-call(s32[1]{0:T(128)} %bitcast.26.core_ref, f32[864,768]{1,0:T(8,128)} %get-tuple-element.669.x_ref.v1_ref, f32[864,768]{1,0:T(8,128)} %get-tuple-element.670.dv2_ref, ...), custom_call_target="tpu_custom_call" | custom-call | flops 6115295232 | bytes 1048576 | tf_op jit(solution)/shard_map/page_bwd/pallas_call | solution.py:123
  402.5 11.5 %window_bwd.2.refs_0_ = bf16[3,864,768]{2,1,0:T(8,128)(2,1)} custom-call(f32[864,768]{1,0:T(8,128)} %get-tuple-element.768.dv1_ref, bf16[3,864,768]{2,1,0:T(8,128)(2,1)} %get-tuple-element.705.mix_ref, bf16[864,768]{1,0:T(8,128)(2,1)} %get-tuple-element.749.att_ref, f32[3,144,144]{2,1,0:T(8,128)} %compare_select_fusion.bias_ref, bf16[8,768,768]{2,1,0:T(8,128)(2,1)} %bitcast.256), custom_call_target="tpu_custom_call" | custom-call | flops 1019215872 | bytes 1048576 | tf_op jit(solution)/shard_map/window_bwd/pallas_call | solution.py:1515
  427.2 11.4 %window_bwd.3.dmix_ref = bf16[3,864,768]{2,1,0:T(8,128)(2,1)} custom-call(f32[864,768]{1,0:T(8,128)} %get-tuple-element.768.dv1_ref, bf16[3,864,768]{2,1,0:T(8,128)(2,1)} %get-tuple-element.705.mix_ref, bf16[864,768]{1,0:T(8,128)(2,1)} %get-tuple-element.749.att_ref, f32[3,144,144]{2,1,0:T(8,128)} %compare_select_fusion.bias_ref, ...), custom_call_target="tpu_custom_call", output_to_operand_aliasing={{}: (5, {})} | custom-call | flops 1019215872 | bytes 1048576 | tf_op jit(solution)/shard_map/window_bwd/pallas_call | solution.py:1515
  449.2 10.2 %query_back.1 = (bf16[128,768]{1,0:T(8,128)(2,1)}, f32[1,768]{1,0:T(1,128)}, f32[1,768]{1,0:T(1,128)}, bf16[4,7,24,768]{3,2,1,0:T(8,128)(2,1)}, bf16[4,7,24,768]{3,2,1,0:T(8,128)(2,1)}) custom-call(s32[1]{0:T(128)} %bitcast.45.chip_ref, s32[1]{0:T(128)} %bitcast.26.core_ref, bf16[128,768]{1,0:T(8,128)(2,1)} %get-tuple-element.723.x_ref, ...), custom_call_target="tpu_custom_call" | custom-call | flops 1073741824 | bytes 1048576 | tf_op jit(solution)/shard_map/query_back/pallas_call | solution.py:123
  472.8 11.4 %window_grads.1 = (bf16[4,4,4,24,768]{4,3,2,1,0:T(8,128)(2,1)}, bf16[4,4,4,24,768]{4,3,2,1,0:T(8,128)(2,1)}) custom-call(s32[1]{0:T(128)} %bitcast.26.core_ref, f32[864,768]{1,0:T(8,128)} %get-tuple-element.768.dv1_ref, bf16[864,768]{1,0:T(8,128)(2,1)} %roll_in.2.x_ref, bf16[3,864,768]{2,1,0:T(8,128)(2,1)} %window_bwd.3.dmix_ref, ...), custom_call_target="tpu_custom_call" | custom-call | flops 4076863488 | bytes 1048576 | tf_op jit(solution)/shard_map/window_grads/pallas_call | solution.py:123
  500.4 9.0 %window_end.1 = (bf16[864,768]{1,0:T(8,128)(2,1)}, f32[1,768]{1,0:T(1,128)}) custom-call(f32[864,768]{1,0:T(8,128)} %get-tuple-element.768.dv1_ref, bf16[864,768]{1,0:T(8,128)(2,1)} %roll_in.2.x_ref, bf16[3,864,768]{2,1,0:T(8,128)(2,1)} %window_bwd.3.dmix_ref, f32[1,768]{1,0:T(1,128)} %get-tuple-element.771.gw_ref, bf16[8,768,768]{2,1,0:T(8,128)(2,1)} %bitcast.259), custom_call_target="tpu_custom_call" | custom-call | flops 3057647616 | bytes 1048576 | tf_op jit(solution)/shard_map/window_end/pallas_call | solution.py:123
  (502 shorter events, 277.3 us)
Async XLA Ops:
  7.2 477.8 %reduce-scatter.5.cloned.1.call-start = ((), (), s32[]{:S(2)}) async-start(), calls=%async_computation.3 | async-start | bytes 1658880 | tf_op jit(solution)/shard_map/reduce_scatter | solution.py:1469
  11.8 31.0 %collective-permute-start.3 = (bf16[432,768]{1,0:T(8,128)(2,1)S(1)}, bf16[432,768]{1,0:T(8,128)(2,1)S(1)}, u32[]{:S(2)}, u32[]{:S(2)}) collective-permute-start(bf16[432,768]{1,0:T(8,128)(2,1)S(1)} %reshape.538), channel_id=1, source_target_pairs={{1,0},{2,1},{3,2},{4,3},{5,4},{6,5},{7,6},{0,7},{9,8},{10,9},{11,1... | collective-permute-start | bytes 1990664 | tf_op jit(solution)/shard_map/ppermute | solution.py:962
  44.2 29.5 %collective-permute-start.8 = (bf16[4,9,24,768]{3,2,1,0:T(8,128)(2,1)S(1)}, bf16[4,9,24,768]{3,2,1,0:T(8,128)(2,1)}, u32[]{:S(2)}, u32[]{:S(2)}) collective-permute-start(bf16[4,9,24,768]{3,2,1,0:T(8,128)(2,1)S(1)} %pad_maximum_fusion.args_0_), channel_id=1, source_target_pairs={{0,2},{1,5},{2,0},{3,7},{4,6},{5,1},{6,4},{7,3},{8,10},{9,13},{10,... | collective-permute-start | bytes 3981320 | tf_op jit(solution)/shard_map/ppermute | solution.py:813
  44.3 29.4 %collective-permute-start.9 = (bf16[4,9,24,768]{3,2,1,0:T(8,128)(2,1)S(1)}, bf16[4,9,24,768]{3,2,1,0:T(8,128)(2,1)}, u32[]{:S(2)}, u32[]{:S(2)}) collective-permute-start(bf16[4,9,24,768]{3,2,1,0:T(8,128)(2,1)S(1)} %pad_maximum_fusion.args_0_), channel_id=1, source_target_pairs={{0,4},{1,3},{2,6},{3,1},{4,0},{5,7},{6,2},{7,5},{8,12},{9,11},{10,... | collective-permute-start | bytes 3981320 | tf_op jit(solution)/shard_map/ppermute | solution.py:813
  104.5 41.2 %collective-permute-start.20 = (bf16[4,7,24,768]{3,2,1,0:T(8,128)(2,1)S(1)}, bf16[4,7,24,768]{3,2,1,0:T(8,128)(2,1)S(1)}, u32[]{:S(2)}, u32[]{:S(2)}) collective-permute-start(bf16[4,7,24,768]{3,2,1,0:T(8,128)(2,1)S(1)} %pad_maximum_fusion.4.args_0_), channel_id=1, source_target_pairs={{0,2},{1,5},{2,0},{3,7},{4,6},{5,1},{6,4},{7,3},{8,10},{9,13},{10,... | collective-permute-start | bytes 3096584 | tf_op jit(solution)/shard_map/ppermute | solution.py:813
  105.8 39.9 %collective-permute-start.21 = (bf16[4,7,24,768]{3,2,1,0:T(8,128)(2,1)S(1)}, bf16[4,7,24,768]{3,2,1,0:T(8,128)(2,1)}, u32[]{:S(2)}, u32[]{:S(2)}) collective-permute-start(bf16[4,7,24,768]{3,2,1,0:T(8,128)(2,1)S(1)} %pad_maximum_fusion.4.args_0_), channel_id=1, source_target_pairs={{0,4},{1,3},{2,6},{3,1},{4,0},{5,7},{6,2},{7,5},{8,12},{9,11},{10,... | collective-permute-start | bytes 3096584 | tf_op jit(solution)/shard_map/ppermute | solution.py:813
  107.8 37.8 %collective-permute-start.17 = (bf16[8,24,768]{2,1,0:T(8,128)(2,1)}, bf16[8,24,768]{2,1,0:T(8,128)(2,1)}, u32[]{:S(2)}, u32[]{:S(2)}) collective-permute-start(bf16[8,24,768]{2,1,0:T(8,128)(2,1)} %get-tuple-element.472), channel_id=1, source_target_pairs={{0,8},{8,0},{16,24},{24,16},{1,9},{9,1},{17,25},{25,17},{2,10},{10... | collective-permute-start | bytes 884744 | tf_op jit(solution)/shard_map/ppermute | solution.py:816
  115.4 30.2 %collective-permute-start.18 = (bf16[8,24,768]{2,1,0:T(8,128)(2,1)}, bf16[8,24,768]{2,1,0:T(8,128)(2,1)}, u32[]{:S(2)}, u32[]{:S(2)}) collective-permute-start(bf16[8,24,768]{2,1,0:T(8,128)(2,1)} %get-tuple-element.472), channel_id=1, source_target_pairs={{0,16},{8,24},{16,0},{24,8},{1,17},{9,25},{17,1},{25,9},{2,18},{10... | collective-permute-start | bytes 884744 | tf_op jit(solution)/shard_map/ppermute | solution.py:816
  116.4 29.3 %collective-permute-start.19 = (bf16[8,24,768]{2,1,0:T(8,128)(2,1)}, bf16[8,24,768]{2,1,0:T(8,128)(2,1)}, u32[]{:S(2)}, u32[]{:S(2)}) collective-permute-start(bf16[8,24,768]{2,1,0:T(8,128)(2,1)} %get-tuple-element.472), channel_id=1, source_target_pairs={{0,24},{8,16},{16,8},{24,0},{1,25},{9,17},{17,9},{25,1},{2,26},{10... | collective-permute-start | bytes 884744 | tf_op jit(solution)/shard_map/ppermute | solution.py:816
  163.4 29.2 %collective-permute-start.30 = (bf16[4,8,24,768]{3,2,1,0:T(8,128)(2,1)S(1)}, bf16[4,8,24,768]{3,2,1,0:T(8,128)(2,1)}, u32[]{:S(2)}, u32[]{:S(2)}) collective-permute-start(bf16[4,8,24,768]{3,2,1,0:T(8,128)(2,1)S(1)} %pad_maximum_fusion.2.args_0_), channel_id=1, source_target_pairs={{0,2},{1,5},{2,0},{3,7},{4,6},{5,1},{6,4},{7,3},{8,10},{9,13},{10,... | collective-permute-start | bytes 3538952 | tf_op jit(solution)/shard_map/ppermute | solution.py:813
  163.7 28.9 %collective-permute-start.31 = (bf16[4,8,24,768]{3,2,1,0:T(8,128)(2,1)S(1)}, bf16[4,8,24,768]{3,2,1,0:T(8,128)(2,1)}, u32[]{:S(2)}, u32[]{:S(2)}) collective-permute-start(bf16[4,8,24,768]{3,2,1,0:T(8,128)(2,1)S(1)} %pad_maximum_fusion.2.args_0_), channel_id=1, source_target_pairs={{0,4},{1,3},{2,6},{3,1},{4,0},{5,7},{6,2},{7,5},{8,12},{9,11},{10,... | collective-permute-start | bytes 3538952 | tf_op jit(solution)/shard_map/ppermute | solution.py:813
  166.5 26.1 %collective-permute-start.28 = (bf16[9,24,768]{2,1,0:T(8,128)(2,1)}, bf16[9,24,768]{2,1,0:T(8,128)(2,1)S(1)}, u32[]{:S(2)}, u32[]{:S(2)}) collective-permute-start(bf16[9,24,768]{2,1,0:T(8,128)(2,1)} %get-tuple-element.506), channel_id=1, source_target_pairs={{0,16},{8,24},{16,0},{24,8},{1,17},{9,25},{17,1},{25,9},{2,18},{10... | collective-permute-start | bytes 995336 | tf_op jit(solution)/shard_map/ppermute | solution.py:816
  246.8 34.8 %collective-permute-start.46 = (bf16[4,9,24,768]{3,2,1,0:T(8,128)(2,1)S(1)}, bf16[4,9,24,768]{3,2,1,0:T(8,128)(2,1)S(1)}, u32[]{:S(2)}, u32[]{:S(2)}) collective-permute-start(bf16[4,9,24,768]{3,2,1,0:T(8,128)(2,1)S(1)} %pad_maximum_fusion.1.args_0_), channel_id=1, source_target_pairs={{0,2},{1,5},{2,0},{3,7},{4,6},{5,1},{6,4},{7,3},{8,10},{9,13},{10,... | collective-permute-start | bytes 3981320 | tf_op jit(solution)/shard_map/ppermute | solution.py:813
  247.6 34.1 %collective-permute-start.47 = (bf16[4,9,24,768]{3,2,1,0:T(8,128)(2,1)S(1)}, bf16[4,9,24,768]{3,2,1,0:T(8,128)(2,1)S(1)}, u32[]{:S(2)}, u32[]{:S(2)}) collective-permute-start(bf16[4,9,24,768]{3,2,1,0:T(8,128)(2,1)S(1)} %pad_maximum_fusion.1.args_0_), channel_id=1, source_target_pairs={{0,4},{1,3},{2,6},{3,1},{4,0},{5,7},{6,2},{7,5},{8,12},{9,11},{10,... | collective-permute-start | bytes 3981320 | tf_op jit(solution)/shard_map/ppermute | solution.py:813
  248.7 31.4 %collective-permute-start.43 = (bf16[128,201]{1,0:T(8,128)(2,1)S(1)}, bf16[128,201]{1,0:T(8,128)(2,1)S(1)}, u32[]{:S(2)}, u32[]{:S(2)}) collective-permute-start(bf16[128,201]{1,0:T(8,128)(2,1)S(1)} %pad_maximum_fusion.15), channel_id=1, source_target_pairs={{0,2},{1,3},{2,0},{3,1},{4,6},{5,7},{6,4},{7,5},{8,10},{9,11},{10,... | collective-permute-start | bytes 154376 | tf_op jit(solution)/shard_map/ppermute | solution.py:813
  250.6 29.5 %collective-permute-start.44 = (bf16[128,201]{1,0:T(8,128)(2,1)S(1)}, bf16[128,201]{1,0:T(8,128)(2,1)S(1)}, u32[]{:S(2)}, u32[]{:S(2)}) collective-permute-start(bf16[128,201]{1,0:T(8,128)(2,1)S(1)} %pad_maximum_fusion.15), channel_id=1, source_target_pairs={{0,4},{1,5},{2,6},{3,7},{4,0},{5,1},{6,2},{7,3},{8,12},{9,13},{10,... | collective-permute-start | bytes 154376 | tf_op jit(solution)/shard_map/ppermute | solution.py:813
  250.9 30.7 %collective-permute-start.45 = (bf16[128,201]{1,0:T(8,128)(2,1)S(1)}, bf16[128,201]{1,0:T(8,128)(2,1)S(1)}, u32[]{:S(2)}, u32[]{:S(2)}) collective-permute-start(bf16[128,201]{1,0:T(8,128)(2,1)S(1)} %pad_maximum_fusion.15), channel_id=1, source_target_pairs={{0,6},{1,7},{2,4},{3,5},{4,2},{5,3},{6,0},{7,1},{8,14},{9,15},{10,... | collective-permute-start | bytes 154376 | tf_op jit(solution)/shard_map/ppermute | solution.py:813
  281.7 27.6 %collective-permute-start.48 = (bf16[4,9,24,768]{3,2,1,0:T(8,128)(2,1)S(1)}, bf16[4,9,24,768]{3,2,1,0:T(8,128)(2,1)S(1)}, u32[]{:S(2)}, u32[]{:S(2)}) collective-permute-start(bf16[4,9,24,768]{3,2,1,0:T(8,128)(2,1)S(1)} %collective-permute-done.46.args_1_), channel_id=1, source_target_pairs={{0,4},{1,3},{2,6},{3,1},{4,0},{5,7},{6,2},{7,5},{8,12},{9,11},{10,... | collective-permute-start | bytes 3981320 | tf_op jit(solution)/shard_map/ppermute | solution.py:813
  283.1 26.2 %collective-permute-start.49 = (bf16[4,9,24,768]{3,2,1,0:T(8,128)(2,1)S(1)}, bf16[4,9,24,768]{3,2,1,0:T(8,128)(2,1)}, u32[]{:S(2)}, u32[]{:S(2)}) collective-permute-start(bf16[4,9,24,768]{3,2,1,0:T(8,128)(2,1)S(1)} %pad_maximum_fusion.1.args_0_), channel_id=1, source_target_pairs={{0,1},{1,0},{2,3},{3,2},{4,5},{5,4},{6,7},{7,6},{8,9},{9,8},{10,11... | collective-permute-start | bytes 3981320 | tf_op jit(solution)/shard_map/ppermute | solution.py:808
  283.1 26.2 %collective-permute-start.50 = (bf16[4,9,24,768]{3,2,1,0:T(8,128)(2,1)S(1)}, bf16[4,9,24,768]{3,2,1,0:T(8,128)(2,1)}, u32[]{:S(2)}, u32[]{:S(2)}) collective-permute-start(bf16[4,9,24,768]{3,2,1,0:T(8,128)(2,1)S(1)} %collective-permute-done.46.args_1_), channel_id=1, source_target_pairs={{0,1},{1,0},{2,3},{3,2},{4,5},{5,4},{6,7},{7,6},{8,9},{9,8},{10,11... | collective-permute-start | bytes 3981320 | tf_op jit(solution)/shard_map/ppermute | solution.py:808
  334.3 28.4 %collective-permute-start.58 = (bf16[4,8,24,768]{3,2,1,0:T(8,128)(2,1)}, bf16[4,8,24,768]{3,2,1,0:T(8,128)(2,1)S(1)}, u32[]{:S(2)}, u32[]{:S(2)}) collective-permute-start(bf16[4,8,24,768]{3,2,1,0:T(8,128)(2,1)} %get-tuple-element.640), channel_id=1, source_target_pairs={{0,4},{1,3},{2,6},{3,1},{4,0},{5,7},{6,2},{7,5},{8,12},{9,11},{10,... | collective-permute-start | bytes 3538952 | tf_op jit(solution)/shard_map/ppermute | solution.py:813
  398.1 86.8 %reduce-scatter.3.cloned.1.call-start = ((), (), s32[]{:S(2)}) async-start(), calls=%async_computation.2 | async-start | bytes 1474560 | tf_op jit(solution)/shard_map/reduce_scatter | solution.py:1508
  492.1 27.3 %collective-permute-start.81 = (bf16[4,4,24,768]{3,2,1,0:T(8,128)(2,1)}, bf16[4,4,24,768]{3,2,1,0:T(8,128)(2,1)S(1)}, u32[]{:S(2)}, u32[]{:S(2)}) collective-permute-start(bf16[4,4,24,768]{3,2,1,0:T(8,128)(2,1)} %get-tuple-element.765), channel_id=1, source_target_pairs={{0,4},{1,3},{2,6},{3,1},{4,0},{5,7},{6,2},{7,5},{8,12},{9,11},{10,... | collective-permute-start | bytes 1769480 | tf_op jit(solution)/shard_map/ppermute | solution.py:813
  493.1 26.3 %collective-permute-start.82 = (bf16[4,4,24,768]{3,2,1,0:T(8,128)(2,1)}, bf16[4,4,24,768]{3,2,1,0:T(8,128)(2,1)S(1)}, u32[]{:S(2)}, u32[]{:S(2)}) collective-permute-start(bf16[4,4,24,768]{3,2,1,0:T(8,128)(2,1)} %get-tuple-element.766), channel_id=1, source_target_pairs={{0,4},{1,3},{2,6},{3,1},{4,0},{5,7},{6,2},{7,5},{8,12},{9,11},{10,... | collective-permute-start | bytes 1769480 | tf_op jit(solution)/shard_map/ppermute | solution.py:813
  (151 other events, 1873.9 us)
Sparse Core Ops, SparseCore 0:
  398.3 35.2 reduce-scatter.4
  435.9 27.9 reduce-scatter.2

commit v4 on v3

--- a/solution.py
+++ b/solution.py
@@ -1175,7 +1175,8 @@
         (lambda args: roll_in(*args, place, bands), (visual, beside_x)),
     )
     ends = spread_order(ends, ends_two, 0)
-    sib_c_one, ends_two, got = tie(place.sibling(c_one), spread(ends, 1), got)
+    sib_c_one, got = tie(place.sibling(c_one), got)
+    ends_two = spread(ends, 1)
     ends = spread_order(ends, ends_two, 1)
     for bit in range(2, nq.bit_length() - 1):
         ends = spread_order(ends, spread(ends, bit), bit)
@@ -1385,16 +1386,18 @@
     for bit in range(2, nq.bit_length() - 1):
         reading = merge([reading, place.hop(reading, 1 << bit)])
     message = jnp.concatenate([reading[:, :GCOLS].astype(bf)] + split_three(reading[:, GCOLS:]), axis=-1)
-    reads, (f_four, s_four), (y, dxn, up_one, down_one) = stage(
+    reads, f_four, sib_four, (y, dxn, up_one, down_one) = stage(
         (place.group_hops, message),
-        (squares, all_four),
+        (place.first_hop, all_four),
+        (place.sibling, all_four),
         (partial(run_mlp, False), (v2, g_vmlp, w_up, w_down, cot)),
     )
-    c_four, sib_four, sib_f_four, sib_s_four, (v3, dv2, dg_vmlp, up_two, down_two) = stage(
+    c_four, s_four, sib_f_four, up_one_got, down_one_got, (v3, dv2, dg_vmlp, up_two, down_two) = stage(
         (place.second_hop, f_four),
-        (place.sibling, all_four),
+        (place.second_hop, all_four),
         (place.sibling, f_four),
-        (place.sibling, s_four),
+        (place.sibling, up_one[1]),
+        (place.sibling, down_one[1]),
         (partial(run_mlp, True), (v2, g_vmlp, w_up, w_down, cot, y, dxn)),
     )
     reads = place.in_order([message] + list(reads))
@@ -1412,16 +1415,15 @@
             4 * rows * D * D,
         )
 
-    sib_c_four, *net_got, (dwq, dwk, dwv, pair_wo) = stage(
+    sib_c_four, sib_s_four, up_two_got, down_two_got, (dwq, dwk, dwv, pair_wo) = stage(
         (place.sibling, c_four),
-        (place.sibling, up_one[1]),
+        (place.sibling, s_four),
         (place.sibling, up_two[1]),
-        (place.sibling, down_one[1]),
         (place.sibling, down_two[1]),
         (run_write_bwd, (dv2, writing, pk, wk, wv, live, w_two)),
     )
-    down_pairs = [(down_one[0], net_got[2]), (down_two[0], net_got[3])]
-    up_pairs = [(up_one[0], net_got[0]), (up_two[0], net_got[1])]
+    down_pairs = [(down_one[0], down_one_got), (down_two[0], down_two_got)]
+    up_pairs = [(up_one[0], up_one_got), (up_two[0], up_two_got)]
     if fast:
         second, corner, first, own_net = net_terms(place, up_pairs, down_pairs)
     else:

time: 575 us -> 569 us (0.990)
  waiting for transfers between devices: 114 us -> 107 us
    ppermute x35, waiting for transfers between devices: 52.6 us -> 45 us  [hop(): return lax.ppermute(x, 'fsdp', route)]
    unnamed x162 -> x168, local copies, waits for them, and re-layouts: 17.8 us -> 17.6 us
  transfers between devices with their start and end apart: 94 -> 94, of which waited for: 24 -> 24; matrix products, arithmetic and copies ran while one was open for 8% -> 8% of each run, Pallas kernels for 42% -> 43%
where the time goes in v4:
time: 569 us; the launch traced here: 564 us
  Pallas kernels  262 us (46%)
  waiting for transfers between devices  107 us (19%)
  starting transfers between devices  97.2 us (17%)
  other arithmetic  42.4 us (7%)
  local copies, waits for them, and re-layouts  39.6 us (7%)
  between operations  15.8 us (3%)
    pallas_call x25, Pallas kernels, call(): pl.pallas_call(body, name=name, out_shape=out_shape, grid=grid, in_specs=...  205 us
    ppermute x21, waiting for transfers between devices, across(): return lax.ppermute(x, 'dp', [(z, z ^ mask) for z in range(self.nz)])  49.4 us
    ppermute x21, starting transfers between devices, across(): return lax.ppermute(x, 'dp', [(z, z ^ mask) for z in range(self.nz)])  49.1 us
    ppermute x35, waiting for transfers between devices, hop(): return lax.ppermute(x, 'fsdp', route)  45 us
    ppermute x35, starting transfers between devices, hop(): return lax.ppermute(x, 'fsdp', route)  36.2 us
    pallas_call x4, Pallas kernels, place_units(): pl.pallas_call(body, name='place_units', grid=(nz,), out_shape=tuple(shap...  35.1 us
    pallas_call x2, Pallas kernels, run_window_bwd(): pl.pallas_call(window_bwd, name='window_bwd', out_shape=sds((3, rows, D),...  22.9 us
    unnamed x168, local copies, waits for them, and re-layouts  17.6 us
  transfers between devices with their start and end apart: 94, of which 24 were waited for; matrix products, arithmetic and copies ran while one was open for 8% of the time, Pallas kernels for 43%

profile of v4, /device:TPU:0, one launch (start us, length us, event | category | flops | bytes accessed | tf_op | source)
XLA Modules:
  0.0 564.0 jit_solution(4626809087894082352)
XLA Ops:
  20.7 8.5 %collective-permute-done = bf16[9,24,768]{2,1,0:T(8,128)(2,1)S(1)} collective-permute-done((bf16[9,24,768]{2,1,0:T(8,128)(2,1)}, bf16[9,24,768]{2,1,0:T(8,128)(2,1)S(1)}, u32[]{:S(2)}, u32[]{:S(2)}) %collective-permute-start) | collective-permute-done | bytes 331808 | tf_op jit(solution)/shard_map/ppermute | solution.py:816
  29.2 13.5 %collective-permute-done.1 = bf16[9,24,768]{2,1,0:T(8,128)(2,1)S(1)} collective-permute-done((bf16[9,24,768]{2,1,0:T(8,128)(2,1)}, bf16[9,24,768]{2,1,0:T(8,128)(2,1)S(1)}, u32[]{:S(2)}, u32[]{:S(2)}) %collective-permute-start.1) | collective-permute-done | bytes 331808 | tf_op jit(solution)/shard_map/ppermute | solution.py:816
  61.8 11.8 %collective-permute-done.6 = bf16[7,24,768]{2,1,0:T(8,128)(2,1)S(1)} collective-permute-done((bf16[7,24,768]{2,1,0:T(8,128)(2,1)}, bf16[7,24,768]{2,1,0:T(8,128)(2,1)S(1)}, u32[]{:S(2)}, u32[]{:S(2)}) %collective-permute-start.6) | collective-permute-done | bytes 258080 | tf_op jit(solution)/shard_map/ppermute | solution.py:816
  80.6 11.2 %collective-permute-done.10.args_3_ = bf16[4,9,24,768]{3,2,1,0:T(8,128)(2,1)} collective-permute-done((bf16[4,9,24,768]{3,2,1,0:T(8,128)(2,1)}, bf16[4,9,24,768]{3,2,1,0:T(8,128)(2,1)}, u32[]{:S(2)}, u32[]{:S(2)}) %collective-permute-start.10) | collective-permute-done | bytes 1327136 | tf_op jit(solution)/shard_map/ppermute | solution.py:813
  105.8 7.9 %collective-permute-start.16 = (bf16[8,24,768]{2,1,0:T(8,128)(2,1)}, bf16[8,24,768]{2,1,0:T(8,128)(2,1)S(1)}, u32[]{:S(2)}, u32[]{:S(2)}) collective-permute-start(bf16[8,24,768]{2,1,0:T(8,128)(2,1)} %get-tuple-element.471), channel_id=1, source_target_pairs={{0,8},{8,0},{16,24},{24,16},{1,9},{9,1},{17,25},{25,17},{2,10},{10... | collective-permute-start | bytes 884744 | tf_op jit(solution)/shard_map/ppermute | solution.py:816
  116.2 8.8 %place_units.4 = (bf16[8,16,48,768]{3,2,1,0:T(8,128)(2,1)}, f32[16,8,768]{2,1,0:T(8,128)}) custom-call(s32[3]{0:T(128)} %pad_add_fusion.table_ref, bf16[4,9,24,768]{3,2,1,0:T(8,128)(2,1)} %copy-done.3, bf16[4,9,24,768]{3,2,1,0:T(8,128)(2,1)} %collective-permute-done.8.args_1_, bf16[4,9,24,768]{3,2,1,0:T(8,128)(2,1)} %collective-permute-done.9.args_2_, ...), custom_call_target="tpu_custom_call" | custom-call | bytes 21233664 | tf_op jit(solution)/shard_map/place_units/pallas_call | solution.py:769
  126.9 15.2 %window_fwd.1 = (bf16[3,864,768]{2,1,0:T(8,128)(2,1)}, bf16[864,768]{1,0:T(8,128)(2,1)}, f32[864,768]{1,0:T(8,128)}) custom-call(bf16[864,768]{1,0:T(8,128)(2,1)} %roll_in.2.x_ref, f32[3,144,144]{2,1,0:T(8,128)} %compare_select_fusion.bias_ref, f32[1,768]{1,0:T(1,128)} %squeeze.150.gw_ref, bf16[8,768,768]{2,1,0:T(8,128)(2,1)} %bitcast.254), custom_call_target="tpu_custom_call" | custom-call | flops 4076863488 | bytes 1048576 | tf_op jit(solution)/shard_map/window_fwd/pallas_call | solution.py:123
  149.9 7.9 %collective-permute-done.22.args_3_ = bf16[4,7,24,768]{3,2,1,0:T(8,128)(2,1)} collective-permute-done((bf16[4,7,24,768]{3,2,1,0:T(8,128)(2,1)S(1)}, bf16[4,7,24,768]{3,2,1,0:T(8,128)(2,1)}, u32[]{:S(2)}, u32[]{:S(2)}) %collective-permute-start.22) | collective-permute-done | bytes 1032224 | tf_op jit(solution)/shard_map/ppermute | solution.py:813
  166.8 7.8 %place_units.5 = bf16[7,16,48,768]{3,2,1,0:T(8,128)(2,1)} custom-call(s32[3]{0:T(128)} %pad_add_fusion.table_ref, bf16[4,7,24,768]{3,2,1,0:T(8,128)(2,1)} %copy-done.6, bf16[4,7,24,768]{3,2,1,0:T(8,128)(2,1)} %copy-done.30, bf16[4,7,24,768]{3,2,1,0:T(8,128)(2,1)} %collective-permute-done.20.args_2_, bf16[4,7,24,768]{3,2,1,0:T(8,128)(2,1)} %collective-permute-done.22.args_3_, ...), custom_call_target="tpu_custom_call" | custom-call | bytes 16515072 | tf_op jit(solution)/shard_map/place_units/pallas_call | solution.py:769
  178.4 7.7 %page_units.1.k_ref.v_ref.wq_ref = bf16[3,864,768]{2,1,0:T(8,128)(2,1)} custom-call(f32[864,768]{1,0:T(8,128)} %get-tuple-element.669.x_ref.v1_ref, f32[1,768]{1,0:T(1,128)} %get-tuple-element.674.g_ref.gp_ref, bf16[7,768,768]{2,1,0:T(8,128)(2,1)} %bitcast.249), custom_call_target="tpu_custom_call" | custom-call | flops 3057647616 | bytes 1048576 | tf_op jit(solution)/shard_map/page_units/pallas_call | solution.py:123
  215.0 8.4 %write_fwd.1 = (bf16[864,768]{1,0:T(8,128)(2,1)}, f32[864,768]{1,0:T(8,128)}) custom-call(f32[864,768]{1,0:T(8,128)} %get-tuple-element.669.x_ref.v1_ref, bf16[3,864,768]{2,1,0:T(8,128)(2,1)} %page_units.1.k_ref.v_ref.wq_ref, bf16[2,128,768]{2,1,0:T(8,128)(2,1)} %get-tuple-element.620.wk_ref, bf16[2,128,768]{2,1,0:T(8,128)(2,1)} %get-tuple-element.621.wv_ref, ...), custom_call_target="tpu_custom_call" | custom-call | flops 1019215872 | bytes 1048576 | tf_op jit(solution)/shard_map/write_fwd/pallas_call | solution.py:123
  230.9 8.8 %place_units.6 = (bf16[4,16,48,768]{3,2,1,0:T(8,128)(2,1)}, bf16[16,192,768]{2,1,0:T(8,128)(2,1)}) custom-call(s32[3]{0:T(128)} %pad_add_fusion.table_ref, bf16[4,8,24,768]{3,2,1,0:T(8,128)(2,1)} %copy-done.4, bf16[4,8,24,768]{3,2,1,0:T(8,128)(2,1)} %collective-permute-done.30.args_1_, bf16[4,8,24,768]{3,2,1,0:T(8,128)(2,1)} %collective-permute-done.31.args_2_, ...), custom_call_target="tpu_custom_call" | custom-call | bytes 18874368 | tf_op jit(solution)/shard_map/place_units/pallas_call | solution.py:769
  247.9 22.5 %mlp_both.2 = (f32[864,768]{1,0:T(8,128)}, f32[864,768]{1,0:T(8,128)}, bf16[4,4,2,24,768]{4,3,2,1,0:T(8,128)(2,1)}, bf16[4,4,2,24,768]{4,3,2,1,0:T(8,128)(2,1)},...) custom-call(s32[1]{0:T(128)} %bitcast.25.core_ref, f32[864,768]{1,0:T(8,128)} %get-tuple-element.592.x_ref, ...), custom_call_target="tpu_custom_call" | custom-call | flops 12230590464 | bytes 1048576 | tf_op jit(solution)/shard_map/mlp_both/pallas_call | solution.py:123
  273.1 25.6 %mlp_both.3 = (bf16[864,768]{1,0:T(8,128)(2,1)}, f32[864,768]{1,0:T(8,128)}, f32[1,768]{1,0:T(1,128)}, bf16[4,4,2,24,768]{4,3,2,1,0:T(8,128)(2,1)}, bf16[4,4,2,2...) custom-call(s32[1]{0:T(128)} %bitcast.25.core_ref, ...), custom_call_target="tpu_custom_call" | custom-call | flops 12230590464 | bytes 1048576 | tf_op jit(solution)/shard_map/mlp_both/pallas_call | solution.py:123
  305.2 13.1 %write_bwd.1 = (bf16[864,768]{1,0:T(8,128)(2,1)}, bf16[2,128,768]{2,1,0:T(8,128)(2,1)}, bf16[2,128,768]{2,1,0:T(8,128)(2,1)}, bf16[4,4,1,24,768]{4,3,2,1,0:T(8,128)(2,1)}, bf16[4,4,1,24,768]{4,3,2,1,0:T(8,128)(2,1)}) custom-call(s32[1]{0:T(128)} %bitcast.25.core_ref, f32[864,768]{1,0:T(8,128)} %get-tuple-element.670.dv2_ref, ...), custom_call_target="tpu_custom_call" | custom-call | flops 2038431744 | bytes 1048576 | tf_op jit(solution)/shard_map/write_bwd/pallas_call | solution.py:123
  328.4 9.7 %place_units.7 = (bf16[5,16,48,768]{3,2,1,0:T(8,128)(2,1)}, bf16[16,192,768]{2,1,0:T(8,128)(2,1)}) custom-call(s32[3]{0:T(128)} %pad_add_fusion.table_ref, bf16[4,9,24,768]{3,2,1,0:T(8,128)(2,1)} %copy-done.2, bf16[4,9,24,768]{3,2,1,0:T(8,128)(2,1)} %copy-done.17, bf16[4,9,24,768]{3,2,1,0:T(8,128)(2,1)} %collective-permute-done.49.args_2_, ...), custom_call_target="tpu_custom_call" | custom-call | bytes 21233664 | tf_op jit(solution)/shard_map/place_units/pallas_call | solution.py:769
  338.0 13.4 %query_mlp.1 = (bf16[128,768]{1,0:T(8,128)(2,1)}, f32[128,768]{1,0:T(8,128)}, bf16[128,1664]{1,0:T(8,128)(2,1)}, f32[1,768]{1,0:T(1,128)}, bf16[4,9,24,768]{3,2,...) custom-call(s32[1]{0:T(128)} %bitcast.45.chip_ref, s32[1]{0:T(128)} %bitcast.25.core_ref, ...), custom_call_target="tpu_custom_call" | custom-call | flops 1073741824 | bytes 1048576 | tf_op jit(solution)/shard_map/query_mlp/pallas_call | solution.py:123
  360.5 7.7 %read_bwd.1 = (bf16[2,128,768]{2,1,0:T(8,128)(2,1)}, bf16[864,768]{1,0:T(8,128)(2,1)}, bf16[864,768]{1,0:T(8,128)(2,1)}) custom-call(bf16[2,128,768]{2,1,0:T(8,128)(2,1)} %get-tuple-element.525.rq_ref, bf16[3,864,768]{2,1,0:T(8,128)(2,1)} %page_units.1.k_ref.v_ref.wq_ref, bf16[3,864,768]{2,1,0:T(8,128)(2,1)} %page_units.1.k_ref.v_ref.wq_ref, ...), custom_call_target="tpu_custom_call" | custom-call | flops 1698693120 | bytes 1048576 | tf_op jit(solution)/shard_map/read_bwd/pallas_call | solution.py:123
  371.3 15.5 %page_bwd.1 = (f32[864,768]{1,0:T(8,128)}, f32[1,768]{1,0:T(1,128)}, bf16[4,4,3,24,768]{4,3,2,1,0:T(8,128)(2,1)}, bf16[4,4,3,24,768]{4,3,2,1,0:T(8,128)(2,1)}) custom-call(s32[1]{0:T(128)} %bitcast.25.core_ref, f32[864,768]{1,0:T(8,128)} %get-tuple-element.669.x_ref.v1_ref, f32[864,768]{1,0:T(8,128)} %get-tuple-element.670.dv2_ref, ...), custom_call_target="tpu_custom_call" | custom-call | flops 6115295232 | bytes 1048576 | tf_op jit(solution)/shard_map/page_bwd/pallas_call | solution.py:123
  396.4 11.5 %window_bwd.2.refs_0_ = bf16[3,864,768]{2,1,0:T(8,128)(2,1)} custom-call(f32[864,768]{1,0:T(8,128)} %get-tuple-element.768.dv1_ref, bf16[3,864,768]{2,1,0:T(8,128)(2,1)} %get-tuple-element.705.mix_ref, bf16[864,768]{1,0:T(8,128)(2,1)} %get-tuple-element.749.att_ref, f32[3,144,144]{2,1,0:T(8,128)} %compare_select_fusion.bias_ref, bf16[8,768,768]{2,1,0:T(8,128)(2,1)} %bitcast.256), custom_call_target="tpu_custom_call" | custom-call | flops 1019215872 | bytes 1048576 | tf_op jit(solution)/shard_map/window_bwd/pallas_call | solution.py:1517
  421.0 11.4 %window_bwd.3.dmix_ref = bf16[3,864,768]{2,1,0:T(8,128)(2,1)} custom-call(f32[864,768]{1,0:T(8,128)} %get-tuple-element.768.dv1_ref, bf16[3,864,768]{2,1,0:T(8,128)(2,1)} %get-tuple-element.705.mix_ref, bf16[864,768]{1,0:T(8,128)(2,1)} %get-tuple-element.749.att_ref, f32[3,144,144]{2,1,0:T(8,128)} %compare_select_fusion.bias_ref, ...), custom_call_target="tpu_custom_call", output_to_operand_aliasing={{}: (5, {})} | custom-call | flops 1019215872 | bytes 1048576 | tf_op jit(solution)/shard_map/window_bwd/pallas_call | solution.py:1517
  442.2 10.2 %query_back.1 = (bf16[128,768]{1,0:T(8,128)(2,1)}, f32[1,768]{1,0:T(1,128)}, f32[1,768]{1,0:T(1,128)}, bf16[4,7,24,768]{3,2,1,0:T(8,128)(2,1)}, bf16[4,7,24,768]{3,2,1,0:T(8,128)(2,1)}) custom-call(s32[1]{0:T(128)} %bitcast.45.chip_ref, s32[1]{0:T(128)} %bitcast.25.core_ref, bf16[128,768]{1,0:T(8,128)(2,1)} %get-tuple-element.723.x_ref, ...), custom_call_target="tpu_custom_call" | custom-call | flops 1073741824 | bytes 1048576 | tf_op jit(solution)/shard_map/query_back/pallas_call | solution.py:123
  465.8 11.4 %window_grads.1 = (bf16[4,4,4,24,768]{4,3,2,1,0:T(8,128)(2,1)}, bf16[4,4,4,24,768]{4,3,2,1,0:T(8,128)(2,1)}) custom-call(s32[1]{0:T(128)} %bitcast.25.core_ref, f32[864,768]{1,0:T(8,128)} %get-tuple-element.768.dv1_ref, bf16[864,768]{1,0:T(8,128)(2,1)} %roll_in.2.x_ref, bf16[3,864,768]{2,1,0:T(8,128)(2,1)} %window_bwd.3.dmix_ref, ...), custom_call_target="tpu_custom_call" | custom-call | flops 4076863488 | bytes 1048576 | tf_op jit(solution)/shard_map/window_grads/pallas_call | solution.py:123
  493.7 9.0 %window_end.1 = (bf16[864,768]{1,0:T(8,128)(2,1)}, f32[1,768]{1,0:T(1,128)}) custom-call(f32[864,768]{1,0:T(8,128)} %get-tuple-element.768.dv1_ref, bf16[864,768]{1,0:T(8,128)(2,1)} %roll_in.2.x_ref, bf16[3,864,768]{2,1,0:T(8,128)(2,1)} %window_bwd.3.dmix_ref, f32[1,768]{1,0:T(1,128)} %get-tuple-element.771.gw_ref, bf16[8,768,768]{2,1,0:T(8,128)(2,1)} %bitcast.259), custom_call_target="tpu_custom_call" | custom-call | flops 3057647616 | bytes 1048576 | tf_op jit(solution)/shard_map/window_end/pallas_call | solution.py:123
  (508 shorter events, 269.6 us)
Async XLA Ops:
  7.2 470.7 %reduce-scatter.5.cloned.1.call-start = ((), (), s32[]{:S(2)}) async-start(), calls=%async_computation.3 | async-start | bytes 1658880 | tf_op jit(solution)/shard_map/reduce_scatter | solution.py:1471
  11.8 31.0 %collective-permute-start.3 = (bf16[432,768]{1,0:T(8,128)(2,1)S(1)}, bf16[432,768]{1,0:T(8,128)(2,1)S(1)}, u32[]{:S(2)}, u32[]{:S(2)}) collective-permute-start(bf16[432,768]{1,0:T(8,128)(2,1)S(1)} %reshape.538), channel_id=1, source_target_pairs={{1,0},{2,1},{3,2},{4,3},{5,4},{6,5},{7,6},{0,7},{9,8},{10,9},{11,1... | collective-permute-start | bytes 1990664 | tf_op jit(solution)/shard_map/ppermute | solution.py:962
  16.7 26.1 %collective-permute-start.1 = (bf16[9,24,768]{2,1,0:T(8,128)(2,1)}, bf16[9,24,768]{2,1,0:T(8,128)(2,1)S(1)}, u32[]{:S(2)}, u32[]{:S(2)}) collective-permute-start(bf16[9,24,768]{2,1,0:T(8,128)(2,1)} %get-tuple-element.443), channel_id=1, source_target_pairs={{0,16},{8,24},{16,0},{24,8},{1,17},{9,25},{17,1},{25,9},{2,18},{10... | collective-permute-start | bytes 995336 | tf_op jit(solution)/shard_map/ppermute | solution.py:816
  44.2 29.5 %collective-permute-start.8 = (bf16[4,9,24,768]{3,2,1,0:T(8,128)(2,1)S(1)}, bf16[4,9,24,768]{3,2,1,0:T(8,128)(2,1)}, u32[]{:S(2)}, u32[]{:S(2)}) collective-permute-start(bf16[4,9,24,768]{3,2,1,0:T(8,128)(2,1)S(1)} %pad_maximum_fusion.args_0_), channel_id=1, source_target_pairs={{0,2},{1,5},{2,0},{3,7},{4,6},{5,1},{6,4},{7,3},{8,10},{9,13},{10,... | collective-permute-start | bytes 3981320 | tf_op jit(solution)/shard_map/ppermute | solution.py:813
  44.3 29.4 %collective-permute-start.9 = (bf16[4,9,24,768]{3,2,1,0:T(8,128)(2,1)S(1)}, bf16[4,9,24,768]{3,2,1,0:T(8,128)(2,1)}, u32[]{:S(2)}, u32[]{:S(2)}) collective-permute-start(bf16[4,9,24,768]{3,2,1,0:T(8,128)(2,1)S(1)} %pad_maximum_fusion.args_0_), channel_id=1, source_target_pairs={{0,4},{1,3},{2,6},{3,1},{4,0},{5,7},{6,2},{7,5},{8,12},{9,11},{10,... | collective-permute-start | bytes 3981320 | tf_op jit(solution)/shard_map/ppermute | solution.py:813
  98.7 43.5 %collective-permute-start.19 = (bf16[4,7,24,768]{3,2,1,0:T(8,128)(2,1)S(1)}, bf16[4,7,24,768]{3,2,1,0:T(8,128)(2,1)S(1)}, u32[]{:S(2)}, u32[]{:S(2)}) collective-permute-start(bf16[4,7,24,768]{3,2,1,0:T(8,128)(2,1)S(1)} %pad_maximum_fusion.4.args_0_), channel_id=1, source_target_pairs={{0,2},{1,5},{2,0},{3,7},{4,6},{5,1},{6,4},{7,3},{8,10},{9,13},{10,... | collective-permute-start | bytes 3096584 | tf_op jit(solution)/shard_map/ppermute | solution.py:813
  100.0 42.2 %collective-permute-start.20 = (bf16[4,7,24,768]{3,2,1,0:T(8,128)(2,1)S(1)}, bf16[4,7,24,768]{3,2,1,0:T(8,128)(2,1)}, u32[]{:S(2)}, u32[]{:S(2)}) collective-permute-start(bf16[4,7,24,768]{3,2,1,0:T(8,128)(2,1)S(1)} %pad_maximum_fusion.4.args_0_), channel_id=1, source_target_pairs={{0,4},{1,3},{2,6},{3,1},{4,0},{5,7},{6,2},{7,5},{8,12},{9,11},{10,... | collective-permute-start | bytes 3096584 | tf_op jit(solution)/shard_map/ppermute | solution.py:813
  105.8 36.3 %collective-permute-start.16 = (bf16[8,24,768]{2,1,0:T(8,128)(2,1)}, bf16[8,24,768]{2,1,0:T(8,128)(2,1)S(1)}, u32[]{:S(2)}, u32[]{:S(2)}) collective-permute-start(bf16[8,24,768]{2,1,0:T(8,128)(2,1)} %get-tuple-element.471), channel_id=1, source_target_pairs={{0,8},{8,0},{16,24},{24,16},{1,9},{9,1},{17,25},{25,17},{2,10},{10... | collective-permute-start | bytes 884744 | tf_op jit(solution)/shard_map/ppermute | solution.py:816
  113.8 28.4 %collective-permute-start.17 = (bf16[8,24,768]{2,1,0:T(8,128)(2,1)}, bf16[8,24,768]{2,1,0:T(8,128)(2,1)S(1)}, u32[]{:S(2)}, u32[]{:S(2)}) collective-permute-start(bf16[8,24,768]{2,1,0:T(8,128)(2,1)} %get-tuple-element.471), channel_id=1, source_target_pairs={{0,16},{8,24},{16,0},{24,8},{1,17},{9,25},{17,1},{25,9},{2,18},{10... | collective-permute-start | bytes 884744 | tf_op jit(solution)/shard_map/ppermute | solution.py:816
  114.7 27.5 %collective-permute-start.18 = (bf16[8,24,768]{2,1,0:T(8,128)(2,1)}, bf16[8,24,768]{2,1,0:T(8,128)(2,1)S(1)}, u32[]{:S(2)}, u32[]{:S(2)}) collective-permute-start(bf16[8,24,768]{2,1,0:T(8,128)(2,1)} %get-tuple-element.471), channel_id=1, source_target_pairs={{0,24},{8,16},{16,8},{24,0},{1,25},{9,17},{17,9},{25,1},{2,26},{10... | collective-permute-start | bytes 884744 | tf_op jit(solution)/shard_map/ppermute | solution.py:816
  160.7 28.9 %collective-permute-start.30 = (bf16[4,8,24,768]{3,2,1,0:T(8,128)(2,1)S(1)}, bf16[4,8,24,768]{3,2,1,0:T(8,128)(2,1)}, u32[]{:S(2)}, u32[]{:S(2)}) collective-permute-start(bf16[4,8,24,768]{3,2,1,0:T(8,128)(2,1)S(1)} %pad_maximum_fusion.2.args_0_), channel_id=1, source_target_pairs={{0,2},{1,5},{2,0},{3,7},{4,6},{5,1},{6,4},{7,3},{8,10},{9,13},{10,... | collective-permute-start | bytes 3538952 | tf_op jit(solution)/shard_map/ppermute | solution.py:813
  162.4 27.1 %collective-permute-start.31 = (bf16[4,8,24,768]{3,2,1,0:T(8,128)(2,1)S(1)}, bf16[4,8,24,768]{3,2,1,0:T(8,128)(2,1)}, u32[]{:S(2)}, u32[]{:S(2)}) collective-permute-start(bf16[4,8,24,768]{3,2,1,0:T(8,128)(2,1)S(1)} %pad_maximum_fusion.2.args_0_), channel_id=1, source_target_pairs={{0,4},{1,3},{2,6},{3,1},{4,0},{5,7},{6,2},{7,5},{8,12},{9,11},{10,... | collective-permute-start | bytes 3538952 | tf_op jit(solution)/shard_map/ppermute | solution.py:813
  163.5 26.1 %collective-permute-start.28 = (bf16[9,24,768]{2,1,0:T(8,128)(2,1)}, bf16[9,24,768]{2,1,0:T(8,128)(2,1)S(1)}, u32[]{:S(2)}, u32[]{:S(2)}) collective-permute-start(bf16[9,24,768]{2,1,0:T(8,128)(2,1)} %get-tuple-element.505), channel_id=1, source_target_pairs={{0,16},{8,24},{16,0},{24,8},{1,17},{9,25},{17,1},{25,9},{2,18},{10... | collective-permute-start | bytes 995336 | tf_op jit(solution)/shard_map/ppermute | solution.py:816
  244.1 26.4 %collective-permute-start.46 = (bf16[4,9,24,768]{3,2,1,0:T(8,128)(2,1)S(1)}, bf16[4,9,24,768]{3,2,1,0:T(8,128)(2,1)S(1)}, u32[]{:S(2)}, u32[]{:S(2)}) collective-permute-start(bf16[4,9,24,768]{3,2,1,0:T(8,128)(2,1)S(1)} %pad_maximum_fusion.1.args_0_), channel_id=1, source_target_pairs={{0,2},{1,5},{2,0},{3,7},{4,6},{5,1},{6,4},{7,3},{8,10},{9,13},{10,... | collective-permute-start | bytes 3981320 | tf_op jit(solution)/shard_map/ppermute | solution.py:813
  244.4 26.0 %collective-permute-start.47 = (bf16[4,9,24,768]{3,2,1,0:T(8,128)(2,1)S(1)}, bf16[4,9,24,768]{3,2,1,0:T(8,128)(2,1)S(1)}, u32[]{:S(2)}, u32[]{:S(2)}) collective-permute-start(bf16[4,9,24,768]{3,2,1,0:T(8,128)(2,1)S(1)} %pad_maximum_fusion.1.args_0_), channel_id=1, source_target_pairs={{0,1},{1,0},{2,3},{3,2},{4,5},{5,4},{6,7},{7,6},{8,9},{9,8},{10,11... | collective-permute-start | bytes 3981320 | tf_op jit(solution)/shard_map/ppermute | solution.py:808
  244.4 26.0 %collective-permute-start.43 = (bf16[128,201]{1,0:T(8,128)(2,1)S(1)}, bf16[128,201]{1,0:T(8,128)(2,1)S(1)}, u32[]{:S(2)}, u32[]{:S(2)}) collective-permute-start(bf16[128,201]{1,0:T(8,128)(2,1)S(1)} %pad_maximum_fusion.15), channel_id=1, source_target_pairs={{0,2},{1,3},{2,0},{3,1},{4,6},{5,7},{6,4},{7,5},{8,10},{9,11},{10,... | collective-permute-start | bytes 154376 | tf_op jit(solution)/shard_map/ppermute | solution.py:813
  270.5 28.3 %collective-permute-start.48 = (bf16[4,9,24,768]{3,2,1,0:T(8,128)(2,1)S(1)}, bf16[4,9,24,768]{3,2,1,0:T(8,128)(2,1)S(1)}, u32[]{:S(2)}, u32[]{:S(2)}) collective-permute-start(bf16[4,9,24,768]{3,2,1,0:T(8,128)(2,1)S(1)} %collective-permute-done.46.args_1_), channel_id=1, source_target_pairs={{0,4},{1,3},{2,6},{3,1},{4,0},{5,7},{6,2},{7,5},{8,12},{9,11},{10,... | collective-permute-start | bytes 3981320 | tf_op jit(solution)/shard_map/ppermute | solution.py:813
  272.5 30.1 %collective-permute-start.49 = (bf16[4,9,24,768]{3,2,1,0:T(8,128)(2,1)S(1)}, bf16[4,9,24,768]{3,2,1,0:T(8,128)(2,1)}, u32[]{:S(2)}, u32[]{:S(2)}) collective-permute-start(bf16[4,9,24,768]{3,2,1,0:T(8,128)(2,1)S(1)} %pad_maximum_fusion.1.args_0_), channel_id=1, source_target_pairs={{0,4},{1,3},{2,6},{3,1},{4,0},{5,7},{6,2},{7,5},{8,12},{9,11},{10,... | collective-permute-start | bytes 3981320 | tf_op jit(solution)/shard_map/ppermute | solution.py:813
  272.6 30.0 %collective-permute-start.50 = (bf16[4,9,24,768]{3,2,1,0:T(8,128)(2,1)S(1)}, bf16[4,9,24,768]{3,2,1,0:T(8,128)(2,1)}, u32[]{:S(2)}, u32[]{:S(2)}) collective-permute-start(bf16[4,9,24,768]{3,2,1,0:T(8,128)(2,1)S(1)} %collective-permute-done.46.args_1_), channel_id=1, source_target_pairs={{0,1},{1,0},{2,3},{3,2},{4,5},{5,4},{6,7},{7,6},{8,9},{9,8},{10,11... | collective-permute-start | bytes 3981320 | tf_op jit(solution)/shard_map/ppermute | solution.py:808
  272.6 26.1 %collective-permute-start.51 = (bf16[4,4,2,24,768]{4,3,2,1,0:T(8,128)(2,1)}, bf16[4,4,2,24,768]{4,3,2,1,0:T(8,128)(2,1)}, u32[]{:S(2)}, u32[]{:S(2)}) collective-permute-start(bf16[4,4,2,24,768]{4,3,2,1,0:T(8,128)(2,1)} %get-tuple-element.590), channel_id=1, source_target_pairs={{0,1},{1,0},{2,3},{3,2},{4,5},{5,4},{6,7},{7,6},{8,9},{9,8},{10,11... | collective-permute-start | bytes 3538952 | tf_op jit(solution)/shard_map/ppermute | solution.py:808
  328.3 27.0 %collective-permute-start.58 = (bf16[4,8,24,768]{3,2,1,0:T(8,128)(2,1)}, bf16[4,8,24,768]{3,2,1,0:T(8,128)(2,1)S(1)}, u32[]{:S(2)}, u32[]{:S(2)}) collective-permute-start(bf16[4,8,24,768]{3,2,1,0:T(8,128)(2,1)} %get-tuple-element.640), channel_id=1, source_target_pairs={{0,4},{1,3},{2,6},{3,1},{4,0},{5,7},{6,2},{7,5},{8,12},{9,11},{10,... | collective-permute-start | bytes 3538952 | tf_op jit(solution)/shard_map/ppermute | solution.py:813
  391.9 86.0 %reduce-scatter.3.cloned.1.call-start = ((), (), s32[]{:S(2)}) async-start(), calls=%async_computation.2 | async-start | bytes 1474560 | tf_op jit(solution)/shard_map/reduce_scatter | solution.py:1510
  485.8 26.8 %collective-permute-start.81 = (bf16[4,4,24,768]{3,2,1,0:T(8,128)(2,1)}, bf16[4,4,24,768]{3,2,1,0:T(8,128)(2,1)S(1)}, u32[]{:S(2)}, u32[]{:S(2)}) collective-permute-start(bf16[4,4,24,768]{3,2,1,0:T(8,128)(2,1)} %get-tuple-element.765), channel_id=1, source_target_pairs={{0,4},{1,3},{2,6},{3,1},{4,0},{5,7},{6,2},{7,5},{8,12},{9,11},{10,... | collective-permute-start | bytes 1769480 | tf_op jit(solution)/shard_map/ppermute | solution.py:813
  486.8 25.8 %collective-permute-start.82 = (bf16[4,4,24,768]{3,2,1,0:T(8,128)(2,1)}, bf16[4,4,24,768]{3,2,1,0:T(8,128)(2,1)S(1)}, u32[]{:S(2)}, u32[]{:S(2)}) collective-permute-start(bf16[4,4,24,768]{3,2,1,0:T(8,128)(2,1)} %get-tuple-element.766), channel_id=1, source_target_pairs={{0,4},{1,3},{2,6},{3,1},{4,0},{5,7},{6,2},{7,5},{8,12},{9,11},{10,... | collective-permute-start | bytes 1769480 | tf_op jit(solution)/shard_map/ppermute | solution.py:813
  (154 other events, 1884.6 us)
Sparse Core Ops, SparseCore 0:
  392.0 35.5 reduce-scatter.4
  429.9 27.9 reduce-scatter.2
